TPU v7x, 32 devices: a whole 2x2x4 slice. The times are simulated.
32 devices in a mesh: dp: 2 (over core), wide: 16 (over z, y, x).
Axes of the slice: x: 2, y: 2, z: 4, core: 2. Of those that a mesh axis runs over, the one named last changes fastest.
Arguments:
- feature_map: float32 [32, 6144], P(None, ('dp', 'wide')), may hold values from -6 to 6
- condition: float32 [12, 1024], P('dp'), may hold values from -6 to 6
- item_lengths: int32 [2, 6], P('dp'), may hold values from 0 to 2240, as said below
- cotangent: bfloat16 [6144, 1024], P(('dp', 'wide')), may hold values from -6 to 6
- code_book: bfloat16 [4096, 1024], replicated, may hold values from -0.5 to 0.5
- qkv_state: float32 [3, 1024, 3072], P(None, 'dp', 'wide'), as said below
- out_state: float32 [3, 1024, 1024], P(None, 'dp', 'wide'), as said below
- up_state: float32 [3, 1024, 4096], P(None, 'dp', 'wide'), as said below
- down_state: float32 [3, 4096, 1024], P(None, 'dp', 'wide'), as said below
- ada_state: float32 [3, 1024, 6144], P(None, 'dp', 'wide'), as said below
- embed_state: float32 [3, 32, 1024], replicated, as said below
- vector_state: float32 [3, 8, 1024], replicated, as said below
Outputs:
- block_out: bfloat16 [6144, 1024], P(('dp', 'wide'))
- map_grad: float32 [32, 6144], P(None, ('dp', 'wide'))
- histogram: float32 [4096], replicated
- qkv_new: float32 [3, 1024, 3072], P(None, 'dp', 'wide')
- qkv_copy: bfloat16 [1024, 3072], P('dp', 'wide')
- out_new: float32 [3, 1024, 1024], P(None, 'dp', 'wide')
- out_copy: bfloat16 [1024, 1024], P('dp', 'wide')
- up_new: float32 [3, 1024, 4096], P(None, 'dp', 'wide')
- up_copy: bfloat16 [1024, 4096], P('dp', 'wide')
- down_new: float32 [3, 4096, 1024], P(None, 'dp', 'wide')
- down_copy: bfloat16 [4096, 1024], P('dp', 'wide')
- ada_new: float32 [3, 1024, 6144], P(None, 'dp', 'wide')
- ada_copy: bfloat16 [1024, 6144], P('dp', 'wide')
- embed_new: float32 [3, 32, 1024], replicated
- vector_new: float32 [3, 8, 1024], replicated
- gain_grad: float32 [1024], replicated
Inputs may be any that keep to these rules, and one draw needn't show every extreme that they name: `item_lengths`: each entry is 0, 680 or 2240; every row holds the same number of 2240 entries (at least one) and the same number of 680 entries, a row's entries sum to at most 3072 and to more than 2392. `qkv_state`: index 0 is the momentum, 1 the weight, 2 the running average. `out_state`: index 0 is the momentum, 1 the weight, 2 the running average. `up_state`: index 0 is the momentum, 1 the weight, 2 the running average. `down_state`: index 0 is the momentum, 1 the weight, 2 the running average. `ada_state`: index 0 is the momentum, 1 the weight, 2 the running average. `embed_state`: index 0 is the momentum, 1 the weight, 2 the running average. `vector_state`: index 0 is the momentum, 1 the value, 2 the running average; the query gain row of the value is positive.
All inputs are finite; a program needn't handle non-finite values.
Results may differ from a plain program's by a relative error of at most 0.019.
Values may be sent and summed in bfloat16 or wider, within the bound.
A program may use at most 320 MiB of HBM per device.

v0:
```python
import math

import jax
import jax.numpy as jnp
from jax import lax
from jax.sharding import PartitionSpec as P

HEADS = 16
LEVELS = 10
STEP = 7


SHORT_SIDES = (1, 2, 3, 4, 5, 6, 8, 10, 13, 16)
LONG_SIDES = (1, 2, 3, 4, 6, 9, 13, 18, 24, 32)
MASKED = -1e30
NORM_EPS = 1e-06
MOMENTUM = 0.9
WEIGHT_DECAY = 0.05
BASE_RATE = 0.37
VECTOR_RATE = 0.22
GRAD_FACTORS = (0.15, 0.1, 0.3, 0.35, 0.3)
EMBED_FACTOR = 0.6
HIGHEST_PRECISION = lax.Precision.HIGHEST


def padded(cells, sides, width):
    for axis, dim in sides:
        count = lax.axis_size(axis)
        ends = count - 1
        head = lax.slice_in_dim(cells, 0, width, axis=dim)
        tail = lax.slice_in_dim(cells, cells.shape[dim] - width, cells.shape[dim], axis=dim)
        cells = jnp.concatenate(
            [
                lax.ppermute(tail, axis, [(i, (i + 1) % count) for i in range(ends)]),
                cells,
                lax.ppermute(head, axis, [((i + 1) % count, i) for i in range(ends)]),
            ],
            axis=dim,
        )
    return cells


def layout(lengths, positions, group_len):
    short_sq = jnp.array([side * side for side in SHORT_SIDES[:LEVELS]], jnp.int32)
    long_sq = jnp.array([side * side for side in LONG_SIDES[:LEVELS]], jnp.int32)
    short_total = sum((side * side for side in SHORT_SIDES[:LEVELS]))
    long_total = sum((side * side for side in LONG_SIDES[:LEVELS]))
    slot_count = lengths.shape[0]
    counts = jnp.where(
        lengths[None, :] == long_total,
        long_sq[:, None],
        jnp.where(lengths[None, :] == short_total, short_sq[:, None], 0),
    )
    unused = group_len - jnp.sum(lengths)
    ordered = jnp.concatenate([counts.reshape(-1), unused[None]])
    boundary = jnp.cumsum(ordered)
    segment = jnp.sum((boundary[None, :] <= positions[:, None]).astype(jnp.int32), axis=1)
    segment = jnp.minimum(segment, ordered.shape[0] - 1)
    unused_id = slot_count * LEVELS
    tok_level = jnp.where(segment >= unused_id, 0, segment // slot_count)
    tok_slot = jnp.where(segment >= unused_id, slot_count, segment % slot_count)
    return (tok_slot, tok_level, segment)


def pre_norm(inputs, scaling, offset_add):
    row_mean = jnp.mean(inputs, axis=-1, keepdims=True)
    centred = inputs - row_mean
    spread = jnp.mean(centred * centred, axis=-1, keepdims=True)
    return centred * lax.rsqrt(spread + NORM_EPS) * (1.0 + scaling) + offset_add


def unit_heads(inputs):
    shaped = inputs.reshape(inputs.shape[0], HEADS, -1)
    shaped = shaped * lax.rsqrt(jnp.sum(shaped * shaped, axis=-1, keepdims=True) + NORM_EPS)
    return shaped.reshape(inputs.shape)


def split_heads(projected, q_gain):
    queries, key_part, value_part = jnp.split(projected, 3, axis=1)
    head_scale = math.sqrt(queries.shape[1] // HEADS)
    return (unit_heads(queries) * (head_scale * (1.0 + q_gain)), unit_heads(key_part), value_part)


def smooth_map(values, left_ok, right_ok, before, following):
    return (left_ok * before + 2.0 * values + right_ok * following) / (2.0 + left_ok + right_ok)


def nesterov(stacked, gradient, step_rate, decay_rate):
    moment, weight, average = (stacked[0], stacked[1], stacked[2])
    step_grad = gradient + decay_rate * weight
    new_moment = MOMENTUM * moment + step_rate * step_grad
    new_weight = weight - (step_rate * step_grad + MOMENTUM * new_moment)
    retain = min(0.999, (1.0 + STEP) / (10.0 + STEP))
    new_average = retain * average + (1.0 - retain) * new_weight
    return jnp.stack([new_moment, new_weight, new_average])


def contract_rows(left_side, right_side, precision=None):
    return lax.dot_general(
        left_side,
        right_side,
        (((0,), (0,)), ((), ())),
        precision=precision,
        preferred_element_type=jnp.float32,
    )


def against(left_side, right_side):
    return lax.dot_general(
        left_side, right_side, (((1,), (1,)), ((), ())), preferred_element_type=jnp.float32
    )


def shards(
    feature_map,
    condition,
    item_lengths,
    cotangent,
    code_book,
    qkv_state,
    out_state,
    up_state,
    down_state,
    ada_state,
    embed_state,
    vector_state,
):
    tok_rows = cotangent.shape[0]
    model_width = cotangent.shape[1]
    head_dim = model_width // HEADS
    wide_count = lax.axis_size("wide")
    group_len = tok_rows * wide_count
    tokens_all = lax.axis_size("dp") * group_len
    lengths = item_lengths[0]
    slot_count = lengths.shape[0]
    positions = lax.axis_index("wide") * tok_rows + jnp.arange(tok_rows, dtype=jnp.int32)
    tok_slot, tok_level, segment = layout(lengths, positions, group_len)
    live_rows = (tok_slot < slot_count).astype(jnp.float32)[:, None]
    left_ok = ((layout(lengths, positions - 1, group_len)[2] == segment) & (positions > 0)).astype(
        jnp.float32
    )
    right_ok = (
        (layout(lengths, positions + 1, group_len)[2] == segment) & (positions < group_len - 1)
    ).astype(jnp.float32)
    rimmed = padded(feature_map, (("wide", 1),), 1)
    smooth = smooth_map(feature_map, left_ok, right_ok, rimmed[:, :-2], rimmed[:, 2:])
    states = (qkv_state, out_state, up_state, down_state, ada_state)
    masters = tuple((stacked[1].astype(jnp.bfloat16) for stacked in states))
    columns = (
        lax.all_gather(masters[0], "wide", axis=1, tiled=True),
        lax.all_gather(masters[1], "wide", axis=1, tiled=True),
        lax.all_gather(masters[2], "wide", axis=1, tiled=True),
        lax.all_gather(masters[3], "wide", axis=1, tiled=True),
    )
    ada_piece = lax.all_gather(masters[4], "wide", axis=1, tiled=True)
    w_qkv, w_out, w_up, w_down, w_ada = (
        lax.all_gather(columns[0], "dp", axis=0, tiled=True),
        lax.all_gather(columns[1], "dp", axis=0, tiled=True),
        lax.all_gather(columns[2], "dp", axis=0, tiled=True),
        lax.all_gather(columns[3], "dp", axis=0, tiled=True),
        lax.all_gather(ada_piece, "dp", axis=0, tiled=True),
    )
    embed_w = embed_state[1]
    vectors = vector_state[1]
    x_zero = (
        lax.dot_general(smooth, embed_w, (((0,), (0,)), ((), ())), precision=HIGHEST_PRECISION)
        + vectors[6]
    )
    silu_cond = jax.nn.silu(condition).astype(jnp.bfloat16)
    ada_product = jnp.dot(silu_cond, w_ada, preferred_element_type=jnp.float32)
    ada_all = ada_product + vectors[:6].reshape(-1)
    one_hot = (tok_slot[:, None] == jnp.arange(slot_count, dtype=jnp.int32)[None, :]).astype(
        jnp.float32
    )
    token_ada = jnp.dot(one_hot, ada_all, precision=HIGHEST_PRECISION)
    gate_one, gate_two, scale_one, scale_two, shift_one, shift_two = jnp.split(token_ada, 6, axis=1)
    h_one_low = pre_norm(x_zero, scale_one, shift_one).astype(jnp.bfloat16)
    projected = jnp.dot(h_one_low, w_qkv, preferred_element_type=jnp.float32)
    (q_unit, k_unit, v_full), heads_back = jax.vjp(split_heads, projected, vectors[7])
    queries = q_unit.astype(jnp.bfloat16)
    keys_low = k_unit.astype(jnp.bfloat16)
    values_low = v_full.astype(jnp.bfloat16)
    query_heads = queries.reshape(tok_rows, HEADS, head_dim)

    def blockwise(advance, running, pieces, first_row):
        key_count = pieces[0].shape[0]
        block_size = math.gcd(key_count, 1024)

        def per_block(current, offset):
            key_part = tuple(
                (lax.dynamic_slice_in_dim(piece_arr, offset, block_size, 0) for piece_arr in pieces)
            )
            first_key = first_row + offset
            k_slot, k_level, _ = layout(
                lengths, first_key + jnp.arange(block_size, dtype=jnp.int32), group_len
            )
            allowed = (tok_slot[:, None] == k_slot[None, :]) & (
                k_level[None, :] <= tok_level[:, None]
            )
            current = advance(current, key_part, allowed, first_key)
            return (current, None)

        offsets = jnp.arange(key_count // block_size, dtype=jnp.int32) * block_size
        return lax.scan(per_block, running, offsets)[0]

    def scores_of(key_block, allowed):
        raw_scores = jnp.einsum(
            "qhd,khd->hqk",
            query_heads,
            key_block.reshape(-1, HEADS, head_dim),
            preferred_element_type=jnp.float32,
        )
        return jnp.where(allowed[None], raw_scores, MASKED)

    def stats_step(running, key_part, allowed, first_key):
        scores = scores_of(key_part[0], allowed)
        top_score, exp_total = running
        new_top = jnp.maximum(top_score, jnp.max(scores, axis=-1, keepdims=True))
        exp_total = exp_total * jnp.exp(top_score - new_top) + jnp.sum(
            jnp.exp(scores - new_top), axis=-1, keepdims=True
        )
        return (new_top, exp_total)

    kv_rows = (
        lax.all_gather(keys_low, "wide", axis=0, tiled=True),
        lax.all_gather(values_low, "wide", axis=0, tiled=True),
    )
    start_stats = (
        jnp.full((HEADS, tok_rows, 1), MASKED, jnp.float32),
        jnp.zeros((HEADS, tok_rows, 1), jnp.float32),
    )
    top_score, exp_total = blockwise(stats_step, start_stats, kv_rows, 0)
    log_total = top_score + jnp.log(exp_total)

    def value_step(running, key_part, allowed, first_key):
        attn_probs = jnp.exp(scores_of(key_part[0], allowed) - log_total).astype(jnp.bfloat16)
        return running + jnp.einsum(
            "hqk,khd->qhd",
            attn_probs,
            key_part[1].reshape(-1, HEADS, head_dim),
            preferred_element_type=jnp.float32,
        )

    attended = blockwise(
        value_step, jnp.zeros((tok_rows, HEADS, head_dim), jnp.float32), kv_rows, 0
    )
    attn_low = attended.reshape(tok_rows, model_width).astype(jnp.bfloat16)
    attn_proj = jnp.dot(attn_low, w_out, preferred_element_type=jnp.float32)
    x_one = x_zero + gate_one * attn_proj
    h_two_low = pre_norm(x_one, scale_two, shift_two).astype(jnp.bfloat16)
    hidden_pre = jnp.dot(h_two_low, w_up, preferred_element_type=jnp.float32)
    act_low = jax.nn.gelu(hidden_pre, approximate=True).astype(jnp.bfloat16)
    mlp_out = jnp.dot(act_low, w_down, preferred_element_type=jnp.float32)
    x_two = x_one + gate_two * mlp_out
    block_out = (x_two * live_rows).astype(jnp.bfloat16)
    logits = against(block_out, code_book)
    code_mass = jnp.sum(jax.nn.softmax(logits, axis=-1) * live_rows, axis=0)
    g_two = cotangent.astype(jnp.float32) * live_rows
    d_mlp = (gate_two * g_two).astype(jnp.bfloat16)
    d_gate_two = g_two * mlp_out
    dw_down = contract_rows(act_low, d_mlp)
    d_act = against(d_mlp, w_down)
    _, gelu_back = jax.vjp(lambda inputs: jax.nn.gelu(inputs, approximate=True), hidden_pre)
    d_hidden = gelu_back(d_act)[0].astype(jnp.bfloat16)
    dw_up = contract_rows(h_two_low, d_hidden)
    d_h_two = against(d_hidden, w_up)
    _, norm_back_two = jax.vjp(pre_norm, x_one, scale_two, shift_two)
    d_x_one, d_scale_two, d_shift_two = norm_back_two(d_h_two)
    d_x_one = d_x_one + g_two
    d_attn = (gate_one * d_x_one).astype(jnp.bfloat16)
    d_gate_one = d_x_one * attn_proj
    dw_out = contract_rows(attn_low, d_attn)
    grad_flat = against(d_attn, w_out).astype(jnp.bfloat16)
    grad_heads = grad_flat.reshape(tok_rows, HEADS, head_dim)

    def delta_step(running, key_part, allowed, first_key):
        attn_probs = jnp.exp(scores_of(key_part[0], allowed) - log_total)
        d_probs = jnp.einsum(
            "qhd,khd->hqk",
            grad_heads,
            key_part[1].reshape(-1, HEADS, head_dim),
            preferred_element_type=jnp.float32,
        )
        return running + jnp.sum(attn_probs * d_probs, axis=-1, keepdims=True)

    row_delta = blockwise(delta_step, jnp.zeros((HEADS, tok_rows, 1), jnp.float32), kv_rows, 0)

    def grad_step(running, key_part, allowed, first_key):
        d_query, d_keys, d_values = running
        key_heads = key_part[0].reshape(-1, HEADS, head_dim)
        value_heads = key_part[1].reshape(-1, HEADS, head_dim)
        block_rows = key_part[0].shape[0]
        attn_probs = jnp.exp(scores_of(key_part[0], allowed) - log_total)
        d_probs = jnp.einsum(
            "qhd,khd->hqk", grad_heads, value_heads, preferred_element_type=jnp.float32
        )
        d_scores = (attn_probs * (d_probs - row_delta)).astype(jnp.bfloat16)
        d_query = d_query + jnp.einsum(
            "hqk,khd->qhd", d_scores, key_heads, preferred_element_type=jnp.float32
        )
        key_grad = jnp.einsum(
            "hqk,qhd->khd", d_scores, query_heads, preferred_element_type=jnp.float32
        )
        value_grad = jnp.einsum(
            "hqk,qhd->khd",
            attn_probs.astype(jnp.bfloat16),
            grad_heads,
            preferred_element_type=jnp.float32,
        )
        key_sum = lax.dynamic_slice_in_dim(d_keys, first_key, block_rows, 0) + key_grad.reshape(
            block_rows, model_width
        )
        value_sum = lax.dynamic_slice_in_dim(
            d_values, first_key, block_rows, 0
        ) + value_grad.reshape(block_rows, model_width)
        d_keys = lax.dynamic_update_slice_in_dim(d_keys, key_sum, first_key, 0)
        d_values = lax.dynamic_update_slice_in_dim(d_values, value_sum, first_key, 0)
        return (d_query, d_keys, d_values)

    grad_init = (
        jnp.zeros((tok_rows, HEADS, head_dim), jnp.float32),
        jnp.zeros((group_len, model_width), jnp.float32),
        jnp.zeros((group_len, model_width), jnp.float32),
    )
    d_query, d_keys, d_values = blockwise(grad_step, grad_init, kv_rows, 0)
    d_keys_own, d_values_own = (
        lax.psum_scatter(
            d_keys.astype(jnp.bfloat16), "wide", scatter_dimension=0, tiled=True
        ).astype(jnp.float32),
        lax.psum_scatter(
            d_values.astype(jnp.bfloat16), "wide", scatter_dimension=0, tiled=True
        ).astype(jnp.float32),
    )
    d_projected, d_gain = heads_back(
        (d_query.reshape(tok_rows, model_width), d_keys_own, d_values_own)
    )
    d_projected_low = d_projected.astype(jnp.bfloat16)
    dw_qkv = contract_rows(h_one_low, d_projected_low)
    d_h_one = against(d_projected_low, w_qkv)
    _, norm_back_one = jax.vjp(pre_norm, x_zero, scale_one, shift_one)
    d_x_zero, d_scale_one, d_shift_one = norm_back_one(d_h_one)
    d_x_zero = d_x_zero + d_x_one
    d_token_ada = jnp.concatenate(
        [d_gate_one, d_gate_two, d_scale_one, d_scale_two, d_shift_one, d_shift_two], axis=1
    )
    d_ada_all = contract_rows(one_hot, d_token_ada, HIGHEST_PRECISION)
    d_smooth = lax.dot_general(
        embed_w, d_x_zero, (((1,), (1,)), ((), ())), precision=HIGHEST_PRECISION
    )
    d_embed = lax.dot_general(
        smooth, d_x_zero, (((1,), (0,)), ((), ())), precision=HIGHEST_PRECISION
    )
    d_vectors = jnp.concatenate(
        [
            jnp.sum(d_ada_all, axis=0).reshape(6, model_width),
            jnp.sum(d_x_zero, axis=0)[None],
            d_gain[None],
        ],
        axis=0,
    )
    grad_share = d_smooth / (2.0 + left_ok + right_ok)
    rim_share = padded(grad_share, (("wide", 1),), 1)
    map_grad = 2.0 * grad_share + left_ok * rim_share[:, :-2] + right_ok * rim_share[:, 2:]
    d_embed_all, d_vectors_all, mass_all = lax.psum((d_embed, d_vectors, code_mass), ("dp", "wide"))
    histogram = mass_all * (code_book.shape[0] / tokens_all)
    ada_term = contract_rows(silu_cond.astype(jnp.float32), d_ada_all, HIGHEST_PRECISION)
    split_cols = (
        lax.psum_scatter(
            dw_qkv.astype(jnp.bfloat16), "wide", scatter_dimension=1, tiled=True
        ).astype(jnp.float32),
        lax.psum_scatter(
            dw_out.astype(jnp.bfloat16), "wide", scatter_dimension=1, tiled=True
        ).astype(jnp.float32),
        lax.psum_scatter(
            dw_up.astype(jnp.bfloat16), "wide", scatter_dimension=1, tiled=True
        ).astype(jnp.float32),
        lax.psum_scatter(
            dw_down.astype(jnp.bfloat16), "wide", scatter_dimension=1, tiled=True
        ).astype(jnp.float32),
        lax.psum_scatter(
            ada_term.astype(jnp.bfloat16), "wide", scatter_dimension=1, tiled=True
        ).astype(jnp.float32),
    )
    ada_cols = split_cols[4]
    owned_grads = (
        lax.psum_scatter(
            split_cols[0].astype(jnp.bfloat16), "dp", scatter_dimension=0, tiled=True
        ).astype(jnp.float32),
        lax.psum_scatter(
            split_cols[1].astype(jnp.bfloat16), "dp", scatter_dimension=0, tiled=True
        ).astype(jnp.float32),
        lax.psum_scatter(
            split_cols[2].astype(jnp.bfloat16), "dp", scatter_dimension=0, tiled=True
        ).astype(jnp.float32),
        lax.psum_scatter(
            split_cols[3].astype(jnp.bfloat16), "dp", scatter_dimension=0, tiled=True
        ).astype(jnp.float32),
        lax.psum_scatter(
            ada_cols.astype(jnp.bfloat16), "dp", scatter_dimension=0, tiled=True
        ).astype(jnp.float32),
    )
    root_tokens = math.sqrt(tokens_all)
    spreads = (
        model_width ** (-0.5),
        (model_width // 16) ** (-0.5),
        model_width ** (-0.5),
        w_up.shape[1] ** (-0.5),
        model_width ** (-0.5),
    )
    new_states = tuple(
        (
            nesterov(
                stacked, gradient, BASE_RATE * spread_w / (factor_g * root_tokens), WEIGHT_DECAY
            )
            for stacked, gradient, spread_w, factor_g in zip(
                states, owned_grads, spreads, GRAD_FACTORS
            )
        )
    )
    embed_new = nesterov(
        embed_state,
        d_embed_all,
        BASE_RATE * embed_w.shape[0] ** (-0.5) / (EMBED_FACTOR * root_tokens),
        0.0,
    )
    vector_new = nesterov(vector_state, d_vectors_all, VECTOR_RATE / root_tokens, 0.0)
    return (
        block_out,
        map_grad,
        histogram,
        new_states[0],
        new_states[0][1].astype(jnp.bfloat16),
        new_states[1],
        new_states[1][1].astype(jnp.bfloat16),
        new_states[2],
        new_states[2][1].astype(jnp.bfloat16),
        new_states[3],
        new_states[3][1].astype(jnp.bfloat16),
        new_states[4],
        new_states[4][1].astype(jnp.bfloat16),
        embed_new,
        vector_new,
        d_vectors_all[7],
    )


def solution(mesh):
    in_specs = (
        P(None, ("dp", "wide")),
        P("dp", None),
        P("dp", None),
        P(("dp", "wide"), None),
        P(),
        P(None, "dp", "wide"),
        P(None, "dp", "wide"),
        P(None, "dp", "wide"),
        P(None, "dp", "wide"),
        P(None, "dp", "wide"),
        P(),
        P(),
    )
    out_specs = (
        P(("dp", "wide"), None),
        P(None, ("dp", "wide")),
        P(),
        P(None, "dp", "wide"),
        P("dp", "wide"),
        P(None, "dp", "wide"),
        P("dp", "wide"),
        P(None, "dp", "wide"),
        P("dp", "wide"),
        P(None, "dp", "wide"),
        P("dp", "wide"),
        P(None, "dp", "wide"),
        P("dp", "wide"),
        P(),
        P(),
        P(),
    )
    return jax.shard_map(shards, mesh=mesh, in_specs=in_specs, out_specs=out_specs, check_vma=False)
```

profile of v0, /device:TPU:0, one launch (start us, length us, event | category | flops | bytes accessed | tf_op | source)
XLA Modules:
  0.0 2299.2 jit_solution(5525777608460058045)
XLA Ops:
  11.0 98.3 %all-gather.13.cloned.1.call-done = bf16[512,6144]{1,0:T(8,128)(2,1)} async-done(((bf16[512,384]{1,0:T(8,128)(2,1)}), bf16[512,6144]{1,0:T(8,128)(2,1)}) %all-gather.13.cloned.1.call-update) | async-done | bytes 6291472 | tf_op jit(solution)/shard_map/all_gather | solution.py:155
  109.4 69.6 %all-gather.17.cloned.1.call-done = bf16[512,3072]{0,1:T(8,128)(2,1)} async-done(((bf16[512,192]{0,1:T(8,128)(2,1)}), bf16[512,3072]{0,1:T(8,128)(2,1)}) %all-gather.17.cloned.1.call-update) | async-done | bytes 3145744 | tf_op jit(solution)/shard_map/all_gather | solution.py:150
  248.0 35.0 %all-gather.25.cloned.1.call-done = bf16[512,1024]{0,1:T(8,128)(2,1)} async-done(((bf16[512,64]{0,1:T(8,128)(2,1)}), bf16[512,1024]{0,1:T(8,128)(2,1)}) %all-gather.25.cloned.1.call-update) | async-done | bytes 1048592 | tf_op jit(solution)/shard_map/all_gather | solution.py:151
  283.1 78.0 %all-gather.33.cloned.1.call-done = bf16[2048,1024]{0,1:T(8,128)(2,1)} async-done(((bf16[2048,64]{0,1:T(8,128)(2,1)}), bf16[2048,1024]{0,1:T(8,128)(2,1)}) %all-gather.33.cloned.1.call-update) | async-done | bytes 4194320 | tf_op jit(solution)/shard_map/all_gather | solution.py:153
  361.3 88.9 %all-gather.29.cloned.1.call-done = bf16[512,4096]{1,0:T(8,128)(2,1)} async-done(((bf16[512,256]{1,0:T(8,128)(2,1)}), bf16[512,4096]{1,0:T(8,128)(2,1)}) %all-gather.29.cloned.1.call-update) | async-done | bytes 4194320 | tf_op jit(solution)/shard_map/all_gather | solution.py:152
  450.7 95.2 %all-gather.23.cloned.1.call-done = bf16[3072,1024]{1,0:T(8,128)(2,1)} async-done(((bf16[192,1024]{1,0:T(8,128)(2,1)}), bf16[3072,1024]{1,0:T(8,128)(2,1)}) %all-gather.23.cloned.1.call-update) | async-done | bytes 6291472 | tf_op jit(solution)/shard_map/all_gather | solution.py:225
  554.6 35.4 %while.62 = (s32[]{:T(128)}, f32[16,192,1]{1,0,2:T(8,128)S(1)}, f32[16,192,1]{1,0,2:T(8,128)S(1)}, s32[192]{0:T(256)S(1)}, s32[1,6]{1,0:T(1,128)S(1)}, /*index=5...) while((s32[]{:T(128)}, f32[16,192,1]{1,0,2:T(8,128)S(1)}, ...), condition=%wide.region_16.17_spmd.clone.clone, body=%wide.region_11.16_spmd.sunk.clone.clone.sunk | while | flops 419194656 | bytes 32637632 | solution.py:204
  590.0 51.8 %all-gather.21.cloned.1.call-done = bf16[3072,1024]{1,0:T(8,128)(2,1)} async-done(((bf16[192,1024]{1,0:T(8,128)(2,1)}), bf16[3072,1024]{1,0:T(8,128)(2,1)}) %all-gather.21.cloned.1.call-update) | async-done | bytes 6291472 | tf_op jit(solution)/shard_map/all_gather | solution.py:226
  641.8 8.8 copy.132
  650.5 55.1 %while.63 = (s32[]{:T(128)}, f32[192,16,64]{0,2,1:T(8,128)}, s32[3]{0:T(128)S(1)}, bf16[3072,1024]{0,1:T(8,128)(2,1)}, s32[192]{0:T(256)S(1)}, /*index=5*/s32[1,...) while((s32[]{:T(128)}, f32[192,16,64]{0,2,1:T(8,128)}, ...), condition=%wide.region_20.21_spmd.clone.clone, body=%wide.region_17.20_spmd.sunk.clone.clone.sunk | while | flops 815934208 | bytes 14992073 | solution.py:204
  720.1 9.9 fusion.51
  749.8 53.1 %while.64 = (s32[]{:T(128)}, f32[16,192,1]{1,2,0:T(1,128)S(1)}, s32[192]{0:T(256)S(1)}, s32[1,6]{1,0:T(1,128)S(1)}, s32[]{:T(128)}, /*index=5*/s32[3]{0:T(128)S(...) while((s32[]{:T(128)}, f32[16,192,1]{1,2,0:T(1,128)S(1)}, ...), condition=%wide.region_29.30_spmd.clone.clone, body=%wide.region_25.29_spmd.sunk.clone.clone.sunk | while | flops 818689792 | bytes 39027408 | solution.py:204
  815.4 263.0 %while.65 = (s32[]{:T(128)}, f32[192,16,64]{0,2,1:T(8,128)}, f32[3072,1024]{1,0:T(8,128)}, f32[3072,1024]{1,0:T(8,128)}, s32[3]{0:T(128)S(1)}, /*index=5*/bf16[3...) while((s32[]{:T(128)}, f32[192,16,64]{0,2,1:T(8,128)}, ...), condition=%wide.region_33.34_spmd.clone.clone, body=%wide.region_30.33_spmd.sunk.clone.clone.sunk | while | flops 2041719552 | bytes 198845264 | solution.py:204
  825.9 8.8 constant_dynamic-slice_fusion.18
  880.2 11.8 dynamic_update_slice.21
  892.0 11.8 dynamic_update_slice.20
  913.9 8.7 constant_dynamic-slice_fusion.18
  968.0 11.8 dynamic_update_slice.21
  979.8 11.8 dynamic_update_slice.20
  1055.7 11.3 dynamic_update_slice.21
  1067.0 11.2 dynamic_update_slice.20
  1119.8 112.0 %reduce-scatter.15.cloned.1.call-done = bf16[192,1024]{1,0:T(8,128)(2,1)} async-done(((bf16[3072,1024]{1,0:T(8,128)(2,1)}), bf16[192,1024]{1,0:T(8,128)(2,1)}) %reduce-scatter.15.cloned.1.call-update) | async-done | bytes 393232 | tf_op jit(solution)/shard_map/reduce_scatter | solution.py:327
  1242.0 139.4 %reduce-scatter.17.cloned.1.call-done = bf16[192,1024]{1,0:T(8,128)(2,1)} async-done(((bf16[3072,1024]{1,0:T(8,128)(2,1)}), bf16[192,1024]{1,0:T(8,128)(2,1)}) %reduce-scatter.17.cloned.1.call-update) | async-done | bytes 393232 | tf_op jit(solution)/shard_map/reduce_scatter | solution.py:330
  1395.6 165.0 %reduce-scatter.27.cloned.1.call-done = bf16[1024,256]{1,0:T(8,128)(2,1)} async-done(((bf16[1024,4096]{1,0:T(8,128)(2,1)}), bf16[1024,256]{1,0:T(8,128)(2,1)}) %reduce-scatter.27.cloned.1.call-update) | async-done | bytes 524304 | tf_op jit(solution)/shard_map/reduce_scatter | solution.py:374
  1563.6 179.4 %reduce-scatter.31.cloned.1.call-done = bf16[4096,64]{0,1:T(8,128)(2,1)} async-done(((bf16[4096,1024]{0,1:T(8,128)(2,1)}), bf16[4096,64]{0,1:T(8,128)(2,1)}) %reduce-scatter.31.cloned.1.call-update) | async-done | bytes 524304 | tf_op jit(solution)/shard_map/reduce_scatter | solution.py:377
  1747.1 12.5 convolution_convert_fusion
  1759.6 16.7 copy.147
  1793.0 43.9 %all-reduce = (f32[4096]{0:T(1024)S(1)}, f32[8,1024]{1,0:T(8,128)S(1)}) all-reduce(f32[4096]{0:T(1024)S(1)} %multiply_reduce_fusion, f32[8,1024]{1,0:T(8,128)S(1)} %pad_maximum_fusion.14), channel_id=1, replica_groups=mesh['dp'=2,'wide'=16] {'dp','wide'}, use_global_device_ids=true, to_apply=%region_43.44 | all-reduce | flops 12288 | bytes 98304 | tf_op jit(solution)/shard_map/psum | solution.py:364
  1839.6 45.2 %all-reduce.3.cloned.1.call-done = f32[32,1024]{1,0:T(8,128)} async-done(((f32[32,1024]{1,0:T(8,128)}), f32[32,1024]{1,0:T(8,128)}) %all-reduce.3.cloned.1.call-update) | async-done | bytes 131088 | tf_op jit(solution)/shard_map/psum | solution.py:364
  1885.7 149.2 %reduce-scatter.19.cloned.1.call-done = bf16[1024,192]{0,1:T(8,128)(2,1)} async-done(((bf16[1024,3072]{0,1:T(8,128)(2,1)}), bf16[1024,192]{0,1:T(8,128)(2,1)}) %reduce-scatter.19.cloned.1.call-update) | async-done | bytes 393232 | tf_op jit(solution)/shard_map/reduce_scatter | solution.py:368
  2046.4 9.3 reduce-scatter.33.cloned.1.call-done
  2057.7 208.9 %reduce-scatter.37.cloned.1.call-done = bf16[384,1024]{1,0:T(8,128)(2,1)} async-done(((bf16[6144,1024]{1,0:T(8,128)(2,1)}), bf16[384,1024]{1,0:T(8,128)(2,1)}) %reduce-scatter.37.cloned.1.call-update) | async-done | bytes 786448
  (602 shorter events, 553.2 us)
Async XLA Ops:
  7.2 102.1 %all-gather.13.cloned.1.call-start = ((), (), s32[]{:S(2)}) async-start(), calls=%async_computation.12 | async-start | bytes 6684672 | tf_op jit(solution)/shard_map/all_gather | solution.py:155
  9.2 169.8 %all-gather.17.cloned.1.call-start = ((), (), s32[]{:S(2)}) async-start(), calls=%async_computation.14 | async-start | bytes 3342336 | tf_op jit(solution)/shard_map/all_gather | solution.py:150
  10.9 193.1 %all-gather.15.cloned.1.call-start = ((), (), s32[]{:S(2)}) async-start(), calls=%async_computation.13 | async-start | bytes 18874368 | tf_op jit(solution)/shard_map/all_gather | solution.py:161
  109.4 114.0 %all-gather.19.cloned.1.call-start = ((), (), s32[]{:S(2)}) async-start(), calls=%async_computation.15 | async-start | bytes 9437184 | tf_op jit(solution)/shard_map/all_gather | solution.py:157
  179.0 104.0 %all-gather.25.cloned.1.call-start = ((), (), s32[]{:S(2)}) async-start(), calls=%async_computation.18 | async-start | bytes 1114112 | tf_op jit(solution)/shard_map/all_gather | solution.py:151
  180.7 180.5 %all-gather.33.cloned.1.call-start = ((), (), s32[]{:S(2)}) async-start(), calls=%async_computation.22 | async-start | bytes 4456448 | tf_op jit(solution)/shard_map/all_gather | solution.py:153
  182.5 267.7 %all-gather.29.cloned.1.call-start = ((), (), s32[]{:S(2)}) async-start(), calls=%async_computation.20 | async-start | bytes 4456448 | tf_op jit(solution)/shard_map/all_gather | solution.py:152
  184.4 361.6 %all-gather.23.cloned.1.call-start = ((), (), s32[]{:S(2)}) async-start(), calls=%async_computation.17 | async-start | bytes 6684672 | tf_op jit(solution)/shard_map/all_gather | solution.py:225
  184.5 10.1 collective-permute-start
  187.8 6.8 collective-permute-start.1
  191.2 552.6 %copy-start.58 = (f32[192]{0:T(256)}, f32[192]{0:T(256)S(1)}, u32[]{:S(2)}) copy-start(f32[192]{0:T(256)S(1)} %get-tuple-element.1373) | copy-start | bytes 2308
  196.6 510.4 %copy-start.7 = (f32[192,1024]{1,0:T(8,128)}, f32[192,1024]{1,0:T(8,128)S(1)}, u32[]{:S(2)}) copy-start(f32[192,1024]{1,0:T(8,128)S(1)} %get-tuple-element.1437) | copy-start | bytes 2359300
  247.1 394.7 %all-gather.21.cloned.1.call-start = ((), (), s32[]{:S(2)}) async-start(), calls=%async_computation.16 | async-start | bytes 6684672 | tf_op jit(solution)/shard_map/all_gather | solution.py:226
  248.0 459.0 %all-gather.27.cloned.1.call-start = ((), (), s32[]{:S(2)}) async-start(), calls=%async_computation.19 | async-start | bytes 3145728 | tf_op jit(solution)/shard_map/all_gather | solution.py:158
  283.1 429.9 %all-gather.35.cloned.1.call-start = ((), (), s32[]{:S(2)}) async-start(), calls=%async_computation.23 | async-start | bytes 12582912 | tf_op jit(solution)/shard_map/all_gather | solution.py:160
  361.2 358.9 %all-gather.31.cloned.1.call-start = ((), (), s32[]{:S(2)}) async-start(), calls=%async_computation.21 | async-start | bytes 12582912 | tf_op jit(solution)/shard_map/all_gather | solution.py:159
  450.2 669.5 %reduce-scatter.23.cloned.1.call-start = ((), (), s32[]{:S(2)}) async-start(), calls=%async_computation.28 | async-start | bytes 2228224 | tf_op jit(solution)/shard_map/reduce_scatter | solution.py:371
  803.0 428.8 %reduce-scatter.15.cloned.1.call-start = ((), (), s32[]{:S(2)}) async-start(), calls=%async_computation.24 | async-start | bytes 6684672 | tf_op jit(solution)/shard_map/reduce_scatter | solution.py:327
  1086.6 294.8 %reduce-scatter.17.cloned.1.call-start = ((), (), s32[]{:S(2)}) async-start(), calls=%async_computation.25 | async-start | bytes 6684672 | tf_op jit(solution)/shard_map/reduce_scatter | solution.py:330
  1095.1 465.5 %reduce-scatter.27.cloned.1.call-start = ((), (), s32[]{:S(2)}) async-start(), calls=%async_computation.30 | async-start | bytes 8912896 | tf_op jit(solution)/shard_map/reduce_scatter | solution.py:374
  1102.2 640.8 %reduce-scatter.31.cloned.1.call-start = ((), (), s32[]{:S(2)}) async-start(), calls=%async_computation.32 | async-start | bytes 8912896 | tf_op jit(solution)/shard_map/reduce_scatter | solution.py:377
  1110.0 675.1 %reduce-scatter.25.cloned.1.call-start = ((), (), s32[]{:S(2)}) async-start(), calls=%async_computation.29 | async-start | bytes 196608 | tf_op jit(solution)/shard_map/reduce_scatter | solution.py:389
  1119.8 765.0 %all-reduce.3.cloned.1.call-start = ((), (), s32[]{:S(2)}) async-start(), calls=%async_computation.35 | async-start | bytes 262144 | tf_op jit(solution)/shard_map/psum | solution.py:364
  1390.6 644.3 %reduce-scatter.19.cloned.1.call-start = ((), (), s32[]{:S(2)}) async-start(), calls=%async_computation.26 | async-start | bytes 6684672 | tf_op jit(solution)/shard_map/reduce_scatter | solution.py:368
  1395.5 648.7 %reduce-scatter.29.cloned.1.call-start = ((), (), s32[]{:S(2)}) async-start(), calls=%async_computation.31 | async-start | bytes 786432 | tf_op jit(solution)/shard_map/reduce_scatter | solution.py:392
  1560.6 495.2 %reduce-scatter.33.cloned.1.call-start = ((), (), s32[]{:S(2)}) async-start(), calls=%async_computation.33 | async-start | bytes 786432 | tf_op jit(solution)/shard_map/reduce_scatter | solution.py:395
  1743.0 523.7 %reduce-scatter.37.cloned.1.call-start = ((), (), s32[]{:S(2)}) async-start(), calls=%async_computation.36 | async-start | bytes 13369344
  1776.3 499.9 %reduce-scatter.21.cloned.1.call-start = ((), (), s32[]{:S(2)}) async-start(), calls=%async_computation.27 | async-start | bytes 589824 | tf_op jit(solution)/shard_map/reduce_scatter | solution.py:386
  1788.3 267.4 %copy-start.28 = (f32[3,2048,64]{1,2,0:T(8,128)S(1)}, f32[3,2048,64]{1,2,0:T(8,128)}, u32[]{:S(2)}) copy-start(f32[3,2048,64]{1,2,0:T(8,128)} %param.42) | copy-start | bytes 4718596
  1788.4 50.4 %collective-permute-start.2 = (f32[32,1]{1,0:T(8,128)S(1)}, f32[32,1]{1,0:T(8,128)S(1)}, u32[]{:S(2)}, u32[]{:S(2)}) collective-permute-start(f32[32,1]{1,0:T(8,128)S(1)} %get-tuple-element.1430), channel_id=1, source_target_pairs={{0,1},{1,2},{2,3},{3,4},{4,5},{5,6},{6,7},{7,8},{8,9},{9,10},{10,1... | collective-permute-start | bytes 392 | tf_op jit(solution)/shard_map/ppermute | solution.py:34
  1791.7 47.1 %collective-permute-start.3 = (f32[32,1]{1,0:T(8,128)S(1)}, f32[32,1]{1,0:T(8,128)S(1)}, u32[]{:S(2)}, u32[]{:S(2)}) collective-permute-start(f32[32,1]{1,0:T(8,128)S(1)} %get-tuple-element.1431), channel_id=1, source_target_pairs={{1,0},{2,1},{3,2},{4,3},{5,4},{6,5},{7,6},{8,7},{9,8},{10,9},{11,1... | collective-permute-start | bytes 392 | tf_op jit(solution)/shard_map/ppermute | solution.py:36
  2034.9 253.6 %reduce-scatter.35.cloned.1.call-start = ((), (), s32[]{:S(2)}) async-start(), calls=%async_computation.34 | async-start | bytes 1179648 | tf_op jit(solution)/shard_map/reduce_scatter | solution.py:398
  (89 other events, 2708.2 us)
Sparse Core Ops, SparseCore 0:
  11.3 97.9 all-gather.12
  112.7 66.3 all-gather.16
  180.6 23.3 all-gather.14
  205.4 17.9 all-gather.18
  226.6 56.4 all-gather.24
  286.2 74.8 all-gather.32
  364.4 85.7 all-gather.28
  453.5 92.3 all-gather.22
  549.3 92.4 all-gather.20
  643.2 8.8 all-gather.26
  653.6 21.0 all-gather.34
  676.1 21.0 all-gather.30
  803.1 79.7 reduce-scatter.22
  1086.8 144.9 reduce-scatter.14
  1236.9 144.4 reduce-scatter.16
  1383.6 176.9 reduce-scatter.26
  1562.7 180.2 reduce-scatter.30
  1745.0 9.8 reduce-scatter.24
  1761.1 123.6 all-reduce.2
  1889.8 144.9 reduce-scatter.18
  2037.1 7.0 reduce-scatter.28
  2046.6 9.1 reduce-scatter.32
  2061.4 205.1 reduce-scatter.36
  2268.8 7.3 reduce-scatter.20
  2279.1 9.3 reduce-scatter.34
where the time goes:
time: 2310 us; the launch traced here: 2300 us
  waiting for transfers between devices  1560 us (68%)
  local copies, waits for them, and re-layouts  327 us (14%)
  matrix products  195 us (8%)
  other arithmetic  121 us (5%)
  blocking collectives  43.9 us (2%)
  loops' own time  25.2 us (1%)
    unnamed x26, waiting for transfers between devices  209 us
    reduce_scatter x1, waiting for transfers between devices, shards(): lax.psum_scatter(dw_down.astype(jnp.bfloat16), 'wide', scatter_dimension=...  179 us
    reduce_scatter x1, waiting for transfers between devices, shards(): lax.psum_scatter(dw_up.astype(jnp.bfloat16), 'wide', scatter_dimension=1,...  165 us
    reduce_scatter x1, waiting for transfers between devices, shards(): lax.psum_scatter(dw_qkv.astype(jnp.bfloat16), 'wide', scatter_dimension=1...  149 us
    reduce_scatter x1, waiting for transfers between devices, shards(): lax.psum_scatter(d_values.astype(jnp.bfloat16), 'wide', scatter_dimension...  139 us
    reduce_scatter x1, waiting for transfers between devices, shards(): lax.psum_scatter(d_keys.astype(jnp.bfloat16), 'wide', scatter_dimension=0...  112 us
    all_gather x1, waiting for transfers between devices, shards(): ada_piece = lax.all_gather(masters[4], 'wide', axis=1, tiled=True)  98.3 us
    all_gather x1, waiting for transfers between devices, shards(): lax.all_gather(keys_low, 'wide', axis=0, tiled=True)  95.2 us
  transfers between devices with their start and end apart: 29, of which 20 were waited for; matrix products, arithmetic and copies ran while one was open for 24% of the time, Pallas kernels for 0%

commit v1 on v0

--- a/solution.py
+++ b/solution.py
@@ -1,8 +1,12 @@
+import functools
 import math
 
 import jax
 import jax.numpy as jnp
+import numpy as np
 from jax import lax
+from jax.experimental import pallas as pl
+from jax.experimental.pallas import tpu as pltpu
 from jax.sharding import PartitionSpec as P
 
 HEADS = 16
@@ -444,7 +448,996 @@
     )
 
 
+MESH_ID = pl.DeviceIdType.MESH
+ANY = pl.BlockSpec(memory_space=pl.ANY)
+VM = pl.BlockSpec(memory_space=pltpu.VMEM)
+VMEM_BYTES = 56 * 1024 * 1024
+LANES = 128
+HALF_LANES = 64
+BIG = 1e30
+
+
+def nt(left_side, right_side):
+    return lax.dot_general(
+        left_side, right_side, (((1,), (1,)), ((), ())), preferred_element_type=jnp.float32
+    )
+
+
+def nn(left_side, right_side):
+    return lax.dot_general(
+        left_side, right_side, (((1,), (0,)), ((), ())), preferred_element_type=jnp.float32
+    )
+
+
+def entry_barrier(peers):
+    barrier = pltpu.get_barrier_semaphore()
+    for peer in peers:
+        pl.semaphore_signal(barrier, inc=1, device_id=peer, device_id_type=MESH_ID)
+    pl.semaphore_wait(barrier, len(peers))
+
+
+def place():
+    core, wide = lax.axis_index("dp"), lax.axis_index("wide")
+    return core, wide // 4, wide % 4
+
+
+def at_dev(core, z, yx):
+    return (core, z * 4 + yx)
+
+
+def gather_kernel(count, has_small, *refs):
+    shards = refs[:count]
+    small = refs[count] if has_small else None
+    base = count + has_small
+    fulls = refs[base : base + count]
+    small_out = refs[base + count] if has_small else None
+    sems = refs[base + count + has_small :]
+    send_x, send_y, send_z, send_s, recv_i, recv_s, local = sems[:7]
+    core, z, yx = place()
+    x_dev, y_dev = at_dev(core, z, yx ^ 1), at_dev(core, z, yx ^ 2)
+    sib = at_dev(1 - core, z, yx)
+    z_devs = [None] + [at_dev(core, lax.rem(z + r, 4), yx) for r in (1, 2, 3)]
+    wide = z * 4 + yx
+    if has_small:
+        everyone = [(core, wide ^ r) for r in range(1, 16)]
+        entry_barrier(everyone + [sib])
+    else:
+        entry_barrier([x_dev, y_dev, sib] + z_devs[1:])
+    pending = []
+
+    def spot(full, dz, d):
+        return full.at[core, lax.rem(z + dz, 4), yx ^ d]
+
+    def push(i, dz, d, src, sem, device, there):
+        copy = pltpu.make_async_remote_copy(
+            src_ref=src,
+            dst_ref=spot(fulls[i], dz, d),
+            send_sem=sem,
+            recv_sem=there,
+            device_id=device,
+            device_id_type=MESH_ID,
+        )
+        copy.start()
+        pending.append(copy)
+
+    def to_x(i, dz, d, src):
+        push(i, dz, d, src, send_x.at[i, dz, d], x_dev, recv_i.at[i, dz, d ^ 1])
+
+    def to_y(i, dz, d, src):
+        push(i, dz, d, src, send_y.at[i, dz, d], y_dev, recv_i.at[i, dz, d ^ 2])
+
+    def to_s(i, dz, d, src):
+        push(i, dz, d, src, send_s.at[i, dz, d], sib, recv_s.at[i, dz, d])
+
+    def arrive(ref, sem):
+        pltpu.make_async_copy(ref, ref, sem).wait()
+
+    def got(i, dz, d):
+        ref = spot(fulls[i], dz, d)
+        arrive(ref, recv_i.at[i, dz, d])
+        return ref
+
+    small_copies = []
+    if has_small:
+        small_send, small_recv, small_local = sems[7:]
+        own = pltpu.make_async_copy(small, small_out.at[wide], small_local)
+        own.start()
+        small_copies.append(own)
+        for r in range(1, 16):
+            copy = pltpu.make_async_remote_copy(
+                src_ref=small,
+                dst_ref=small_out.at[wide],
+                send_sem=small_send.at[r],
+                recv_sem=small_recv.at[r],
+                device_id=(core, wide ^ r),
+                device_id_type=MESH_ID,
+            )
+            copy.start()
+            small_copies.append(copy)
+    locals_ = []
+    for i in range(count):
+        src = shards[i]
+        for r in (1, 3, 2):
+            push(i, 0, 0, src, send_z.at[i, r], z_devs[r], recv_i.at[i, (4 - r) % 4, 0])
+        to_x(i, 0, 0, src)
+        to_y(i, 0, 0, src)
+        to_s(i, 0, 0, src)
+        copy = pltpu.make_async_copy(src, spot(fulls[i], 0, 0), local.at[i])
+        copy.start()
+        locals_.append(copy)
+    for i in range(count):
+        ref = got(i, 0, 1)
+        to_y(i, 0, 1, ref)
+        to_s(i, 0, 1, ref)
+        ref = got(i, 0, 2)
+        to_s(i, 0, 2, ref)
+    for i in range(count):
+        for dz in (1, 3, 2):
+            ref = got(i, dz, 0)
+            to_x(i, dz, 0, ref)
+            to_y(i, dz, 0, ref)
+            to_s(i, dz, 0, ref)
+        for dz in (1, 3, 2):
+            ref = got(i, dz, 1)
+            if dz == 1:
+                to_y(i, dz, 1, ref)
+            to_s(i, dz, 1, ref)
+            ref = got(i, dz, 2)
+            if dz != 1:
+                to_x(i, dz, 2, ref)
+            to_s(i, dz, 2, ref)
+    for i in range(count):
+        for dz in (0, 1, 3, 2):
+            to_s(i, dz, 3, got(i, dz, 3))
+    for i in range(count):
+        for dz in range(4):
+            for d in range(4):
+                ref = fulls[i].at[1 - core, lax.rem(z + dz, 4), yx ^ d]
+                arrive(ref, recv_s.at[i, dz, d])
+    for copy in pending:
+        copy.wait_send()
+    for copy in locals_ + small_copies:
+        copy.wait()
+
+
+def gather_weights(shards, small, call_id):
+    count, has_small = len(shards), int(small is not None)
+    dma = pltpu.SemaphoreType.DMA
+    scratch = [
+        dma((count, 4, 4)),
+        dma((count, 4, 4)),
+        dma((count, 4)),
+        dma((count, 4, 4)),
+        dma((count, 4, 4)),
+        dma((count, 4, 4)),
+        dma((count,)),
+    ]
+    outs = [jax.ShapeDtypeStruct((2, 4, 4) + s.shape, s.dtype) for s in shards]
+    args = list(shards)
+    if has_small:
+        scratch += [dma((16,)), dma((16,)), dma]
+        outs.append(jax.ShapeDtypeStruct((16,) + small.shape, small.dtype))
+        args.append(small)
+    return pl.pallas_call(
+        functools.partial(gather_kernel, count, has_small),
+        out_shape=outs,
+        in_specs=[ANY] * len(args),
+        out_specs=[ANY] * len(outs),
+        scratch_shapes=scratch,
+        compiler_params=pltpu.CompilerParams(
+            collective_id=call_id, has_side_effects=True, vmem_limit_bytes=VMEM_BYTES
+        ),
+    )(*args)
+
+
+def scatter_kernel(count, *refs):
+    parts = refs[:count]
+    outs = refs[count : 2 * count]
+    bufs = refs[2 * count : 2 * count + 8 * count]
+    sems = refs[2 * count + 8 * count :]
+    send, recv = sems
+    core, z, yx = place()
+    x_dev, y_dev = at_dev(core, z, yx ^ 1), at_dev(core, z, yx ^ 2)
+    z_devs = [None] + [at_dev(core, lax.rem(z + r, 4), yx) for r in (1, 2, 3)]
+    entry_barrier([x_dev, y_dev] + z_devs[1:])
+    pending = []
+
+    def push(i, slot, src, dst, device):
+        copy = pltpu.make_async_remote_copy(
+            src_ref=src,
+            dst_ref=dst,
+            send_sem=send.at[i, slot],
+            recv_sem=recv.at[i, slot],
+            device_id=device,
+            device_id_type=MESH_ID,
+        )
+        copy.start()
+        pending.append(copy)
+        return copy
+
+    def part(i, dz, d):
+        return parts[i].at[lax.rem(z + dz, 4), yx ^ d]
+
+    def f32(ref):
+        return ref[...].astype(jnp.float32)
+
+    arrivals = []
+    for i in range(count):
+        a_x, a_y, r_x, r_y, t_x, t_y, s_z, r_z = bufs[8 * i : 8 * i + 8]
+        here = {}
+        for j, dz in enumerate((0, 1)):
+            here["ax", dz] = push(i, j, part(i, dz, 3), a_x.at[j], x_dev)
+        for j, dz in enumerate((2, 3)):
+            here["ay", dz] = push(i, 2 + j, part(i, dz, 3), a_y.at[j], y_dev)
+        for j, dz in enumerate((0, 1)):
+            here["rx", dz] = push(i, 4 + dz, part(i, dz, 1), r_x.at[dz], x_dev)
+        for j, dz in enumerate((2, 3)):
+            here["ry", dz] = push(i, 8 + dz, part(i, dz, 2), r_y.at[dz], y_dev)
+        arrivals.append(here)
+    for i in range(count):
+        a_x, a_y, r_x, r_y, t_x, t_y, s_z, r_z = bufs[8 * i : 8 * i + 8]
+        here = arrivals[i]
+        for j, (low, high) in enumerate(((1, 2), (0, 3))):
+            here["ax", low].wait_recv()
+            t_y[j] = (f32(part(i, low, 2)) + f32(a_x.at[low])).astype(jnp.bfloat16)
+            here["ry", low] = push(i, 8 + low, t_y.at[j], r_y.at[low], y_dev)
+            here["ay", high].wait_recv()
+            t_x[j] = (f32(part(i, high, 1)) + f32(a_y.at[high - 2])).astype(jnp.bfloat16)
+            here["rx", high] = push(i, 4 + high, t_x.at[j], r_x.at[high], x_dev)
+    for i in range(count):
+        a_x, a_y, r_x, r_y, t_x, t_y, s_z, r_z = bufs[8 * i : 8 * i + 8]
+        here = arrivals[i]
+        for dz in (1, 2, 3, 0):
+            here["rx", dz].wait_recv()
+            here["ry", dz].wait_recv()
+            total = f32(part(i, dz, 0)) + f32(r_x.at[dz]) + f32(r_y.at[dz])
+            if dz:
+                s_z[dz - 1] = total.astype(jnp.bfloat16)
+                here["rz", dz] = push(i, 12 + dz, s_z.at[dz - 1], r_z.at[dz - 1], z_devs[dz])
+            else:
+                outs[i][...] = total
+    for i in range(count):
+        r_z = bufs[8 * i + 7]
+        for dz in (1, 2, 3):
+            arrivals[i]["rz", dz].wait_recv()
+        outs[i][...] += f32(r_z.at[0]) + f32(r_z.at[1]) + f32(r_z.at[2])
+    for copy in pending:
+        copy.wait_send()
+
+
+def scatter_grads(parts, call_id):
+    count = len(parts)
+    scratch = []
+    for part in parts:
+        for depth in (2, 2, 4, 4, 2, 2, 3, 3):
+            scratch.append(pltpu.VMEM((depth,) + part.shape[2:], jnp.bfloat16))
+    dma = pltpu.SemaphoreType.DMA
+    scratch += [dma((count, 16)), dma((count, 16))]
+    return pl.pallas_call(
+        functools.partial(scatter_kernel, count),
+        out_shape=[jax.ShapeDtypeStruct(part.shape[2:], jnp.float32) for part in parts],
+        in_specs=[VM] * count,
+        out_specs=[VM] * count,
+        scratch_shapes=scratch,
+        compiler_params=pltpu.CompilerParams(
+            collective_id=call_id, has_side_effects=True, vmem_limit_bytes=VMEM_BYTES
+        ),
+    )(*parts)
+
+
+def small_kernel(ada_rows, slots, part_ref, ada_ref, all_ref, landed, summed, other, mine, *sems):
+    send_a, recv_a, send_b, recv_b, send_s, recv_s = sems
+    core, z, yx = place()
+    wide = z * 4 + yx
+    sib = (1 - core, wide)
+    peers = [(core, wide ^ r) for r in range(1, 16)]
+    entry_barrier(peers + [sib])
+    first = []
+    for r in range(1, 16):
+        copy = pltpu.make_async_remote_copy(
+            src_ref=part_ref.at[wide ^ r],
+            dst_ref=landed.at[r],
+            send_sem=send_a.at[r],
+            recv_sem=recv_a.at[r],
+            device_id=peers[r - 1],
+            device_id_type=MESH_ID,
+        )
+        copy.start()
+        first.append(copy)
+    total = part_ref[wide]
+    for r, copy in enumerate(first):
+        copy.wait_recv()
+        total = total + landed[r + 1]
+    summed[...] = total
+    swap = pltpu.make_async_remote_copy(
+        src_ref=summed,
+        dst_ref=other,
+        send_sem=send_s,
+        recv_sem=recv_s,
+        device_id=sib,
+        device_id_type=MESH_ID,
+    )
+    swap.start()
+    swap.wait()
+    ada_ref[core] = summed[0:ada_rows]
+    ada_ref[1 - core] = other[0:ada_rows]
+    both = summed[...] + other[...]
+    rest = both.shape[0] - ada_rows
+    width = ada_rows // slots
+    bias = both[0:width]
+    for j in range(1, slots):
+        bias = bias + both[j * width : (j + 1) * width]
+    mine[0:rest] = both[ada_rows:]
+    mine[rest : rest + width] = bias
+    all_ref[wide] = mine[...]
+    second = []
+    for r in range(1, 16):
+        copy = pltpu.make_async_remote_copy(
+            src_ref=mine,
+            dst_ref=all_ref.at[wide],
+            send_sem=send_b.at[r],
+            recv_sem=recv_b.at[r],
+            device_id=peers[r - 1],
+            device_id_type=MESH_ID,
+        )
+        copy.start()
+        second.append(copy)
+    for copy in second:
+        copy.wait_recv()
+    for copy in first + second:
+        copy.wait_send()
+
+
+def small_sums(parts, ada_rows, slots, call_id):
+    rows = parts.shape[1]
+    out_rows = rows - ada_rows + ada_rows // slots
+    dma = pltpu.SemaphoreType.DMA
+    f32 = jnp.float32
+    return pl.pallas_call(
+        functools.partial(small_kernel, ada_rows, slots),
+        out_shape=[
+            jax.ShapeDtypeStruct((2, ada_rows, LANES), f32),
+            jax.ShapeDtypeStruct((16, out_rows, LANES), f32),
+        ],
+        in_specs=[VM],
+        out_specs=[VM, VM],
+        scratch_shapes=[
+            pltpu.VMEM((16, rows, LANES), f32),
+            pltpu.VMEM((rows, LANES), f32),
+            pltpu.VMEM((rows, LANES), f32),
+            pltpu.VMEM((out_rows, LANES), f32),
+            dma((16,)),
+            dma((16,)),
+            dma((16,)),
+            dma((16,)),
+            dma,
+            dma,
+        ],
+        compiler_params=pltpu.CompilerParams(collective_id=call_id, has_side_effects=True),
+    )(parts)
+
+
+def lane_iota(shape):
+    return lax.broadcasted_iota(jnp.int32, shape, len(shape) - 1)
+
+
+def swap_halves(pair):
+    return pltpu.roll(pair, HALF_LANES, 1)
+
+
+def head_sums(values):
+    width = values.shape[1]
+    rows = lax.broadcasted_iota(jnp.int32, (width, width), 0) // HALF_LANES
+    cols = lax.broadcasted_iota(jnp.int32, (width, width), 1) // HALF_LANES
+    ones = (rows == cols).astype(jnp.float32)
+    return lax.dot_general(
+        values,
+        ones,
+        (((1,), (0,)), ((), ())),
+        precision=HIGHEST_PRECISION,
+        preferred_element_type=jnp.float32,
+    )
+
+
+def qkv_kernel(h_ref, w_ref, gain_ref, pack_ref, kept_ref):
+    tokens, width = h_ref.shape
+    half = width // 2
+    mid = tokens // 2
+    group = 256
+    low = jnp.bfloat16
+    lane = lane_iota((tokens, LANES))
+    lane_mid = lane_iota((mid, LANES))
+
+    def project(first):
+        rows = pl.ds(first, group)
+        return nt(h_ref[:, :half], w_ref[0, rows, :]) + nt(h_ref[:, half:], w_ref[1, rows, :])
+
+    def step(g, carry):
+        first = pl.multiple_of(g * group, group)
+        q_all, k_all, v_all = (project(first + part * width) for part in range(3))
+        kept_ref[:, pl.ds(first, group)] = q_all
+        kept_ref[:, pl.ds(first + width, group)] = k_all
+        q_all = q_all * lax.rsqrt(head_sums(q_all * q_all) + NORM_EPS)
+        q_all = q_all * (8.0 * (1.0 + gain_ref[:, pl.ds(first, group)]))
+        k_all = k_all * lax.rsqrt(head_sums(k_all * k_all) + NORM_EPS)
+        for pair in range(group // LANES):
+            cols = slice(pair * LANES, (pair + 1) * LANES)
+            q, k, v = q_all[:, cols], k_all[:, cols], v_all[:, cols]
+            head = g * (group // HALF_LANES) + 2 * pair
+            pack_ref[head, 0:tokens, :] = jnp.where(lane < HALF_LANES, q, swap_halves(k)).astype(low)
+            pack_ref[head + 1, 0:tokens, :] = jnp.where(lane < HALF_LANES, swap_halves(q), k).astype(low)
+            v_a, v_b = v[:mid], v[mid:]
+            pack_ref[head, tokens:, :] = jnp.where(lane_mid < HALF_LANES, v_a, swap_halves(v_b)).astype(low)
+            pack_ref[head + 1, tokens:, :] = jnp.where(lane_mid < HALF_LANES, swap_halves(v_a), v_b).astype(low)
+        return carry
+
+    lax.fori_loop(0, width // group, step, 0)
+
+
+def project_heads(h_low, w_all, gain):
+    tokens, width = h_low.shape
+    return pl.pallas_call(
+        qkv_kernel,
+        out_shape=[
+            jax.ShapeDtypeStruct((HEADS, tokens + tokens // 2, LANES), jnp.bfloat16),
+            jax.ShapeDtypeStruct((tokens, 2 * width), jnp.float32),
+        ],
+        in_specs=[VM] * 3,
+        out_specs=[VM] * 2,
+        compiler_params=pltpu.CompilerParams(vmem_limit_bytes=VMEM_BYTES),
+    )(h_low, w_all, gain)
+
+
+def heads_back_kernel(got_ref, kept_ref, gain_ref, out_ref, gain_grad_ref):
+    tokens = kept_ref.shape[0]
+    width = kept_ref.shape[1] // 2
+    mid = tokens // 2
+    f32, low = jnp.float32, jnp.bfloat16
+    lane = lane_iota((tokens, LANES))
+    lane_mid = lane_iota((mid, LANES))
+
+    def unnormalize(values, grad):
+        inverse = lax.rsqrt(head_sums(values * values) + NORM_EPS)
+        unit = values * inverse
+        return inverse * (grad - unit * head_sums(unit * grad)), unit
+
+    def step(pair, carry):
+        cols = pl.ds(pl.multiple_of(pair * LANES, LANES), LANES)
+        key_cols = pl.ds(pl.multiple_of(pair * LANES + width, LANES), LANES)
+        val_cols = pl.ds(pl.multiple_of(pair * LANES + 2 * width, LANES), LANES)
+        even = got_ref[2 * pair].astype(f32)
+        odd = got_ref[2 * pair + 1].astype(f32)
+        even_qk, odd_qk = even[:tokens], odd[:tokens]
+        d_query = jnp.where(lane < HALF_LANES, even_qk, swap_halves(odd_qk))
+        d_key = jnp.where(lane < HALF_LANES, swap_halves(even_qk), odd_qk)
+        even_v, odd_v = even[tokens:], odd[tokens:]
+        out_ref[0:mid, val_cols] = jnp.where(lane_mid < HALF_LANES, even_v, swap_halves(odd_v)).astype(low)
+        out_ref[mid:, val_cols] = jnp.where(lane_mid < HALF_LANES, swap_halves(even_v), odd_v).astype(low)
+        scaled = d_query * (8.0 * (1.0 + gain_ref[:, cols]))
+        d_q, unit = unnormalize(kept_ref[:, cols], scaled)
+        gain_grad_ref[:, cols] = jnp.sum(d_query * unit, axis=0, keepdims=True) * 8.0
+        out_ref[:, cols] = d_q.astype(low)
+        out_ref[:, key_cols] = unnormalize(kept_ref[:, key_cols], d_key)[0].astype(low)
+        return carry
+
+    lax.fori_loop(0, width // LANES, step, 0)
+
+
+def heads_backward(got, kept, gain):
+    tokens, width = kept.shape[0], kept.shape[1] // 2
+    return pl.pallas_call(
+        heads_back_kernel,
+        out_shape=[
+            jax.ShapeDtypeStruct((tokens, 3 * width), jnp.bfloat16),
+            jax.ShapeDtypeStruct((1, width), jnp.float32),
+        ],
+        in_specs=[VM] * 3,
+        out_specs=[VM] * 2,
+        compiler_params=pltpu.CompilerParams(vmem_limit_bytes=VMEM_BYTES),
+    )(got, kept, gain)
+
+
+ROWS = 256
+CHUNK = 512
+
+
+def key_limits(group_len, slots):
+    short_total = sum(side * side for side in SHORT_SIDES)
+    long_total = sum(side * side for side in LONG_SIDES)
+    limits = [0] * (group_len // ROWS)
+    for longs in range(1, slots + 1):
+        for shorts in range(slots - longs + 1):
+            total = longs * long_total + shorts * short_total
+            if not group_len - short_total < total <= group_len:
+                continue
+            ends, position = [], 0
+            for long_side, short_side in zip(LONG_SIDES, SHORT_SIDES):
+                position += longs * long_side**2 + shorts * short_side**2
+                ends.append(position)
+            ends.append(group_len)
+            for block in range(len(limits)):
+                last = block * ROWS + ROWS - 1
+                seen = min(end for end in ends if end > last)
+                limits[block] = max(limits[block], -(-seen // LANES) * LANES)
+    return limits
+
+
+def same_limits(limits):
+    groups = []
+    for block, limit in enumerate(limits):
+        if groups and groups[-1][2] == limit:
+            groups[-1][1] = block + 1
+        else:
+            groups.append([block, block + 1, limit])
+    return groups
+
+
+def chunks_of(limit, step):
+    whole = limit // CHUNK
+
+    def body(c, carry):
+        step(pl.multiple_of(c * CHUNK, CHUNK), CHUNK)
+        return carry
+
+    lax.fori_loop(0, whole, body, 0)
+    if limit % CHUNK:
+        step(whole * CHUNK, limit % CHUNK)
+
+
+def fold_lanes(values, combine):
+    total = values[:, :LANES]
+    for j in range(1, values.shape[1] // LANES):
+        total = combine(total, values[:, j * LANES : (j + 1) * LANES])
+    return total
+
+
+def split_three(values):
+    high = values.astype(jnp.bfloat16).astype(jnp.float32)
+    rest = values - high
+    mid = rest.astype(jnp.bfloat16).astype(jnp.float32)
+    return high, mid, rest - mid
+
+
+def lanes_three(lane, first, values, otherwise):
+    high, mid, rest = split_three(values)
+    return jnp.where(
+        lane == first, high, jnp.where(lane == first + 1, mid, jnp.where(lane == first + 2, rest, otherwise))
+    )
+
+
+def attend_kernel(
+    groups, got_ref, starts_ref, ends_ref, rule_ref, out_ref, out32_ref, q_ref, k_ref, kt_ref, vt_ref, v_ref, s_ref
+):
+    owners = got_ref.shape[0]
+    tokens = got_ref.shape[1] * 2 // 3
+    mid = tokens // 2
+    f32, low = jnp.float32, jnp.bfloat16
+    two = 2 * tokens
+    lane = lane_iota((two, LANES))
+    lane_mid = lane_iota((mid, LANES))
+
+    def unpack(pair, carry):
+        first = pl.multiple_of(pair * two, two)
+        qk = jnp.concatenate([got_ref[2 * pair + e, 0:tokens, :].astype(f32) for e in range(2)], axis=0)
+        spot = first + lax.broadcasted_iota(jnp.int32, (two, LANES), 0)
+        runs = ((spot >= starts_ref[...]) & (spot < ends_ref[...])).astype(f32)
+        barred = nn(runs.astype(low), rule_ref[...])
+        rows = pl.ds(first, two)
+        q_ref[rows, :] = jnp.where(lane < HALF_LANES, qk, barred).astype(low)
+        tail = jnp.where(lane >= LANES - 3, 1.0, runs)
+        keys = jnp.where(lane < HALF_LANES, swap_halves(qk), tail)
+        k_ref[rows, :] = keys.astype(low)
+        kt_ref[:, rows] = keys.T.astype(low)
+        ones = ((lane_mid >= HALF_LANES) & (lane_mid < HALF_LANES + 3)).astype(f32)
+        pieces = []
+        for e in range(2):
+            v = got_ref[2 * pair + e, tokens:, :].astype(f32)
+            pieces.append(jnp.where(lane_mid < HALF_LANES, v, ones))
+            pieces.append(jnp.where(lane_mid < HALF_LANES, swap_halves(v), ones))
+        values = jnp.concatenate(pieces, axis=0)
+        v_ref[rows, :] = values.astype(low)
+        vt_ref[:, rows] = values.T.astype(low)
+        return carry
+
+    lax.fori_loop(0, owners // 2, unpack, 0)
+    lane_q = lane_iota((ROWS, LANES))
+
+    def query_block(limit, b, carry):
+        rows = pl.ds(pl.multiple_of(b * ROWS, ROWS), ROWS)
+        q = q_ref[rows, :]
+
+        def score(c, top):
+            cols = pl.ds(pl.multiple_of(c * CHUNK, CHUNK), CHUNK)
+            s = nn(q, kt_ref[:, cols])
+            s_ref[:, cols] = s
+            return jnp.maximum(top, fold_lanes(s, jnp.maximum))
+
+        whole, left = limit // CHUNK, limit % CHUNK
+        top = lax.fori_loop(0, whole, score, jnp.full((ROWS, LANES), -3e38, f32))
+        if left:
+            tail = slice(whole * CHUNK, limit)
+            s = nn(q, kt_ref[:, tail])
+            s_ref[:, tail] = s
+            top = jnp.maximum(top, fold_lanes(s, jnp.maximum))
+        peak = jnp.max(top, axis=1, keepdims=True)
+
+        def weigh(cols, carry):
+            total, acc = carry
+            p = jnp.exp(s_ref[:, cols] - peak)
+            return total + fold_lanes(p, jnp.add), acc + nn(p.astype(low), v_ref[cols, :])
+
+        zero = jnp.zeros((ROWS, LANES), f32)
+        total, acc = lax.fori_loop(
+            0,
+            whole,
+            lambda c, carry: weigh(pl.ds(pl.multiple_of(c * CHUNK, CHUNK), CHUNK), carry),
+            (zero, zero),
+        )
+        if left:
+            total, acc = weigh(slice(whole * CHUNK, limit), (total, acc))
+        total = jnp.sum(total, axis=1, keepdims=True)
+        out32_ref[rows, :] = acc / total
+        log_total = peak + jnp.log(total)
+        q_ref[rows, :] = lanes_three(lane_q, LANES - 3, -log_total, q.astype(f32)).astype(low)
+        return carry
+
+    for first, last, limit in groups:
+        lax.fori_loop(first, last, functools.partial(query_block, limit), 0)
+
+    def send_out(w, carry):
+        rows = pl.multiple_of(w * tokens, tokens)
+        a = out32_ref[pl.ds(rows, mid), :]
+        b = out32_ref[pl.ds(rows + mid, mid), :]
+        out_ref[w] = jnp.where(lane_mid < HALF_LANES, a, swap_halves(b)).astype(low)
+        return carry
+
+    lax.fori_loop(0, owners, send_out, 0)
+
+
+def attend(got, starts, ends, rule, groups):
+    owners, packed, _ = got.shape
+    tokens = packed * 2 // 3
+    group_len = owners * tokens
+    low = jnp.bfloat16
+    whole = jax.ShapeDtypeStruct((group_len, LANES), low)
+    flipped = jax.ShapeDtypeStruct((LANES, group_len), low)
+    return pl.pallas_call(
+        functools.partial(attend_kernel, groups),
+        out_shape=[
+            jax.ShapeDtypeStruct((owners, tokens // 2, LANES), low),
+            jax.ShapeDtypeStruct((group_len, LANES), jnp.float32),
+            whole,
+            whole,
+            flipped,
+            flipped,
+        ],
+        in_specs=[VM] * 4,
+        out_specs=[VM] * 6,
+        scratch_shapes=[
+            pltpu.VMEM((group_len, LANES), low),
+            pltpu.VMEM((ROWS, group_len), jnp.float32),
+        ],
+        compiler_params=pltpu.CompilerParams(vmem_limit_bytes=VMEM_BYTES),
+    )(got, starts, ends, rule)
+
+
+def attend_back_kernel(
+    groups, got_ref, out32_ref, q_ref, k_ref, kt_ref, vt_ref, pack_ref, g_ref, gt_ref, qt_ref, dq_ref, dkt_ref, dvt_ref
+):
+    owners = got_ref.shape[0]
+    mid = got_ref.shape[1]
+    tokens = 2 * mid
+    two = 2 * tokens
+    f32, low = jnp.float32, jnp.bfloat16
+    lane = lane_iota((two, LANES))
+    lane_mid = lane_iota((mid, LANES))
+
+    def unpack(pair, carry):
+        rows = pl.ds(pl.multiple_of(pair * two, two), two)
+        pieces = []
+        for e in range(2):
+            g = got_ref[2 * pair + e].astype(f32)
+            pieces += [g, swap_halves(g)]
+        grad = jnp.where(lane < HALF_LANES, jnp.concatenate(pieces, axis=0), 0.0)
+        delta = jnp.sum(grad * out32_ref[rows, :], axis=1, keepdims=True)
+        grad = lanes_three(lane, HALF_LANES, -delta, grad)
+        g_ref[rows, :] = grad.astype(low)
+        gt_ref[:, rows] = grad.T[:HALF_LANES].astype(low)
+        qt_ref[:, rows] = q_ref[rows, :].astype(f32).T[:HALF_LANES].astype(low)
+        return carry
+
+    lax.fori_loop(0, owners // 2, unpack, 0)
+    dkt_ref[...] = jnp.zeros_like(dkt_ref)
+    dvt_ref[...] = jnp.zeros_like(dvt_ref)
+
+    def query_block(limit, b, carry):
+        rows = pl.ds(pl.multiple_of(b * ROWS, ROWS), ROWS)
+        q, g = q_ref[rows, :], g_ref[rows, :]
+        qt, gt = qt_ref[:, rows], gt_ref[:, rows]
+
+        def chunk(cols, acc):
+            p = jnp.exp(nn(q, kt_ref[:, cols]))
+            ds = (p * nn(g, vt_ref[:, cols])).astype(low)
+            dvt_ref[:, cols] += nn(gt, p.astype(low))
+            dkt_ref[:, cols] += nn(qt, ds)
+            return acc + nn(ds, k_ref[cols, :])
+
+        whole, left = limit // CHUNK, limit % CHUNK
+        acc = lax.fori_loop(
+            0,
+            whole,
+            lambda c, acc: chunk(pl.ds(pl.multiple_of(c * CHUNK, CHUNK), CHUNK), acc),
+            jnp.zeros((ROWS, LANES), f32),
+        )
+        if left:
+            acc = chunk(slice(whole * CHUNK, limit), acc)
+        dq_ref[rows, :] = acc
+        return carry
+
+    for first, last, limit in groups:
+        lax.fori_loop(first, last, functools.partial(query_block, limit), 0)
+
+    def send_out(pair, carry):
+        first = pl.multiple_of(pair * two, two)
+        rows = pl.ds(first, two)
+        dkv = jnp.concatenate([dkt_ref[:, rows], dvt_ref[:, rows]], axis=0).T
+        dq = dq_ref[rows, :]
+        qk = jnp.where(lane < HALF_LANES, dq, swap_halves(dkv)).astype(low)
+        for e in range(2):
+            pack_ref[2 * pair + e, 0:tokens, :] = qk[e * tokens : (e + 1) * tokens]
+            a = dkv[e * tokens : e * tokens + mid]
+            b = dkv[e * tokens + mid : (e + 1) * tokens]
+            pack_ref[2 * pair + e, tokens:, :] = jnp.where(lane_mid < HALF_LANES, swap_halves(a), b).astype(low)
+        return carry
+
+    lax.fori_loop(0, owners // 2, send_out, 0)
+
+
+def attend_back(got, kept, groups):
+    owners, mid, _ = got.shape
+    group_len = owners * mid * 2
+    low = jnp.bfloat16
+    return pl.pallas_call(
+        functools.partial(attend_back_kernel, groups),
+        out_shape=jax.ShapeDtypeStruct((owners, 3 * mid, LANES), low),
+        in_specs=[VM] * 6,
+        out_specs=VM,
+        scratch_shapes=[
+            pltpu.VMEM((group_len, LANES), low),
+            pltpu.VMEM((HALF_LANES, group_len), low),
+            pltpu.VMEM((HALF_LANES, group_len), low),
+            pltpu.VMEM((group_len, LANES), jnp.float32),
+            pltpu.VMEM((HALF_LANES, group_len), jnp.float32),
+            pltpu.VMEM((HALF_LANES, group_len), jnp.float32),
+        ],
+        compiler_params=pltpu.CompilerParams(vmem_limit_bytes=VMEM_BYTES),
+    )(got, *kept)
+
+
+def run_bounds(lengths, group_len):
+    short_sq = jnp.array([side * side for side in SHORT_SIDES], jnp.int32)
+    long_sq = jnp.array([side * side for side in LONG_SIDES], jnp.int32)
+    counts = jnp.where(
+        lengths[None, :] == sum(side * side for side in LONG_SIDES),
+        long_sq[:, None],
+        jnp.where(lengths[None, :] == sum(side * side for side in SHORT_SIDES), short_sq[:, None], 0),
+    ).reshape(-1)
+    ends = jnp.cumsum(counts)
+    starts = ends - counts
+    pad = lambda v, last: jnp.concatenate([v, last])
+    ends = pad(ends, jnp.full((1,), group_len, jnp.int32))
+    starts = pad(starts, ends[-2:-1])
+    return starts, ends
+
+
+def attention_rule(slots):
+    runs = slots * LEVELS + 1
+    rule = np.zeros((LANES, LANES), np.float32)
+    for a in range(runs):
+        for b in range(runs):
+            slot_a, level_a = (slots, 0) if a == runs - 1 else (a % slots, a // slots)
+            slot_b, level_b = (slots, 0) if b == runs - 1 else (b % slots, b // slots)
+            if slot_a != slot_b or level_b > level_a:
+                rule[HALF_LANES + a, HALF_LANES + b] = -BIG
+    return rule
+
+
+def from_heads(blocks):
+    heads, mid, _ = blocks.shape
+    return blocks.reshape(heads, mid, 2, HALF_LANES).transpose(2, 1, 0, 3).reshape(2 * mid, -1)
+
+
+def to_heads(rows):
+    tokens = rows.shape[0]
+    split = rows.reshape(2, tokens // 2, HEADS, HALF_LANES)
+    return split.transpose(2, 1, 0, 3).reshape(HEADS, tokens // 2, LANES)
+
+
+def fast_shards(
+    feature_map,
+    condition,
+    item_lengths,
+    cotangent,
+    code_book,
+    qkv_state,
+    out_state,
+    up_state,
+    down_state,
+    ada_state,
+    embed_state,
+    vector_state,
+):
+    tok_rows, model_width = cotangent.shape
+    low, f32 = jnp.bfloat16, jnp.float32
+    half = model_width // 2
+    core, wide = lax.axis_index("dp"), lax.axis_index("wide")
+    group_len = tok_rows * lax.axis_size("wide")
+    tokens_all = lax.axis_size("dp") * group_len
+    lengths = item_lengths[0]
+    slot_count = lengths.shape[0]
+    swap = [(0, 1), (1, 0)]
+
+    states = (qkv_state, out_state, up_state, down_state, ada_state)
+    flipped = tuple(stacked[1].astype(low).T for stacked in states[:4])
+    w_ada = ada_state[1].astype(low)
+
+    silu_own = jax.nn.silu(condition).astype(low)
+    silu_all = lax.all_gather(silu_own, "dp", axis=0, tiled=True)
+    silu_rows = lax.dynamic_slice_in_dim(silu_all, core * half, half, 1)
+    ada_part = jnp.dot(silu_rows, w_ada, preferred_element_type=f32)
+    ada_theirs = lax.dynamic_slice_in_dim(ada_part, (1 - core) * slot_count, slot_count, 0)
+    ada_mine = lax.dynamic_slice_in_dim(ada_part, core * slot_count, slot_count, 0)
+    ada_mine = ada_mine + lax.ppermute(ada_theirs, "dp", swap)
+    ada_block = jnp.pad(ada_mine, ((0, 8 - slot_count), (0, 0)))
+
+    g_qkv, ada_gathered = gather_weights([flipped[0]], ada_block, 0)
+    g_out, g_up, g_down = gather_weights(list(flipped[1:]), None, 1)
+    ada_product = ada_gathered[:, :slot_count].transpose(1, 0, 2).reshape(slot_count, -1)
+    w_qkv, w_out, w_up, w_down = (g.reshape(2, -1, g.shape[-1]) for g in (g_qkv, g_out, g_up, g_down))
+
+    starts, ends = run_bounds(lengths, group_len)
+    positions = wide * tok_rows + jnp.arange(tok_rows, dtype=jnp.int32)
+    after_start = positions[:, None] >= starts[None, :]
+    before_end = positions[:, None] < ends[None, :]
+    runs_of = (after_start & before_end).astype(f32)
+    live_rows = 1.0 - runs_of[:, -1:]
+    left_ok = 1.0 - jnp.sum(((positions[:, None] == starts[None, :]) & before_end).astype(f32), axis=1)
+    right_ok = 1.0 - jnp.sum(((positions[:, None] == ends[None, :] - 1) & after_start).astype(f32), axis=1)
+    one_hot = jnp.sum(runs_of[:, :-1].reshape(tok_rows, LEVELS, slot_count), axis=1)
+
+    rimmed = padded(feature_map, (("wide", 1),), 1)
+    smooth = smooth_map(feature_map, left_ok, right_ok, rimmed[:, :-2], rimmed[:, 2:])
+    embed_w = embed_state[1]
+    vectors = vector_state[1]
+    gain = vectors[7:8]
+    x_zero = (
+        lax.dot_general(smooth, embed_w, (((0,), (0,)), ((), ())), precision=HIGHEST_PRECISION)
+        + vectors[6]
+    )
+    ada_all = ada_product + vectors[:6].reshape(-1)
+    token_ada = jnp.dot(one_hot, ada_all, precision=HIGHEST_PRECISION)
+    gate_one, gate_two, scale_one, scale_two, shift_one, shift_two = jnp.split(token_ada, 6, axis=1)
+    h_one_low = pre_norm(x_zero, scale_one, shift_one).astype(low)
+
+    pack, kept_qk = project_heads(h_one_low, w_qkv, gain)
+    got = lax.all_to_all(pack, "wide", 0, 0, tiled=True)
+    groups = same_limits(key_limits(group_len, slot_count))
+    lane_pad = lambda v: jnp.pad(v, (HALF_LANES, HALF_LANES - v.shape[0]))[None]
+    rule = jnp.asarray(attention_rule(slot_count), low)
+    att_pack, *kept = attend(got, lane_pad(starts), lane_pad(ends), rule, groups)
+    attn_low = from_heads(lax.all_to_all(att_pack, "wide", 0, 0, tiled=True))
+
+    attn_proj = against(attn_low[:, :half], w_out[0]) + against(attn_low[:, half:], w_out[1])
+    x_one = x_zero + gate_one * attn_proj
+    h_two_low = pre_norm(x_one, scale_two, shift_two).astype(low)
+    hidden_pre = against(h_two_low[:, :half], w_up[0]) + against(h_two_low[:, half:], w_up[1])
+    act_low = jax.nn.gelu(hidden_pre, approximate=True).astype(low)
+    hidden_half = w_down.shape[2]
+    mlp_out = against(act_low[:, :hidden_half], w_down[0]) + against(act_low[:, hidden_half:], w_down[1])
+    x_two = x_one + gate_two * mlp_out
+    block_out = (x_two * live_rows).astype(low)
+    logits = against(block_out, code_book)
+    code_mass = jnp.sum(jax.nn.softmax(logits, axis=-1) * live_rows, axis=0)
+
+    g_two = cotangent.astype(f32) * live_rows
+    d_mlp = (gate_two * g_two).astype(low)
+    d_gate_two = g_two * mlp_out
+
+    def summed_over_cores(grad_rows, inputs):
+        width = inputs.shape[1] // 2
+        other = lax.dynamic_slice_in_dim(inputs, (1 - core) * width, width, 1)
+        own = lax.dynamic_slice_in_dim(inputs, core * width, width, 1)
+        theirs = lax.ppermute(contract_rows(grad_rows, other).astype(low), "dp", swap)
+        total = (contract_rows(grad_rows, own) + theirs.astype(f32)).astype(low)
+        return total.reshape(4, 4, -1, width)
+
+    def both_halves(values, weights):
+        return jnp.concatenate(
+            [jnp.dot(values, weights[h], preferred_element_type=f32) for h in range(2)], axis=1
+        )
+
+    p_down = summed_over_cores(d_mlp, act_low)
+    d_act = both_halves(d_mlp, w_down)
+    _, gelu_back = jax.vjp(lambda inputs: jax.nn.gelu(inputs, approximate=True), hidden_pre)
+    d_hidden = gelu_back(d_act)[0].astype(low)
+    p_up = summed_over_cores(d_hidden, h_two_low)
+    d_h_two = both_halves(d_hidden, w_up)
+    _, norm_back_two = jax.vjp(pre_norm, x_one, scale_two, shift_two)
+    d_x_one, d_scale_two, d_shift_two = norm_back_two(d_h_two)
+    d_x_one = d_x_one + g_two
+    d_attn = (gate_one * d_x_one).astype(low)
+    d_gate_one = d_x_one * attn_proj
+    p_out = summed_over_cores(d_attn, attn_low)
+    d_attended = both_halves(d_attn, w_out).astype(low)
+    s_out, s_up, s_down = scatter_grads([p_out, p_up, p_down], 2)
+
+    back = lax.all_to_all(to_heads(d_attended), "wide", 0, 0, tiled=True)
+    d_pack = attend_back(back, kept, groups)
+    d_got = lax.all_to_all(d_pack, "wide", 0, 0, tiled=True)
+    d_projected_low, d_gain = heads_backward(d_got, kept_qk, gain)
+    p_qkv = summed_over_cores(d_projected_low, h_one_low)
+    (s_qkv,) = scatter_grads([p_qkv], 3)
+    d_h_one = both_halves(d_projected_low, w_qkv)
+    _, norm_back_one = jax.vjp(pre_norm, x_zero, scale_one, shift_one)
+    d_x_zero, d_scale_one, d_shift_one = norm_back_one(d_h_one)
+    d_x_zero = d_x_zero + d_x_one
+    d_token_ada = jnp.concatenate(
+        [d_gate_one, d_gate_two, d_scale_one, d_scale_two, d_shift_one, d_shift_two], axis=1
+    )
+    d_ada_part = contract_rows(one_hot, d_token_ada, HIGHEST_PRECISION)
+    d_smooth = lax.dot_general(embed_w, d_x_zero, (((1,), (1,)), ((), ())), precision=HIGHEST_PRECISION)
+    d_embed = lax.dot_general(smooth, d_x_zero, (((1,), (0,)), ((), ())), precision=HIGHEST_PRECISION)
+    grad_share = d_smooth / (2.0 + left_ok + right_ok)
+    rim_share = padded(grad_share, (("wide", 1),), 1)
+    map_grad = 2.0 * grad_share + left_ok * rim_share[:, :-2] + right_ok * rim_share[:, 2:]
+
+    wides = lax.axis_size("wide")
+    ada_rows = d_ada_part.reshape(slot_count, wides, -1, LANES)
+    per_slot = ada_rows.shape[2]
+    ada_rows = ada_rows.transpose(1, 0, 2, 3).reshape(wides, -1, LANES)
+    code_rows = code_mass.reshape(-1, model_width)
+    common = jnp.concatenate([d_embed, jnp.sum(d_x_zero, axis=0)[None], d_gain, code_rows], axis=0)
+    common_rows = common.shape[0]
+    common = common.reshape(common_rows, wides, -1).transpose(1, 0, 2).reshape(wides, -1, LANES)
+    plain_rows = common.shape[1]
+    small_in = jnp.concatenate([ada_rows, common], axis=1)
+    ada_count = ada_rows.shape[1]
+    d_ada_both, sums = small_sums(small_in, ada_count, slot_count, 4)
+    common_sum = sums[:, :plain_rows].reshape(wides, common_rows, -1).transpose(1, 0, 2)
+    common_sum = common_sum.reshape(common_rows, model_width)
+    embed_rows = embed_w.shape[0]
+    d_embed_all = common_sum[:embed_rows]
+    bias_sum = sums[:, plain_rows:].reshape(6, model_width)
+    d_vectors_all = jnp.concatenate([bias_sum, common_sum[embed_rows : embed_rows + 2]], axis=0)
+    histogram = common_sum[embed_rows + 2 :].reshape(-1) * (code_book.shape[0] / tokens_all)
+    d_ada_own = d_ada_both.reshape(2 * slot_count, per_slot * LANES)
+    grad_ada = contract_rows(silu_rows.astype(f32), d_ada_own, HIGHEST_PRECISION)
+
+    owned_grads = (s_qkv.T, s_out.T, s_up.T, s_down.T, grad_ada)
+    root_tokens = math.sqrt(tokens_all)
+    spreads = (
+        model_width ** (-0.5),
+        (model_width // 16) ** (-0.5),
+        model_width ** (-0.5),
+        w_up.shape[1] ** (-0.5),
+        model_width ** (-0.5),
+    )
+    new_states = tuple(
+        nesterov(stacked, gradient, BASE_RATE * spread_w / (factor_g * root_tokens), WEIGHT_DECAY)
+        for stacked, gradient, spread_w, factor_g in zip(states, owned_grads, spreads, GRAD_FACTORS)
+    )
+    embed_new = nesterov(
+        embed_state, d_embed_all, BASE_RATE * embed_rows ** (-0.5) / (EMBED_FACTOR * root_tokens), 0.0
+    )
+    vector_new = nesterov(vector_state, d_vectors_all, VECTOR_RATE / root_tokens, 0.0)
+    outputs = [block_out, map_grad, histogram]
+    for state in new_states:
+        outputs += [state, state[1].astype(low)]
+    return tuple(outputs + [embed_new, vector_new, d_vectors_all[7]])
+
+
 def solution(mesh):
+    body = fast_shards if dict(mesh.shape) == {"dp": 2, "wide": 16} else shards
     in_specs = (
         P(None, ("dp", "wide")),
         P("dp", None),
@@ -477,4 +1470,4 @@
         P(),
         P(),
     )
-    return jax.shard_map(shards, mesh=mesh, in_specs=in_specs, out_specs=out_specs, check_vma=False)
+    return jax.shard_map(body, mesh=mesh, in_specs=in_specs, out_specs=out_specs, check_vma=False)

time: 2310 us -> 707 us (0.31)
  waiting for transfers between devices: 1560 us -> 14.8 us
  Pallas kernels: 0 us -> 423 us
  local copies, waits for them, and re-layouts: 327 us -> 91.6 us
  matrix products: 195 us -> 80.2 us
  other arithmetic: 121 us -> 43.7 us
  blocking collectives: 43.9 us -> 1.83 us
  starting transfers between devices: 10.6 us -> 39.9 us
  loops' own time: 25.2 us -> 0 us
    reduce_scatter x11 -> x0, waiting for transfers between devices: 774 us -> none  [the longest x1 179 us: shards(): lax.psum_scatter(dw_down.astype(jnp.bfloat16), 'wide', scatter_dimension=...]
    all_gather x12 -> x0, waiting for transfers between devices: 532 us -> none  [the longest x1 98.3 us: shards(): ada_piece = lax.all_gather(masters[4], 'wide', axis=1, tiled=True)]
    pallas_call x0 -> x9, Pallas kernels: none -> 423 us  [the longest x2 162 us: gather_weights(): pl.pallas_call(functools.partial(gather_kernel, count, has_small), out_sh...]
    unnamed x26 -> x0, waiting for transfers between devices: 209 us -> none
    dynamic_slice x33 -> x1, local copies, waits for them, and re-layouts: 126 us -> 0.02 us  [fast_shards(): lax.dynamic_slice_in_dim(ada_part, (1 - core) * slot_count, slot_count, 0)]
    dot_general x36 -> x13, matrix products: 133 us -> 21.4 us  [the longest x8 9.85 us: both_halves(): jnp.dot(values, weights[h], preferred_element_type=f32)]
    dynamic_update_slice x12 -> x0, local copies, waits for them, and re-layouts: 102 us -> none  [the longest x6 51 us: grad_step(): lax.dynamic_update_slice_in_dim(d_values, value_sum, first_key, 0)]
    psum x1 -> x0, waiting for transfers between devices: 45.2 us -> none  [shards(): lax.psum((d_embed, d_vectors, code_mass), ('dp', 'wide'))]
  transfers between devices with their start and end apart: 29 -> 13, of which waited for: 20 -> 3; matrix products, arithmetic and copies ran while one was open for 24% -> 23% of each run, Pallas kernels for 0% -> 41%
where the time goes in v1:
time: 707 us; the launch traced here: 697 us
  Pallas kernels  423 us (60%)
  local copies, waits for them, and re-layouts  91.6 us (13%)
  matrix products  80.2 us (11%)
  other arithmetic  43.7 us (6%)
  starting transfers between devices  39.9 us (6%)
  waiting for transfers between devices  14.8 us (2%)
    pallas_call x2, Pallas kernels, gather_weights(): pl.pallas_call(functools.partial(gather_kernel, count, has_small), out_sh...  162 us
    pallas_call x2, Pallas kernels, scatter_grads(): pl.pallas_call(functools.partial(scatter_kernel, count), out_shape=[jax.S...  155 us
    dot_general x10, matrix products, contract_rows(): lax.dot_general(left_side, right_side, (((0,), (0,)), ((), ())), precisio...  40 us
    pallas_call x1, Pallas kernels, attend_back(): pl.pallas_call(functools.partial(attend_back_kernel, groups), out_shape=j...  33.6 us
    pallas_call x1, Pallas kernels, attend(): pl.pallas_call(functools.partial(attend_kernel, groups), out_shape=[jax.S...  31.2 us
    pallas_call x1, Pallas kernels, small_sums(): pl.pallas_call(functools.partial(small_kernel, ada_rows, slots), out_shap...  23.5 us
    dot_general x7, matrix products, against(): lax.dot_general(left_side, right_side, (((1,), (1,)), ((), ())), preferre...  18.8 us
    unnamed x161, local copies, waits for them, and re-layouts  15.3 us
  transfers between devices with their start and end apart: 13, of which 3 were waited for; matrix products, arithmetic and copies ran while one was open for 23% of the time, Pallas kernels for 41%

profile of v1, /device:TPU:0, one launch (start us, length us, event | category | flops | bytes accessed | tf_op | source)
XLA Modules:
  0.0 696.7 jit_solution(12476093873041435288)
XLA Ops:
  1.5 4.8 collective-permute-start
  24.8 47.2 %shard_map.270 = (bf16[2,4,4,192,512]{4,3,2,1,0:T(8,128)(2,1)}, f32[16,8,384]{2,1,0:T(8,128)}) custom-call(bf16[192,512]{1,0:T(8,128)(2,1)} %fusion.49.refs_0_, f32[8,384]{1,0:T(8,128)} %pad.11.refs_1_), custom_call_target="tpu_custom_call" | custom-call | tf_op jit(solution)/shard_map/pallas_call | solution.py:621
  72.0 4.9 fusion.63
  80.2 8.5 %shard_map.271 = (bf16[16,288,128]{2,1,0:T(8,128)(2,1)}, f32[192,2048]{1,0:T(8,128)}) custom-call(bf16[192,1024]{1,0:T(8,128)(2,1)} %fusion.19.h_ref, bf16[2,3072,512]{2,1,0:T(8,128)(2,1)} %bitcast.303, f32[1,1024]{1,0:T(1,128)} %get-tuple-element.186.gain_ref), custom_call_target="tpu_custom_call" | custom-call | tf_op jit(solution)/shard_map/pallas_call | solution.py:879
  88.7 7.2 %all-to-all-start = ((bf16[16,288,128]{2,1,0:T(8,128)(2,1)}), bf16[16,288,128]{2,1,0:T(8,128)(2,1)}, u32[]{:S(2)}, u32[]{:S(2)}) async-start(bf16[16,288,128]{2,1,0:T(8,128)(2,1)} %get-tuple-element.38), calls=%async_computation | async-start | bytes 2359296 | tf_op jit(solution)/shard_map/all_to_all | solution.py:1323
  100.0 115.1 %shard_map.273 = (bf16[2,4,4,64,512]{4,3,2,1,0:T(8,128)(2,1)}, bf16[2,4,4,256,512]{4,3,2,1,0:T(8,128)(2,1)}, bf16[2,4,4,64,2048]{4,3,2,1,0:T(8,128)(2,1)}) custom-call(bf16[64,512]{1,0:T(8,128)(2,1)} %fusion.73.refs_0_, bf16[256,512]{1,0:T(8,128)(2,1)} %fusion.39.refs_1_, bf16[64,2048]{1,0:T(8,128)(2,1)} %fusion.40.refs_2_), custom_call_target="tpu_custom_call" | custom-call | tf_op jit(solution)/shard_map/pallas_call | solution.py:621
  219.0 6.3 fusion.114
  225.2 31.2 %shard_map.272 = (bf16[16,96,128]{2,1,0:T(8,128)(2,1)}, f32[3072,128]{1,0:T(8,128)}, bf16[3072,128]{1,0:T(8,128)(2,1)}, bf16[3072,128]{1,0:T(8,128)(2,1)}, bf16[...) custom-call(bf16[16,288,128]{2,1,0:T(8,128)(2,1)} %all-to-all-done.got_ref, s32[1,128]{1,0:T(1,128)} %pad_bitcast_fusion.1.starts_ref, ...), custom_call_target="tpu_custom_call" | custom-call | tf_op jit(solution)/shard_map/pallas_call | solution.py:1104
  256.4 8.8 %all-to-all-start.1 = ((bf16[16,96,128]{2,1,0:T(8,128)(2,1)}), bf16[16,96,128]{2,1,0:T(8,128)(2,1)S(1)}, u32[]{:S(2)}, u32[]{:S(2)}) async-start(bf16[16,96,128]{2,1,0:T(8,128)(2,1)} %get-tuple-element.39), calls=%async_computation.1 | async-start | bytes 786432 | tf_op jit(solution)/shard_map/all_to_all | solution.py:1328
  265.2 6.1 fusion.113
  271.3 7.1 %all-to-all-done.1 = bf16[16,96,128]{2,1,0:T(8,128)(2,1)S(1)} async-done(((bf16[16,96,128]{2,1,0:T(8,128)(2,1)}), bf16[16,96,128]{2,1,0:T(8,128)(2,1)S(1)}, u32[]{:S(2)}, u32[]{:S(2)}) %all-to-all-start.1) | async-done | bytes 393248 | tf_op jit(solution)/shard_map/all_to_all | solution.py:1328
  291.5 3.8 fusion.8
  313.5 4.2 all-to-all-start.2
  321.8 6.2 fusion.115
  329.5 33.6 %shard_map.274 = bf16[16,288,128]{2,1,0:T(8,128)(2,1)} custom-call(bf16[16,96,128]{2,1,0:T(8,128)(2,1)} %all-to-all-done.2.got_ref, f32[3072,128]{1,0:T(8,128)} %get-tuple-element.43.out32_ref, bf16[3072,128]{1,0:T(8,128)(2,1)} %get-tuple-element.44.q_ref, bf16[3072,128]{1,0:T(8,128)(2,1)} %get-tuple-element.45.k_ref, ...), custom_call_target="tpu_custom_call" | custom-call | tf_op jit(solution)/shard_map/pallas_call | solution.py:1200
  363.1 7.3 %all-to-all-start.3 = ((bf16[16,288,128]{2,1,0:T(8,128)(2,1)}), bf16[16,288,128]{2,1,0:T(8,128)(2,1)}, u32[]{:S(2)}, u32[]{:S(2)}) async-start(bf16[16,288,128]{2,1,0:T(8,128)(2,1)} %shard_map.274), calls=%async_computation.3 | async-start | bytes 2359296 | tf_op jit(solution)/shard_map/all_to_all | solution.py:1376
  370.4 6.5 fusion.121
  381.7 4.5 convolution_convert_fusion.2
  386.5 3.2 convolution_convert_fusion
  393.8 3.9 all-to-all-done.3.got_ref
  397.7 8.7 %shard_map.275 = (bf16[192,3072]{1,0:T(8,128)(2,1)}, f32[1,1024]{1,0:T(1,128)}) custom-call(bf16[16,288,128]{2,1,0:T(8,128)(2,1)} %all-to-all-done.3.got_ref, f32[192,2048]{1,0:T(8,128)} %get-tuple-element.48.kept_ref, f32[1,1024]{1,0:T(1,128)} %get-tuple-element.186.gain_ref), custom_call_target="tpu_custom_call" | custom-call | tf_op jit(solution)/shard_map/pallas_call | solution.py:928
  411.9 3.2 fusion.110
  419.4 8.5 %dot_general.113 = f32[16,3,128,192]{2,1,0,3:T(4,128)} reshape(f32[6144,192]{0,1:T(8,128)} %bitcast.37) | data formatting | bytes 9437184 | tf_op jit(solution)/shard_map/dot_general | solution.py:103
  428.0 8.0 %fusion.11 = f32[16,6,3,128]{3,1,2,0:T(8,128)S(1)} fusion(f32[16,3,128,192]{2,1,0,3:T(4,128)} %dot_general.113, f32[192,6]{0,1:T(8,128)S(1)} %reduce_sum.126), kind=kOutput, calls=%fused_computation.38 | convolution fusion | flops 84934656 | bytes 4870656 | tf_op jit(solution)/shard_map/dot_general | solution.py:103
  451.2 23.5 %shard_map.276 = (f32[2,18,128]{2,1,0:T(8,128)}, f32[16,22,128]{2,1,0:T(8,128)}) custom-call(f32[16,37,128]{2,1,0:T(8,128)} %pad_maximum_fusion.10.part_ref), custom_call_target="tpu_custom_call" | custom-call | tf_op jit(solution)/shard_map/pallas_call | solution.py:796
  494.0 3.9 collective-permute-start.3
  506.8 3.8 collective-permute-done.4
  512.1 5.8 add_convert_fusion
  517.9 5.5 add_convert_fusion.1
  523.4 107.6 %shard_map.278 = (f32[64,512]{1,0:T(8,128)}, f32[256,512]{1,0:T(8,128)}, f32[64,2048]{1,0:T(8,128)}) custom-call(bf16[4,4,64,512]{3,2,1,0:T(8,128)(2,1)} %bitcast.316, bf16[4,4,256,512]{3,2,1,0:T(8,128)(2,1)} %bitcast.301, bf16[4,4,64,2048]{3,2,1,0:T(8,128)(2,1)} %bitcast.302), custom_call_target="tpu_custom_call" | custom-call | tf_op jit(solution)/shard_map/pallas_call | solution.py:716
  641.7 4.6 add_convert_fusion.2
  646.3 47.2 %shard_map.277 = f32[192,512]{1,0:T(8,128)} custom-call(bf16[4,4,192,512]{3,2,1,0:T(8,128)(2,1)} %bitcast.308), custom_call_target="tpu_custom_call" | custom-call | tf_op jit(solution)/shard_map/pallas_call | solution.py:716
  (309 shorter events, 144.1 us)
Async XLA Ops:
  1.5 20.3 %collective-permute-start = (f32[32,1]{1,0:T(8,128)S(1)}, f32[32,1]{1,0:T(8,128)S(1)}, u32[]{:S(2)}, u32[]{:S(2)}) collective-permute-start(f32[32,1]{1,0:T(8,128)S(1)} %get-tuple-element.190), channel_id=1, source_target_pairs={{0,1},{1,2},{2,3},{3,4},{4,5},{5,6},{6,7},{7,8},{8,9},{9,10},{10,1... | collective-permute-start | bytes 392 | tf_op jit(solution)/shard_map/ppermute | solution.py:38
  6.3 15.5 %collective-permute-start.1 = (f32[32,1]{1,0:T(8,128)S(1)}, f32[32,1]{1,0:T(8,128)S(1)}, u32[]{:S(2)}, u32[]{:S(2)}) collective-permute-start(f32[32,1]{1,0:T(8,128)S(1)} %get-tuple-element.191), channel_id=1, source_target_pairs={{1,0},{2,1},{3,2},{4,3},{5,4},{6,5},{7,6},{8,7},{9,8},{10,9},{11,1... | collective-permute-start | bytes 392 | tf_op jit(solution)/shard_map/ppermute | solution.py:40
  7.6 14.2 %copy-start.42 = (f32[32,192]{1,0:T(8,128)S(1)}, f32[32,192]{1,0:T(8,128)}, u32[]{:S(2)}) copy-start(f32[32,192]{1,0:T(8,128)} %param.15) | copy-start | bytes 73732
  10.2 11.3 %copy-start.45 = (bf16[12,1024]{1,0:T(8,128)(2,1)}, bf16[12,1024]{1,0:T(8,128)(2,1)S(1)}, u32[]{:S(2)}) copy-start(bf16[12,1024]{1,0:T(8,128)(2,1)S(1)} %reshape.319) | copy-start | bytes 73732
  11.6 12.6 %collective-permute-start.2 = (f32[6,384]{1,0:T(8,128)S(1)}, f32[6,384]{1,0:T(8,128)S(1)}, u32[]{:S(2)}, u32[]{:S(2)}) collective-permute-start(f32[6,384]{1,0:T(8,128)S(1)} %constant_dynamic-slice_fusion), channel_id=1, source_target_pairs={{0,16},{16,0},{1,17},{17,1},{2,18},{18,2},{3,19},{19,3},{4,20},{20... | collective-permute-start | bytes 27656 | tf_op jit(solution)/shard_map/ppermute | solution.py:1290
  21.7 75.7 %copy-start.28 = (f32[1,512,256]{1,2,0:T(8,128)}, f32[1,512,256]{1,2,0:T(8,128)S(1)}, u32[]{:S(2)}) copy-start(f32[1,512,256]{1,2,0:T(8,128)S(1)} %copy.121) | copy-start | bytes 1572868
  21.8 55.1 %copy-start.48 = (f32[32,1]{1,0:T(8,128)}, f32[32,1]{1,0:T(8,128)S(1)}, u32[]{:S(2)}) copy-start(f32[32,1]{1,0:T(8,128)S(1)} %collective-permute-done) | copy-start | bytes 388
  21.8 55.1 %copy-start.50 = (f32[32,1]{1,0:T(8,128)}, f32[32,1]{1,0:T(8,128)S(1)}, u32[]{:S(2)}) copy-start(f32[32,1]{1,0:T(8,128)S(1)} %collective-permute-done.1) | copy-start | bytes 388
  23.9 56.3 %copy-start.54 = (f32[192]{0:T(256)}, f32[192]{0:T(256)S(1)}, u32[]{:S(2)}) copy-start(f32[192]{0:T(256)S(1)} %broadcast_multiply_fusion.1) | copy-start | bytes 2308
  24.1 56.1 %copy-start.71 = (f32[192]{0:T(256)}, f32[192]{0:T(256)S(1)}, u32[]{:S(2)}) copy-start(f32[192]{0:T(256)S(1)} %multiply_reduce_fusion.4) | copy-start | bytes 2308
  24.1 56.0 %copy-start.67 = (f32[192]{0:T(256)}, f32[192]{0:T(256)S(1)}, u32[]{:S(2)}) copy-start(f32[192]{0:T(256)S(1)} %fusion.99) | copy-start | bytes 2308
  88.7 136.6 %all-to-all-start = ((bf16[16,288,128]{2,1,0:T(8,128)(2,1)}), bf16[16,288,128]{2,1,0:T(8,128)(2,1)}, u32[]{:S(2)}, u32[]{:S(2)}) async-start(bf16[16,288,128]{2,1,0:T(8,128)(2,1)} %get-tuple-element.38), calls=%async_computation | async-start | bytes 2359296 | tf_op jit(solution)/shard_map/all_to_all | solution.py:1323
  219.0 60.6 %copy-start.15 = (bf16[1,4,4,64,512]{4,3,2,1,0:T(8,128)(2,1)}, bf16[1,4,4,64,512]{4,3,2,1,0:T(8,128)(2,1)S(1)}, u32[]{:S(2)}) copy-start(bf16[1,4,4,64,512]{4,3,2,1,0:T(8,128)(2,1)S(1)} %get-tuple-element.176) | copy-start | bytes 3145732
  256.4 22.0 %all-to-all-start.1 = ((bf16[16,96,128]{2,1,0:T(8,128)(2,1)}), bf16[16,96,128]{2,1,0:T(8,128)(2,1)S(1)}, u32[]{:S(2)}, u32[]{:S(2)}) async-start(bf16[16,96,128]{2,1,0:T(8,128)(2,1)} %get-tuple-element.39), calls=%async_computation.1 | async-start | bytes 786432 | tf_op jit(solution)/shard_map/all_to_all | solution.py:1328
  282.5 16.7 %copy-start.56 = (f32[192]{0:T(256)}, f32[192]{0:T(256)S(1)}, u32[]{:S(2)}) copy-start(f32[192]{0:T(256)S(1)} %fusion.100) | copy-start | bytes 2308
  313.5 16.0 %all-to-all-start.2 = ((bf16[16,96,128]{2,1,0:T(8,128)(2,1)}), bf16[16,96,128]{2,1,0:T(8,128)(2,1)}, u32[]{:S(2)}, u32[]{:S(2)}) async-start(bf16[16,96,128]{2,1,0:T(8,128)(2,1)} %copy.108), calls=%async_computation.2 | async-start | bytes 786432 | tf_op jit(solution)/shard_map/all_to_all | solution.py:1374
  329.5 61.6 %collective-permute-start.6 = (bf16[1024,512]{1,0:T(8,128)(2,1)}, bf16[1024,512]{1,0:T(8,128)(2,1)}, u32[]{:S(2)}, u32[]{:S(2)}) collective-permute-start(bf16[1024,512]{1,0:T(8,128)(2,1)} %convolution_convert_fusion.3), channel_id=1, source_target_pairs={{0,16},{16,0},{1,17},{17,1},{2,18},{18,2},{3,19},{19,3},{4,20},{20... | collective-permute-start | bytes 3145736 | tf_op jit(solution)/shard_map/ppermute | solution.py:1350
  363.1 34.7 %all-to-all-start.3 = ((bf16[16,288,128]{2,1,0:T(8,128)(2,1)}), bf16[16,288,128]{2,1,0:T(8,128)(2,1)}, u32[]{:S(2)}, u32[]{:S(2)}) async-start(bf16[16,288,128]{2,1,0:T(8,128)(2,1)} %shard_map.274), calls=%async_computation.3 | async-start | bytes 2359296 | tf_op jit(solution)/shard_map/all_to_all | solution.py:1376
  386.2 126.0 %collective-permute-start.8 = (bf16[1024,2048]{1,0:T(8,128)(2,1)}, bf16[1024,2048]{1,0:T(8,128)(2,1)}, u32[]{:S(2)}, u32[]{:S(2)}) collective-permute-start(bf16[1024,2048]{1,0:T(8,128)(2,1)} %convolution_convert_fusion.2), channel_id=1, source_target_pairs={{0,16},{16,0},{1,17},{17,1},{2,18},{18,2},{3,19},{19,3},{4,20},{20... | collective-permute-start | bytes 12582920 | tf_op jit(solution)/shard_map/ppermute | solution.py:1350
  389.7 128.2 %collective-permute-start.7 = (bf16[4096,512]{1,0:T(8,128)(2,1)}, bf16[4096,512]{1,0:T(8,128)(2,1)}, u32[]{:S(2)}, u32[]{:S(2)}) collective-permute-start(bf16[4096,512]{1,0:T(8,128)(2,1)} %convolution_convert_fusion), channel_id=1, source_target_pairs={{0,16},{16,0},{1,17},{17,1},{2,18},{18,2},{3,19},{19,3},{4,20},{20... | collective-permute-start | bytes 12582920 | tf_op jit(solution)/shard_map/ppermute | solution.py:1350
  397.7 11.8 %copy-start.7 = (bf16[1,4,4,192,512]{4,3,2,1,0:T(8,128)(2,1)S(1)}, bf16[1,4,4,192,512]{4,3,2,1,0:T(8,128)(2,1)}, u32[]{:S(2)}) copy-start(bf16[1,4,4,192,512]{4,3,2,1,0:T(8,128)(2,1)} %get-tuple-element.167) | copy-start | bytes 9437188
  438.0 47.6 %copy-start.5 = (bf16[192,3072]{1,0:T(8,128)(2,1)S(1)}, bf16[192,3072]{1,0:T(8,128)(2,1)}, u32[]{:S(2)}) copy-start(bf16[192,3072]{1,0:T(8,128)(2,1)} %get-tuple-element.49) | copy-start | bytes 3538948
  438.0 47.6 %copy-start.30 = (bf16[192,1024]{1,0:T(8,128)(2,1)S(1)}, bf16[192,1024]{1,0:T(8,128)(2,1)}, u32[]{:S(2)}) copy-start(bf16[192,1024]{1,0:T(8,128)(2,1)} %fusion.19.h_ref) | copy-start | bytes 1179652
  485.6 12.4 %copy-start.53 = (f32[1,2,1024]{2,1,0:T(2,128)S(1)}, f32[1,2,1024]{2,1,0:T(2,128)}, u32[]{:S(2)}) copy-start(f32[1,2,1024]{2,1,0:T(2,128)} %concatenate.84) | copy-start | bytes 24580
  488.4 153.3 %collective-permute-start.5 = (bf16[3072,512]{1,0:T(8,128)(2,1)}, bf16[3072,512]{1,0:T(8,128)(2,1)}, u32[]{:S(2)}, u32[]{:S(2)}) collective-permute-start(bf16[3072,512]{1,0:T(8,128)(2,1)} %convolution_convert_fusion.1), channel_id=1, source_target_pairs={{0,16},{16,0},{1,17},{17,1},{2,18},{18,2},{3,19},{19,3},{4,20},{20... | collective-permute-start | bytes 9437192 | tf_op jit(solution)/shard_map/ppermute | solution.py:1350
  491.2 10.2 %copy-start.46 = (bf16[12,1024]{1,0:T(8,128)(2,1)S(1)}, bf16[12,1024]{1,0:T(8,128)(2,1)}, u32[]{:S(2)}) copy-start(bf16[12,1024]{1,0:T(8,128)(2,1)} %copy-done.45) | copy-start | bytes 73732
  491.2 10.2 %copy-start.47 = (f32[12,384]{1,0:T(8,128)S(1)}, f32[12,384]{1,0:T(8,128)}, u32[]{:S(2)}) copy-start(f32[12,384]{1,0:T(8,128)} %reshape.317) | copy-start | bytes 55300
  494.0 12.8 %collective-permute-start.3 = (f32[32,1]{1,0:T(8,128)}, f32[32,1]{1,0:T(8,128)}, u32[]{:S(2)}, u32[]{:S(2)}) collective-permute-start(f32[32,1]{1,0:T(8,128)} %get-tuple-element.188), channel_id=1, source_target_pairs={{0,1},{1,2},{2,3},{3,4},{4,5},{5,6},{6,7},{7,8},{8,9},{9,10},{10,1... | collective-permute-start | bytes 392 | tf_op jit(solution)/shard_map/ppermute | solution.py:38
  504.6 5.9 collective-permute-start.4
  523.4 107.6 %copy-start.29 = (f32[1,512,256]{1,2,0:T(8,128)S(1)}, f32[1,512,256]{1,2,0:T(8,128)}, u32[]{:S(2)}) copy-start(f32[1,512,256]{1,2,0:T(8,128)} %copy-done.28) | copy-start | bytes 1572868
  523.4 107.6 %copy-start.39 = (f32[1,512,256]{1,2,0:T(8,128)S(1)}, f32[1,512,256]{1,2,0:T(8,128)}, u32[]{:S(2)}) copy-start(f32[1,512,256]{1,2,0:T(8,128)} %copy.122) | copy-start | bytes 1572868
  646.3 47.2 %copy-start.40 = (f32[3,512,192]{1,2,0:T(8,128)S(1)}, f32[3,512,192]{1,2,0:T(8,128)}, u32[]{:S(2)}) copy-start(f32[3,512,192]{1,2,0:T(8,128)} %param.20) | copy-start | bytes 3538948
  (57 other events, 270.9 us)

commit v2 on v1

--- a/solution.py
+++ b/solution.py
@@ -483,151 +483,6 @@
 
 def at_dev(core, z, yx):
     return (core, z * 4 + yx)
-
-
-def gather_kernel(count, has_small, *refs):
-    shards = refs[:count]
-    small = refs[count] if has_small else None
-    base = count + has_small
-    fulls = refs[base : base + count]
-    small_out = refs[base + count] if has_small else None
-    sems = refs[base + count + has_small :]
-    send_x, send_y, send_z, send_s, recv_i, recv_s, local = sems[:7]
-    core, z, yx = place()
-    x_dev, y_dev = at_dev(core, z, yx ^ 1), at_dev(core, z, yx ^ 2)
-    sib = at_dev(1 - core, z, yx)
-    z_devs = [None] + [at_dev(core, lax.rem(z + r, 4), yx) for r in (1, 2, 3)]
-    wide = z * 4 + yx
-    if has_small:
-        everyone = [(core, wide ^ r) for r in range(1, 16)]
-        entry_barrier(everyone + [sib])
-    else:
-        entry_barrier([x_dev, y_dev, sib] + z_devs[1:])
-    pending = []
-
-    def spot(full, dz, d):
-        return full.at[core, lax.rem(z + dz, 4), yx ^ d]
-
-    def push(i, dz, d, src, sem, device, there):
-        copy = pltpu.make_async_remote_copy(
-            src_ref=src,
-            dst_ref=spot(fulls[i], dz, d),
-            send_sem=sem,
-            recv_sem=there,
-            device_id=device,
-            device_id_type=MESH_ID,
-        )
-        copy.start()
-        pending.append(copy)
-
-    def to_x(i, dz, d, src):
-        push(i, dz, d, src, send_x.at[i, dz, d], x_dev, recv_i.at[i, dz, d ^ 1])
-
-    def to_y(i, dz, d, src):
-        push(i, dz, d, src, send_y.at[i, dz, d], y_dev, recv_i.at[i, dz, d ^ 2])
-
-    def to_s(i, dz, d, src):
-        push(i, dz, d, src, send_s.at[i, dz, d], sib, recv_s.at[i, dz, d])
-
-    def arrive(ref, sem):
-        pltpu.make_async_copy(ref, ref, sem).wait()
-
-    def got(i, dz, d):
-        ref = spot(fulls[i], dz, d)
-        arrive(ref, recv_i.at[i, dz, d])
-        return ref
-
-    small_copies = []
-    if has_small:
-        small_send, small_recv, small_local = sems[7:]
-        own = pltpu.make_async_copy(small, small_out.at[wide], small_local)
-        own.start()
-        small_copies.append(own)
-        for r in range(1, 16):
-            copy = pltpu.make_async_remote_copy(
-                src_ref=small,
-                dst_ref=small_out.at[wide],
-                send_sem=small_send.at[r],
-                recv_sem=small_recv.at[r],
-                device_id=(core, wide ^ r),
-                device_id_type=MESH_ID,
-            )
-            copy.start()
-            small_copies.append(copy)
-    locals_ = []
-    for i in range(count):
-        src = shards[i]
-        for r in (1, 3, 2):
-            push(i, 0, 0, src, send_z.at[i, r], z_devs[r], recv_i.at[i, (4 - r) % 4, 0])
-        to_x(i, 0, 0, src)
-        to_y(i, 0, 0, src)
-        to_s(i, 0, 0, src)
-        copy = pltpu.make_async_copy(src, spot(fulls[i], 0, 0), local.at[i])
-        copy.start()
-        locals_.append(copy)
-    for i in range(count):
-        ref = got(i, 0, 1)
-        to_y(i, 0, 1, ref)
-        to_s(i, 0, 1, ref)
-        ref = got(i, 0, 2)
-        to_s(i, 0, 2, ref)
-    for i in range(count):
-        for dz in (1, 3, 2):
-            ref = got(i, dz, 0)
-            to_x(i, dz, 0, ref)
-            to_y(i, dz, 0, ref)
-            to_s(i, dz, 0, ref)
-        for dz in (1, 3, 2):
-            ref = got(i, dz, 1)
-            if dz == 1:
-                to_y(i, dz, 1, ref)
-            to_s(i, dz, 1, ref)
-            ref = got(i, dz, 2)
-            if dz != 1:
-                to_x(i, dz, 2, ref)
-            to_s(i, dz, 2, ref)
-    for i in range(count):
-        for dz in (0, 1, 3, 2):
-            to_s(i, dz, 3, got(i, dz, 3))
-    for i in range(count):
-        for dz in range(4):
-            for d in range(4):
-                ref = fulls[i].at[1 - core, lax.rem(z + dz, 4), yx ^ d]
-                arrive(ref, recv_s.at[i, dz, d])
-    for copy in pending:
-        copy.wait_send()
-    for copy in locals_ + small_copies:
-        copy.wait()
-
-
-def gather_weights(shards, small, call_id):
-    count, has_small = len(shards), int(small is not None)
-    dma = pltpu.SemaphoreType.DMA
-    scratch = [
-        dma((count, 4, 4)),
-        dma((count, 4, 4)),
-        dma((count, 4)),
-        dma((count, 4, 4)),
-        dma((count, 4, 4)),
-        dma((count, 4, 4)),
-        dma((count,)),
-    ]
-    outs = [jax.ShapeDtypeStruct((2, 4, 4) + s.shape, s.dtype) for s in shards]
-    args = list(shards)
-    if has_small:
-        scratch += [dma((16,)), dma((16,)), dma]
-        outs.append(jax.ShapeDtypeStruct((16,) + small.shape, small.dtype))
-        args.append(small)
-    return pl.pallas_call(
-        functools.partial(gather_kernel, count, has_small),
-        out_shape=outs,
-        in_specs=[ANY] * len(args),
-        out_specs=[ANY] * len(outs),
-        scratch_shapes=scratch,
-        compiler_params=pltpu.CompilerParams(
-            collective_id=call_id, has_side_effects=True, vmem_limit_bytes=VMEM_BYTES
-        ),
-    )(*args)
 
 
 def scatter_kernel(count, *refs):
@@ -839,55 +694,6 @@
     )
 
 
-def qkv_kernel(h_ref, w_ref, gain_ref, pack_ref, kept_ref):
-    tokens, width = h_ref.shape
-    half = width // 2
-    mid = tokens // 2
-    group = 256
-    low = jnp.bfloat16
-    lane = lane_iota((tokens, LANES))
-    lane_mid = lane_iota((mid, LANES))
-
-    def project(first):
-        rows = pl.ds(first, group)
-        return nt(h_ref[:, :half], w_ref[0, rows, :]) + nt(h_ref[:, half:], w_ref[1, rows, :])
-
-    def step(g, carry):
-        first = pl.multiple_of(g * group, group)
-        q_all, k_all, v_all = (project(first + part * width) for part in range(3))
-        kept_ref[:, pl.ds(first, group)] = q_all
-        kept_ref[:, pl.ds(first + width, group)] = k_all
-        q_all = q_all * lax.rsqrt(head_sums(q_all * q_all) + NORM_EPS)
-        q_all = q_all * (8.0 * (1.0 + gain_ref[:, pl.ds(first, group)]))
-        k_all = k_all * lax.rsqrt(head_sums(k_all * k_all) + NORM_EPS)
-        for pair in range(group // LANES):
-            cols = slice(pair * LANES, (pair + 1) * LANES)
-            q, k, v = q_all[:, cols], k_all[:, cols], v_all[:, cols]
-            head = g * (group // HALF_LANES) + 2 * pair
-            pack_ref[head, 0:tokens, :] = jnp.where(lane < HALF_LANES, q, swap_halves(k)).astype(low)
-            pack_ref[head + 1, 0:tokens, :] = jnp.where(lane < HALF_LANES, swap_halves(q), k).astype(low)
-            v_a, v_b = v[:mid], v[mid:]
-            pack_ref[head, tokens:, :] = jnp.where(lane_mid < HALF_LANES, v_a, swap_halves(v_b)).astype(low)
-            pack_ref[head + 1, tokens:, :] = jnp.where(lane_mid < HALF_LANES, swap_halves(v_a), v_b).astype(low)
-        return carry
-
-    lax.fori_loop(0, width // group, step, 0)
-
-
-def project_heads(h_low, w_all, gain):
-    tokens, width = h_low.shape
-    return pl.pallas_call(
-        qkv_kernel,
-        out_shape=[
-            jax.ShapeDtypeStruct((HEADS, tokens + tokens // 2, LANES), jnp.bfloat16),
-            jax.ShapeDtypeStruct((tokens, 2 * width), jnp.float32),
-        ],
-        in_specs=[VM] * 3,
-        out_specs=[VM] * 2,
-        compiler_params=pltpu.CompilerParams(vmem_limit_bytes=VMEM_BYTES),
-    )(h_low, w_all, gain)
-
-
 def heads_back_kernel(got_ref, kept_ref, gain_ref, out_ref, gain_grad_ref):
     tokens = kept_ref.shape[0]
     width = kept_ref.shape[1] // 2
@@ -972,18 +778,6 @@
     return groups
 
 
-def chunks_of(limit, step):
-    whole = limit // CHUNK
-
-    def body(c, carry):
-        step(pl.multiple_of(c * CHUNK, CHUNK), CHUNK)
-        return carry
-
-    lax.fori_loop(0, whole, body, 0)
-    if limit % CHUNK:
-        step(whole * CHUNK, limit % CHUNK)
-
-
 def fold_lanes(values, combine):
     total = values[:, :LANES]
     for j in range(1, values.shape[1] // LANES):
@@ -1003,122 +797,6 @@
     return jnp.where(
         lane == first, high, jnp.where(lane == first + 1, mid, jnp.where(lane == first + 2, rest, otherwise))
     )
-
-
-def attend_kernel(
-    groups, got_ref, starts_ref, ends_ref, rule_ref, out_ref, out32_ref, q_ref, k_ref, kt_ref, vt_ref, v_ref, s_ref
-):
-    owners = got_ref.shape[0]
-    tokens = got_ref.shape[1] * 2 // 3
-    mid = tokens // 2
-    f32, low = jnp.float32, jnp.bfloat16
-    two = 2 * tokens
-    lane = lane_iota((two, LANES))
-    lane_mid = lane_iota((mid, LANES))
-
-    def unpack(pair, carry):
-        first = pl.multiple_of(pair * two, two)
-        qk = jnp.concatenate([got_ref[2 * pair + e, 0:tokens, :].astype(f32) for e in range(2)], axis=0)
-        spot = first + lax.broadcasted_iota(jnp.int32, (two, LANES), 0)
-        runs = ((spot >= starts_ref[...]) & (spot < ends_ref[...])).astype(f32)
-        barred = nn(runs.astype(low), rule_ref[...])
-        rows = pl.ds(first, two)
-        q_ref[rows, :] = jnp.where(lane < HALF_LANES, qk, barred).astype(low)
-        tail = jnp.where(lane >= LANES - 3, 1.0, runs)
-        keys = jnp.where(lane < HALF_LANES, swap_halves(qk), tail)
-        k_ref[rows, :] = keys.astype(low)
-        kt_ref[:, rows] = keys.T.astype(low)
-        ones = ((lane_mid >= HALF_LANES) & (lane_mid < HALF_LANES + 3)).astype(f32)
-        pieces = []
-        for e in range(2):
-            v = got_ref[2 * pair + e, tokens:, :].astype(f32)
-            pieces.append(jnp.where(lane_mid < HALF_LANES, v, ones))
-            pieces.append(jnp.where(lane_mid < HALF_LANES, swap_halves(v), ones))
-        values = jnp.concatenate(pieces, axis=0)
-        v_ref[rows, :] = values.astype(low)
-        vt_ref[:, rows] = values.T.astype(low)
-        return carry
-
-    lax.fori_loop(0, owners // 2, unpack, 0)
-    lane_q = lane_iota((ROWS, LANES))
-
-    def query_block(limit, b, carry):
-        rows = pl.ds(pl.multiple_of(b * ROWS, ROWS), ROWS)
-        q = q_ref[rows, :]
-
-        def score(c, top):
-            cols = pl.ds(pl.multiple_of(c * CHUNK, CHUNK), CHUNK)
-            s = nn(q, kt_ref[:, cols])
-            s_ref[:, cols] = s
-            return jnp.maximum(top, fold_lanes(s, jnp.maximum))
-
-        whole, left = limit // CHUNK, limit % CHUNK
-        top = lax.fori_loop(0, whole, score, jnp.full((ROWS, LANES), -3e38, f32))
-        if left:
-            tail = slice(whole * CHUNK, limit)
-            s = nn(q, kt_ref[:, tail])
-            s_ref[:, tail] = s
-            top = jnp.maximum(top, fold_lanes(s, jnp.maximum))
-        peak = jnp.max(top, axis=1, keepdims=True)
-
-        def weigh(cols, carry):
-            total, acc = carry
-            p = jnp.exp(s_ref[:, cols] - peak)
-            return total + fold_lanes(p, jnp.add), acc + nn(p.astype(low), v_ref[cols, :])
-
-        zero = jnp.zeros((ROWS, LANES), f32)
-        total, acc = lax.fori_loop(
-            0,
-            whole,
-            lambda c, carry: weigh(pl.ds(pl.multiple_of(c * CHUNK, CHUNK), CHUNK), carry),
-            (zero, zero),
-        )
-        if left:
-            total, acc = weigh(slice(whole * CHUNK, limit), (total, acc))
-        total = jnp.sum(total, axis=1, keepdims=True)
-        out32_ref[rows, :] = acc / total
-        log_total = peak + jnp.log(total)
-        q_ref[rows, :] = lanes_three(lane_q, LANES - 3, -log_total, q.astype(f32)).astype(low)
-        return carry
-
-    for first, last, limit in groups:
-        lax.fori_loop(first, last, functools.partial(query_block, limit), 0)
-
-    def send_out(w, carry):
-        rows = pl.multiple_of(w * tokens, tokens)
-        a = out32_ref[pl.ds(rows, mid), :]
-        b = out32_ref[pl.ds(rows + mid, mid), :]
-        out_ref[w] = jnp.where(lane_mid < HALF_LANES, a, swap_halves(b)).astype(low)
-        return carry
-
-    lax.fori_loop(0, owners, send_out, 0)
-
-
-def attend(got, starts, ends, rule, groups):
-    owners, packed, _ = got.shape
-    tokens = packed * 2 // 3
-    group_len = owners * tokens
-    low = jnp.bfloat16
-    whole = jax.ShapeDtypeStruct((group_len, LANES), low)
-    flipped = jax.ShapeDtypeStruct((LANES, group_len), low)
-    return pl.pallas_call(
-        functools.partial(attend_kernel, groups),
-        out_shape=[
-            jax.ShapeDtypeStruct((owners, tokens // 2, LANES), low),
-            jax.ShapeDtypeStruct((group_len, LANES), jnp.float32),
-            whole,
-            whole,
-            flipped,
-            flipped,
-        ],
-        in_specs=[VM] * 4,
-        out_specs=[VM] * 6,
-        scratch_shapes=[
-            pltpu.VMEM((group_len, LANES), low),
-            pltpu.VMEM((ROWS, group_len), jnp.float32),
-        ],
-        compiler_params=pltpu.CompilerParams(vmem_limit_bytes=VMEM_BYTES),
-    )(got, starts, ends, rule)
 
 
 def attend_back_kernel(
@@ -1214,6 +892,470 @@
     )(got, *kept)
 
 
+class Gather:
+    KINDS = ("up", "down", "x", "y", "turn")
+
+    def __init__(self, shards, fulls, sems, pieces):
+        self.shards, self.fulls, self.pieces = shards, fulls, pieces
+        self.send, self.recv, self.send_s, self.recv_s, self.local = sems
+        self.core, self.z, self.yx = place()
+        core, z, yx = self.core, self.z, self.yx
+        self.up_dev, self.down_dev = at_dev(core, lax.min(z + 1, 3), yx), at_dev(core, lax.max(z - 1, 0), yx)
+        self.x_dev, self.y_dev = at_dev(core, z, yx ^ 1), at_dev(core, z, yx ^ 2)
+        self.sib = at_dev(1 - core, z, yx)
+        self.ends = []
+
+    @staticmethod
+    def scratch(count):
+        dma = pltpu.SemaphoreType.DMA
+        return [dma((count, 5, 4)), dma((count, 4, 4)), dma((count, 4, 4)), dma((count, 4, 4)), dma((count,))]
+
+    def spot(self, p, z_at, d, core=None):
+        i, first, rows = self.pieces[p]
+        core = self.core if core is None else core
+        size = self.shards[i].shape[0]
+        start = pl.multiple_of((z_at * 4 + (self.yx ^ d)) * size + first, 16)
+        return self.fulls[i].at[core, pl.ds(start, rows)]
+
+    def copy(self, p, kind, z_at, d, src=None):
+        there = {0: 0, 1: 0, 2: 1, 3: 2, 4: 3}[kind]
+        ref = self.spot(p, z_at, d)
+        device = (self.up_dev, self.down_dev, self.x_dev, self.y_dev)[kind] if kind < 4 else (self.y_dev if d == 1 else self.x_dev)
+        return pltpu.make_async_remote_copy(
+            src_ref=ref if src is None else src,
+            dst_ref=ref,
+            send_sem=self.send.at[p, kind, z_at],
+            recv_sem=self.recv.at[p, there, z_at],
+            device_id=device,
+            device_id_type=MESH_ID,
+        )
+
+    def go(self, condition, p, kind, z_at, d, src=None):
+        def start():
+            self.copy(p, kind, z_at, d, src).start()
+
+        def end():
+            self.copy(p, kind, z_at, d, src).wait_send()
+
+        if condition is None:
+            start()
+            self.ends.append(end)
+        else:
+            pl.when(condition)(start)
+            self.ends.append(lambda: pl.when(condition)(end))
+
+    def across(self, p, d):
+        for z_at in range(4):
+            ref = self.spot(p, z_at, d)
+            copy = pltpu.make_async_remote_copy(
+                src_ref=ref,
+                dst_ref=ref,
+                send_sem=self.send_s.at[p, d, z_at],
+                recv_sem=self.recv_s.at[p, d, z_at],
+                device_id=self.sib,
+                device_id_type=MESH_ID,
+            )
+            copy.start()
+            self.ends.append(copy.wait_send)
+
+    def arrive(self, p, kind, z_at, d):
+        ref = self.spot(p, z_at, d)
+        pltpu.make_async_copy(ref, ref, self.recv.at[p, kind, z_at]).wait()
+
+    def own(self, p):
+        i, first, rows = self.pieces[p]
+        src = self.shards[i].at[pl.ds(first, rows)]
+        z = self.z
+        self.go(z < 3, p, 0, z, 0, src)
+        self.go(z > 0, p, 1, z, 0, src)
+        self.go(None, p, 2, z, 0, src)
+        self.go(None, p, 3, z, 0, src)
+        copy = pltpu.make_async_copy(src, self.spot(p, z, 0), self.local.at[p])
+        copy.start()
+        self.locals_ = getattr(self, "locals_", {})
+        self.locals_[p] = copy
+
+    def z_step(self, p, r):
+        z = self.z
+        for side in (-1, 1):
+            there = (z - r >= 0) if side < 0 else (z + r <= 3)
+            z_at = z + side * r
+
+            def landed(z_at=z_at):
+                self.arrive(p, 0, z_at, 0)
+
+            pl.when(there)(landed)
+            if side < 0:
+                self.go(there & (z < 3), p, 0, z_at, 0)
+            else:
+                self.go(there & (z > 0), p, 1, z_at, 0)
+            self.go(there, p, 2, z_at, 0)
+            self.go(there, p, 3, z_at, 0)
+
+    def plane_step(self, p, r):
+        z = self.z
+        for side in (-1, 1) if r else (0,):
+            z_at = z + side * r
+            there = None if not r else ((z - r >= 0) if side < 0 else (z + r <= 3))
+
+            def landed(z_at=z_at):
+                self.arrive(p, 1, z_at, 1)
+                self.arrive(p, 2, z_at, 2)
+
+            if there is None:
+                landed()
+            else:
+                pl.when(there)(landed)
+            low_z, high_z = z_at < 2, z_at >= 2
+            self.go(low_z if there is None else there & low_z, p, 4, z_at, 1)
+            self.go(high_z if there is None else there & high_z, p, 4, z_at, 2)
+
+    def stage(self, p, s):
+        if s == 0:
+            self.own(p)
+        elif s == 1:
+            self.z_step(p, 1)
+            self.plane_step(p, 0)
+        elif s == 2:
+            self.z_step(p, 2)
+            self.plane_step(p, 1)
+        elif s == 3:
+            self.z_step(p, 3)
+            self.locals_[p].wait()
+            self.across(p, 0)
+            self.plane_step(p, 2)
+        elif s == 4:
+            self.plane_step(p, 3)
+            self.across(p, 1)
+            self.across(p, 2)
+        elif s == 5:
+            for z_at in range(4):
+                self.arrive(p, 3, z_at, 3)
+            self.across(p, 3)
+
+    STAGES = 6
+
+    def steps(self):
+        return len(self.pieces) + self.STAGES - 1
+
+    def run(self, t):
+        for s in range(self.STAGES):
+            if 0 <= t - s < len(self.pieces):
+                self.stage(t - s, s)
+
+    def landed(self):
+        for p in range(len(self.pieces)):
+            for d in range(4):
+                for z_at in range(4):
+                    ref = self.spot(p, z_at, d, 1 - self.core)
+                    pltpu.make_async_copy(ref, ref, self.recv_s.at[p, d, z_at]).wait()
+
+    def finish(self):
+        for end in self.ends:
+            end()
+
+
+def pieces_of(shards, splits):
+    pieces = []
+    for i, (shard, split) in enumerate(zip(shards, splits)):
+        rows = shard.shape[0] // split
+        pieces += [(i, j * rows, rows) for j in range(split)]
+    return pieces
+
+
+class Exchange:
+    def __init__(self, out, landed, sems):
+        self.out, self.landed = out, landed
+        self.send, self.recv = sems
+        self.core, z, yx = place()
+        self.wide = z * 4 + yx
+
+    def copy(self, w):
+        return pltpu.make_async_remote_copy(
+            src_ref=self.out.at[w],
+            dst_ref=self.landed.at[self.wide],
+            send_sem=self.send.at[w],
+            recv_sem=self.recv.at[self.wide],
+            device_id=(self.core, w),
+            device_id_type=MESH_ID,
+        )
+
+    def push(self, w):
+        pl.when(w != self.wide)(lambda: self.copy(w).start())
+
+        def keep():
+            self.landed[w] = self.out[w]
+
+        pl.when(w == self.wide)(keep)
+
+    def wait(self, w):
+        def landed():
+            ref = self.landed.at[w]
+            pltpu.make_async_copy(ref, ref, self.recv.at[w]).wait()
+
+        pl.when(w != self.wide)(landed)
+
+    def finish(self):
+        for w in range(16):
+            pl.when(w != self.wide)(lambda w=w: self.copy(w).wait_send())
+
+
+def front_kernel(groups, *refs):
+    (s_qkv, s_out, s_up, s_down, ada_in, x_ref, one_hot_ref, vec_ref, starts_ref, ends_ref, rule_ref) = refs[:11]
+    (f_qkv, f_out, f_up, f_down, ada_ref, h_ref, kept_ref, out32_ref, q_ref, k_ref, kt_ref, vt_ref, low_ref) = refs[11:24]
+    (w_ref, send_ref, got_ref, back_send, back_got, v_ref, s_ref, load_sem) = refs[24:32]
+    sems = refs[32:]
+    first_flow = Gather([s_qkv], [f_qkv], sems[:5], pieces_of([s_qkv], (2,)))
+    flow = Gather([s_out, s_up, s_down], [f_out, f_up, f_down], sems[5:10], pieces_of([s_out, s_up, s_down], (1, 2, 2)))
+    ada_send, ada_recv = sems[10:12]
+    there = Exchange(send_ref, got_ref, sems[12:14])
+    home = Exchange(back_send, back_got, sems[14:16])
+    core, z, yx = place()
+    wide = z * 4 + yx
+    tokens, width = x_ref.shape
+    half = width // 2
+    mid = tokens // 2
+    two = 2 * tokens
+    f32, low = jnp.float32, jnp.bfloat16
+    entry_barrier([(core, wide ^ r) for r in range(1, 16)] + [(1 - core, wide)])
+
+    first_flow.run(0)
+    ada_copies = []
+    for r in range(1, 16):
+        copy = pltpu.make_async_remote_copy(
+            src_ref=ada_in,
+            dst_ref=ada_ref.at[wide],
+            send_sem=ada_send.at[r],
+            recv_sem=ada_recv.at[r],
+            device_id=(core, wide ^ r),
+            device_id_type=MESH_ID,
+        )
+        copy.start()
+        ada_copies.append(copy)
+    ada_ref[wide] = ada_in[...]
+    first_flow.run(1)
+    x = x_ref[...]
+    centred = x - jnp.mean(x, axis=1, keepdims=True)
+    unit = centred * lax.rsqrt(jnp.mean(centred * centred, axis=1, keepdims=True) + NORM_EPS)
+    first_flow.run(2)
+    for copy in ada_copies:
+        copy.wait_recv()
+    ada = jnp.concatenate([ada_ref[w] for w in range(16)], axis=1)
+
+    def of_tokens(block):
+        rows = ada[:, block * width : (block + 1) * width] + vec_ref[block : block + 1, :]
+        return lax.dot_general(
+            one_hot_ref[...],
+            rows,
+            (((1,), (0,)), ((), ())),
+            precision=HIGHEST_PRECISION,
+            preferred_element_type=f32,
+        )
+
+    h_ref[...] = (unit * (1.0 + of_tokens(2)) + of_tokens(4)).astype(low)
+    for t in range(3, first_flow.steps()):
+        first_flow.run(t)
+    flow.run(0)
+    first_flow.landed()
+
+    group = 256
+    loads = []
+
+    def load(j):
+        g = lax.rem(z + 1 + j, 4)
+        out = []
+        for c in range(2):
+            for part in range(3):
+                rows = pl.ds(pl.multiple_of(g * group + part * width, group), group)
+                out.append(pltpu.make_async_copy(f_qkv.at[c, rows], w_ref.at[j, c, part], load_sem.at[j, c, part]))
+        return out
+
+    for j in range(4):
+        loads.append(load(j))
+        for copy in loads[-1]:
+            copy.start()
+    lane = lane_iota((tokens, LANES))
+    lane_mid = lane_iota((mid, LANES))
+    for j in range(4):
+        g = lax.rem(z + 1 + j, 4)
+        first = pl.multiple_of(g * group, group)
+        for copy in loads[j]:
+            copy.wait()
+
+        def project(part):
+            return nt(h_ref[:, :half], w_ref[j, 0, part]) + nt(h_ref[:, half:], w_ref[j, 1, part])
+
+        q_all, k_all, v_all = (project(part) for part in range(3))
+        kept_ref[:, pl.ds(first, group)] = q_all
+        kept_ref[:, pl.ds(pl.multiple_of(first + width, group), group)] = k_all
+        q_all = q_all * lax.rsqrt(head_sums(q_all * q_all) + NORM_EPS)
+        q_all = q_all * (8.0 * (1.0 + vec_ref[7:8, pl.ds(first, group)]))
+        k_all = k_all * lax.rsqrt(head_sums(k_all * k_all) + NORM_EPS)
+        for pair in range(group // LANES):
+            cols = slice(pair * LANES, (pair + 1) * LANES)
+            q, k, v = q_all[:, cols], k_all[:, cols], v_all[:, cols]
+            head = g * (group // HALF_LANES) + 2 * pair
+            send_ref[head, 0:tokens, :] = jnp.where(lane < HALF_LANES, q, swap_halves(k)).astype(low)
+            send_ref[head + 1, 0:tokens, :] = jnp.where(lane < HALF_LANES, swap_halves(q), k).astype(low)
+            v_a, v_b = v[:mid], v[mid:]
+            send_ref[head, tokens:, :] = jnp.where(lane_mid < HALF_LANES, v_a, swap_halves(v_b)).astype(low)
+            send_ref[head + 1, tokens:, :] = jnp.where(lane_mid < HALF_LANES, swap_halves(v_a), v_b).astype(low)
+        for e in range(4):
+            there.push(g * 4 + e)
+        if j == 1:
+            flow.run(1)
+
+    lane_two = lane_iota((two, LANES))
+
+    def unpack(pair, carry):
+        for e in range(2):
+            there.wait(2 * pair + e)
+        first = pl.multiple_of(pair * two, two)
+        qk = jnp.concatenate([got_ref[2 * pair + e, 0:tokens, :].astype(f32) for e in range(2)], axis=0)
+        spot = first + lax.broadcasted_iota(jnp.int32, (two, LANES), 0)
+        runs = ((spot >= starts_ref[...]) & (spot < ends_ref[...])).astype(f32)
+        barred = nn(runs.astype(low), rule_ref[...])
+        rows = pl.ds(first, two)
+        q_ref[rows, :] = jnp.where(lane_two < HALF_LANES, qk, barred).astype(low)
+        tail = jnp.where(lane_two >= LANES - 3, 1.0, runs)
+        keys = jnp.where(lane_two < HALF_LANES, swap_halves(qk), tail)
+        k_ref[rows, :] = keys.astype(low)
+        kt_ref[:, rows] = keys.T.astype(low)
+        ones = ((lane_mid >= HALF_LANES) & (lane_mid < HALF_LANES + 3)).astype(f32)
+        pieces = []
+        for e in range(2):
+            v = got_ref[2 * pair + e, tokens:, :].astype(f32)
+            pieces.append(jnp.where(lane_mid < HALF_LANES, v, ones))
+            pieces.append(jnp.where(lane_mid < HALF_LANES, swap_halves(v), ones))
+        values = jnp.concatenate(pieces, axis=0)
+        v_ref[rows, :] = values.astype(low)
+        vt_ref[:, rows] = values.T.astype(low)
+        return carry
+
+    lane_q = lane_iota((ROWS, LANES))
+
+    def query_block(limit, b, carry):
+        rows = pl.ds(pl.multiple_of(b * ROWS, ROWS), ROWS)
+        q = q_ref[rows, :]
+
+        def score(c, top):
+            cols = pl.ds(pl.multiple_of(c * CHUNK, CHUNK), CHUNK)
+            s = nn(q, kt_ref[:, cols])
+            s_ref[:, cols] = s
+            return jnp.maximum(top, fold_lanes(s, jnp.maximum))
+
+        whole, left = limit // CHUNK, limit % CHUNK
+        top = lax.fori_loop(0, whole, score, jnp.full((ROWS, LANES), -3e38, f32))
+        if left:
+            tail = slice(whole * CHUNK, limit)
+            s = nn(q, kt_ref[:, tail])
+            s_ref[:, tail] = s
+            top = jnp.maximum(top, fold_lanes(s, jnp.maximum))
+        peak = jnp.max(top, axis=1, keepdims=True)
+
+        def weigh(cols, carry):
+            total, acc = carry
+            p = jnp.exp(s_ref[:, cols] - peak)
+            return total + fold_lanes(p, jnp.add), acc + nn(p.astype(low), v_ref[cols, :])
+
+        zero = jnp.zeros((ROWS, LANES), f32)
+        total, acc = lax.fori_loop(
+            0,
+            whole,
+            lambda c, carry: weigh(pl.ds(pl.multiple_of(c * CHUNK, CHUNK), CHUNK), carry),
+            (zero, zero),
+        )
+        if left:
+            total, acc = weigh(slice(whole * CHUNK, limit), (total, acc))
+        total = jnp.sum(total, axis=1, keepdims=True)
+        out32_ref[rows, :] = acc / total
+        log_total = peak + jnp.log(total)
+        q_ref[rows, :] = lanes_three(lane_q, LANES - 3, -log_total, q.astype(f32)).astype(low)
+        return carry
+
+    def give_back(w, carry):
+        rows = pl.multiple_of(w * tokens, tokens)
+        a = out32_ref[pl.ds(rows, mid), :]
+        b = out32_ref[pl.ds(pl.multiple_of(rows + mid, mid), mid), :]
+        back_send[w] = jnp.where(lane_mid < HALF_LANES, a, swap_halves(b)).astype(low)
+        home.push(w)
+        return carry
+
+    lax.fori_loop(0, 4, unpack, 0)
+    flow.run(2)
+    lax.fori_loop(4, 8, unpack, 0)
+    flow.run(3)
+    plane = 4 * tokens // ROWS
+    t = 4
+    for p in range(4):
+        for first, last, limit in groups:
+            begin, end = max(first, p * plane), min(last, (p + 1) * plane)
+            if begin < end:
+                lax.fori_loop(begin, end, functools.partial(query_block, limit), 0)
+        lax.fori_loop(4 * p, 4 * p + 4, give_back, 0)
+        if p and t < flow.steps():
+            flow.run(t)
+            t += 1
+    for i in range(t, flow.steps()):
+        flow.run(i)
+    for pair in range(8):
+        home.wait(2 * pair)
+        home.wait(2 * pair + 1)
+        cols = slice(pair * LANES, (pair + 1) * LANES)
+        even, odd = back_got[2 * pair].astype(f32), back_got[2 * pair + 1].astype(f32)
+        low_ref[0:mid, cols] = jnp.where(lane_mid < HALF_LANES, even, swap_halves(odd)).astype(low)
+        low_ref[mid:, cols] = jnp.where(lane_mid < HALF_LANES, swap_halves(even), odd).astype(low)
+    flow.landed()
+    first_flow.finish()
+    flow.finish()
+    there.finish()
+    home.finish()
+    for copy in ada_copies:
+        copy.wait_send()
+
+
+def front(shards, ada_block, x_zero, one_hot, vectors, starts, ends, rule, groups):
+    tokens, width = x_zero.shape
+    group_len = 16 * tokens
+    f32, low = jnp.float32, jnp.bfloat16
+    dma = pltpu.SemaphoreType.DMA
+    shape = jax.ShapeDtypeStruct
+    fulls = [shape((2, 16 * s.shape[0], s.shape[1]), low) for s in shards]
+    outs = fulls + [
+        shape((16,) + ada_block.shape, f32),
+        shape((tokens, width), low),
+        shape((tokens, 2 * width), f32),
+        shape((group_len, LANES), f32),
+        shape((group_len, LANES), low),
+        shape((group_len, LANES), low),
+        shape((LANES, group_len), low),
+        shape((LANES, group_len), low),
+        shape((tokens, width), low),
+    ]
+    packed, mid = tokens * 3 // 2, tokens // 2
+    scratch = [
+        pltpu.VMEM((4, 2, 3, 256, width // 2), low),
+        pltpu.VMEM((16, packed, LANES), low),
+        pltpu.VMEM((16, packed, LANES), low),
+        pltpu.VMEM((16, mid, LANES), low),
+        pltpu.VMEM((16, mid, LANES), low),
+        pltpu.VMEM((group_len, LANES), low),
+        pltpu.VMEM((ROWS, group_len), f32),
+        dma((4, 2, 3)),
+    ]
+    scratch += Gather.scratch(2) + Gather.scratch(5) + [dma((16,)) for _ in range(6)]
+    return pl.pallas_call(
+        functools.partial(front_kernel, groups),
+        out_shape=outs,
+        in_specs=[ANY] * 4 + [VM] * 7,
+        out_specs=[ANY] * 4 + [VM] * 9,
+        scratch_shapes=scratch,
+        compiler_params=pltpu.CompilerParams(
+            collective_id=0, has_side_effects=True, vmem_limit_bytes=VMEM_BYTES
+        ),
+    )(*shards, ada_block, x_zero, one_hot, vectors, starts, ends, rule)
+
+
 def run_bounds(lengths, group_len):
     short_sq = jnp.array([side * side for side in SHORT_SIDES], jnp.int32)
     long_sq = jnp.array([side * side for side in LONG_SIDES], jnp.int32)
@@ -1240,11 +1382,6 @@
             if slot_a != slot_b or level_b > level_a:
                 rule[HALF_LANES + a, HALF_LANES + b] = -BIG
     return rule
-
-
-def from_heads(blocks):
-    heads, mid, _ = blocks.shape
-    return blocks.reshape(heads, mid, 2, HALF_LANES).transpose(2, 1, 0, 3).reshape(2 * mid, -1)
 
 
 def to_heads(rows):
@@ -1290,11 +1427,6 @@
     ada_mine = ada_mine + lax.ppermute(ada_theirs, "dp", swap)
     ada_block = jnp.pad(ada_mine, ((0, 8 - slot_count), (0, 0)))
 
-    g_qkv, ada_gathered = gather_weights([flipped[0]], ada_block, 0)
-    g_out, g_up, g_down = gather_weights(list(flipped[1:]), None, 1)
-    ada_product = ada_gathered[:, :slot_count].transpose(1, 0, 2).reshape(slot_count, -1)
-    w_qkv, w_out, w_up, w_down = (g.reshape(2, -1, g.shape[-1]) for g in (g_qkv, g_out, g_up, g_down))
-
     starts, ends = run_bounds(lengths, group_len)
     positions = wide * tok_rows + jnp.arange(tok_rows, dtype=jnp.int32)
     after_start = positions[:, None] >= starts[None, :]
@@ -1314,18 +1446,18 @@
         lax.dot_general(smooth, embed_w, (((0,), (0,)), ((), ())), precision=HIGHEST_PRECISION)
         + vectors[6]
     )
+    groups = same_limits(key_limits(group_len, slot_count))
+    lane_pad = lambda v: jnp.pad(v, (HALF_LANES, HALF_LANES - v.shape[0]))[None]
+    rule = jnp.asarray(attention_rule(slot_count), low)
+    one_hot_wide = jnp.pad(one_hot, ((0, 0), (0, 8 - slot_count)))
+    (w_qkv, w_out, w_up, w_down, ada_gathered, h_one_low, kept_qk, out32, *kept, attn_low) = front(
+        flipped, ada_block, x_zero, one_hot_wide, vectors, lane_pad(starts), lane_pad(ends), rule, groups
+    )
+    kept = [out32] + kept
+    ada_product = ada_gathered[:, :slot_count].transpose(1, 0, 2).reshape(slot_count, -1)
     ada_all = ada_product + vectors[:6].reshape(-1)
     token_ada = jnp.dot(one_hot, ada_all, precision=HIGHEST_PRECISION)
     gate_one, gate_two, scale_one, scale_two, shift_one, shift_two = jnp.split(token_ada, 6, axis=1)
-    h_one_low = pre_norm(x_zero, scale_one, shift_one).astype(low)
-
-    pack, kept_qk = project_heads(h_one_low, w_qkv, gain)
-    got = lax.all_to_all(pack, "wide", 0, 0, tiled=True)
-    groups = same_limits(key_limits(group_len, slot_count))
-    lane_pad = lambda v: jnp.pad(v, (HALF_LANES, HALF_LANES - v.shape[0]))[None]
-    rule = jnp.asarray(attention_rule(slot_count), low)
-    att_pack, *kept = attend(got, lane_pad(starts), lane_pad(ends), rule, groups)
-    attn_low = from_heads(lax.all_to_all(att_pack, "wide", 0, 0, tiled=True))
 
     attn_proj = against(attn_low[:, :half], w_out[0]) + against(attn_low[:, half:], w_out[1])
     x_one = x_zero + gate_one * attn_proj

time: 707 us -> 613 us (0.87)
  local copies, waits for them, and re-layouts: 91.6 us -> 50.9 us
  Pallas kernels: 423 us -> 384 us
  starting transfers between devices: 39.9 us -> 21.8 us
    pallas_call x4 -> x1, Pallas kernels: 202 us -> 165 us  [front(): pl.pallas_call(functools.partial(front_kernel, groups), out_shape=outs, i...]
    slice x4 -> x0, local copies, waits for them, and re-layouts: 21.2 us -> none  [the longest x1 6.26 us: fast_shards(): w_up[1]]
    all_to_all x2 -> x0, starting transfers between devices: 16.1 us -> none  [the longest x1 8.82 us: fast_shards(): attn_low = from_heads(lax.all_to_all(att_pack, 'wide', 0, 0, tiled=True))]
    all_to_all x2 -> x0, waiting for transfers between devices: 7.09 us -> none  [the longest x1 7.09 us: fast_shards(): attn_low = from_heads(lax.all_to_all(att_pack, 'wide', 0, 0, tiled=True))]
    unnamed x161 -> x151, local copies, waits for them, and re-layouts: 15.3 us -> 14.4 us
  transfers between devices with their start and end apart: 13 -> 11, of which waited for: 3 -> 3; matrix products, arithmetic and copies ran while one was open for 23% -> 21% of each run, Pallas kernels for 41% -> 23%
where the time goes in v2:
time: 613 us; the launch traced here: 603 us
  Pallas kernels  384 us (63%)
  matrix products  86.1 us (14%)
  local copies, waits for them, and re-layouts  50.9 us (8%)
  other arithmetic  37.9 us (6%)
  starting transfers between devices  21.8 us (4%)
  waiting for transfers between devices  18.5 us (3%)
    pallas_call x1, Pallas kernels, front(): pl.pallas_call(functools.partial(front_kernel, groups), out_shape=outs, i...  165 us
    pallas_call x2, Pallas kernels, scatter_grads(): pl.pallas_call(functools.partial(scatter_kernel, count), out_shape=[jax.S...  155 us
    dot_general x10, matrix products, contract_rows(): lax.dot_general(left_side, right_side, (((0,), (0,)), ((), ())), precisio...  39.9 us
    pallas_call x1, Pallas kernels, attend_back(): pl.pallas_call(functools.partial(attend_back_kernel, groups), out_shape=j...  33.6 us
    dot_general x7, matrix products, against(): lax.dot_general(left_side, right_side, (((1,), (1,)), ((), ())), preferre...  24.1 us
    pallas_call x1, Pallas kernels, small_sums(): pl.pallas_call(functools.partial(small_kernel, ada_rows, slots), out_shap...  22.1 us
    unnamed x151, local copies, waits for them, and re-layouts  14.4 us
  transfers between devices with their start and end apart: 11, of which 3 were waited for; matrix products, arithmetic and copies ran while one was open for 21% of the time, Pallas kernels for 23%

profile of v2, /device:TPU:0, one launch (start us, length us, event | category | flops | bytes accessed | tf_op | source)
XLA Modules:
  0.0 603.3 jit_solution(166393166529408891)
XLA Ops:
  1.5 4.8 collective-permute-start
  29.8 2.7 convolution_add_fusion.3.refs_5_
  33.1 165.3 %shard_map.270 = (bf16[2,3072,512]{2,1,0:T(8,128)(2,1)}, bf16[2,1024,512]{2,1,0:T(8,128)(2,1)}, bf16[2,4096,512]{2,1,0:T(8,128)(2,1)}, bf16[2,1024,2048]{2,1,0:T...) custom-call(bf16[192,512]{1,0:T(8,128)(2,1)} %fusion.80.refs_0_, ...), custom_call_target="tpu_custom_call" | custom-call | tf_op jit(solution)/shard_map/pallas_call | solution.py:1347
  200.4 4.9 fusion.100
  207.3 3.7 copy-done.68
  215.2 4.0 fusion.31
  221.3 3.9 fusion.4
  225.6 5.0 fusion.148
  234.5 5.2 all-to-all-start
  239.8 6.5 %fusion.153 = (f32[192]{0:T(256)S(1)}, f32[192,4096]{1,0:T(8,128)S(1)}) fusion(bf16[192,1024]{1,0:T(8,128)(2,1)} %get-tuple-element.164, bf16[4096,1024]{1,0:T(8,128)(2,1)} %param.19), kind=kOutput, calls=%fused_computation.270 | convolution fusion | flops 1611398912 | bytes 11928320 | tf_op jit(solution)/shard_map/dot_general | solution.py:113
  248.0 4.7 all-to-all-done.got_ref
  252.7 33.6 %shard_map.271 = bf16[16,288,128]{2,1,0:T(8,128)(2,1)} custom-call(bf16[16,96,128]{2,1,0:T(8,128)(2,1)} %all-to-all-done.got_ref, f32[3072,128]{1,0:T(8,128)} %get-tuple-element.41.out32_ref, bf16[3072,128]{1,0:T(8,128)(2,1)} %get-tuple-element.42.q_ref, bf16[3072,128]{1,0:T(8,128)(2,1)} %get-tuple-element.43.k_ref, ...), custom_call_target="tpu_custom_call" | custom-call | tf_op jit(solution)/shard_map/pallas_call | solution.py:878
  286.3 4.6 all-to-all-start.1
  290.8 2.1 multiply_reduce_fusion
  296.0 4.5 convolution_convert_fusion.2
  301.0 3.3 convolution_convert_fusion
  307.5 9.9 %all-to-all-done.1.got_ref = bf16[16,288,128]{2,1,0:T(8,128)(2,1)} async-done(((bf16[16,288,128]{2,1,0:T(8,128)(2,1)}), bf16[16,288,128]{2,1,0:T(8,128)(2,1)}, u32[]{:S(2)}, u32[]{:S(2)}) %all-to-all-start.1) | async-done | bytes 1179680 | tf_op jit(solution)/shard_map/all_to_all | solution.py:1508
  317.5 8.5 %shard_map.272 = (bf16[192,3072]{1,0:T(8,128)(2,1)}, f32[1,1024]{1,0:T(1,128)}) custom-call(bf16[16,288,128]{2,1,0:T(8,128)(2,1)} %all-to-all-done.1.got_ref, f32[192,2048]{1,0:T(8,128)} %get-tuple-element.46.kept_ref, f32[1,1024]{1,0:T(1,128)} %get-tuple-element.181.gain_ref), custom_call_target="tpu_custom_call" | custom-call | tf_op jit(solution)/shard_map/pallas_call | solution.py:734
  326.0 3.1 fusion.34
  329.1 2.7 fusion.32
  333.6 3.2 fusion.147
  341.2 8.5 %dot_general.113 = f32[16,3,128,192]{2,1,0,3:T(4,128)} reshape(f32[6144,192]{0,1:T(8,128)} %bitcast.35) | data formatting | bytes 9437184 | tf_op jit(solution)/shard_map/dot_general | solution.py:103
  349.7 8.0 %fusion.43 = f32[16,6,3,128]{3,1,2,0:T(8,128)S(1)} fusion(f32[16,3,128,192]{2,1,0,3:T(4,128)} %dot_general.113, f32[192,6]{0,1:T(8,128)S(1)} %reduce_sum.126), kind=kOutput, calls=%fused_computation.67 | convolution fusion | flops 84934656 | bytes 4870656 | tf_op jit(solution)/shard_map/dot_general | solution.py:103
  366.1 22.1 %shard_map.273 = (f32[2,18,128]{2,1,0:T(8,128)}, f32[16,22,128]{2,1,0:T(8,128)}) custom-call(f32[16,37,128]{2,1,0:T(8,128)} %pad_maximum_fusion.10.part_ref), custom_call_target="tpu_custom_call" | custom-call | tf_op jit(solution)/shard_map/pallas_call | solution.py:651
  393.8 3.7 convolution_convert_fusion.1
  403.1 3.7 collective-permute-start.3
  415.2 3.9 collective-permute-done.4
  420.6 5.7 add_convert_fusion
  426.3 5.6 add_convert_fusion.1
  431.9 108.3 %shard_map.275 = (f32[64,512]{1,0:T(8,128)}, f32[256,512]{1,0:T(8,128)}, f32[64,2048]{1,0:T(8,128)}) custom-call(bf16[4,4,64,512]{3,2,1,0:T(8,128)(2,1)} %bitcast.315, bf16[4,4,256,512]{3,2,1,0:T(8,128)(2,1)} %bitcast.309, bf16[4,4,64,2048]{3,2,1,0:T(8,128)(2,1)} %bitcast.310), custom_call_target="tpu_custom_call" | custom-call | tf_op jit(solution)/shard_map/pallas_call | solution.py:571
  549.1 4.5 add_convert_fusion.2
  553.6 46.5 %shard_map.274 = f32[192,512]{1,0:T(8,128)} custom-call(bf16[4,4,192,512]{3,2,1,0:T(8,128)(2,1)} %bitcast.311), custom_call_target="tpu_custom_call" | custom-call | tf_op jit(solution)/shard_map/pallas_call | solution.py:571
  (284 shorter events, 94.4 us)
Async XLA Ops:
  1.5 28.3 %collective-permute-start = (f32[32,1]{1,0:T(8,128)S(1)}, f32[32,1]{1,0:T(8,128)S(1)}, u32[]{:S(2)}, u32[]{:S(2)}) collective-permute-start(f32[32,1]{1,0:T(8,128)S(1)} %get-tuple-element.185), channel_id=1, source_target_pairs={{0,1},{1,2},{2,3},{3,4},{4,5},{5,6},{6,7},{7,8},{8,9},{9,10},{10,1... | collective-permute-start | bytes 392 | tf_op jit(solution)/shard_map/ppermute | solution.py:38
  6.3 23.5 %collective-permute-start.1 = (f32[32,1]{1,0:T(8,128)S(1)}, f32[32,1]{1,0:T(8,128)S(1)}, u32[]{:S(2)}, u32[]{:S(2)}) collective-permute-start(f32[32,1]{1,0:T(8,128)S(1)} %get-tuple-element.186), channel_id=1, source_target_pairs={{1,0},{2,1},{3,2},{4,3},{5,4},{6,5},{7,6},{8,7},{9,8},{10,9},{11,1... | collective-permute-start | bytes 392 | tf_op jit(solution)/shard_map/ppermute | solution.py:40
  11.6 20.9 %collective-permute-start.2 = (f32[6,384]{1,0:T(8,128)S(1)}, f32[6,384]{1,0:T(8,128)S(1)}, u32[]{:S(2)}, u32[]{:S(2)}) collective-permute-start(f32[6,384]{1,0:T(8,128)S(1)} %constant_dynamic-slice_fusion), channel_id=1, source_target_pairs={{0,16},{16,0},{1,17},{17,1},{2,18},{18,2},{3,19},{19,3},{4,20},{20... | collective-permute-start | bytes 27656 | tf_op jit(solution)/shard_map/ppermute | solution.py:1427
  21.8 176.6 %copy-start.11 = (f32[1,512,256]{1,2,0:T(8,128)}, f32[1,512,256]{1,2,0:T(8,128)S(1)}, u32[]{:S(2)}) copy-start(f32[1,512,256]{1,2,0:T(8,128)S(1)} %copy.119) | copy-start | bytes 1572868
  29.7 175.6 %copy-start.51 = (f32[192]{0:T(256)}, f32[192]{0:T(256)S(1)}, u32[]{:S(2)}) copy-start(f32[192]{0:T(256)S(1)} %get-tuple-element.189) | copy-start | bytes 2308
  29.7 175.6 %copy-start.54 = (f32[192]{0:T(256)}, f32[192]{0:T(256)S(1)}, u32[]{:S(2)}) copy-start(f32[192]{0:T(256)S(1)} %get-tuple-element.191) | copy-start | bytes 2308
  29.7 175.7 %copy-start.57 = (f32[192]{0:T(256)}, f32[192]{0:T(256)S(1)}, u32[]{:S(2)}) copy-start(f32[192]{0:T(256)S(1)} %get-tuple-element.190) | copy-start | bytes 2308
  29.7 175.6 %copy-start.47 = (f32[32,1]{1,0:T(8,128)}, f32[32,1]{1,0:T(8,128)S(1)}, u32[]{:S(2)}) copy-start(f32[32,1]{1,0:T(8,128)S(1)} %collective-permute-done) | copy-start | bytes 388
  29.8 175.6 %copy-start.49 = (f32[32,1]{1,0:T(8,128)}, f32[32,1]{1,0:T(8,128)S(1)}, u32[]{:S(2)}) copy-start(f32[32,1]{1,0:T(8,128)S(1)} %collective-permute-done.1) | copy-start | bytes 388
  205.4 25.2 %copy-start = (f32[192,6144]{1,0:T(8,128)}, f32[192,6144]{1,0:T(8,128)S(1)}, u32[]{:S(2)}) copy-start(f32[192,6144]{1,0:T(8,128)S(1)} %fusion.100) | copy-start | bytes 14155780
  206.7 18.9 %copy-start.5 = (f32[192,1024]{1,0:T(8,128)}, f32[192,1024]{1,0:T(8,128)S(1)}, u32[]{:S(2)}) copy-start(f32[192,1024]{1,0:T(8,128)S(1)} %get-tuple-element.163) | copy-start | bytes 2359300
  206.9 18.6 %copy-start.61 = (f32[192]{0:T(256)}, f32[192]{0:T(256)S(1)}, u32[]{:S(2)}) copy-start(f32[192]{0:T(256)S(1)} %fusion.136) | copy-start | bytes 2308
  234.5 18.2 %all-to-all-start = ((bf16[16,96,128]{2,1,0:T(8,128)(2,1)}), bf16[16,96,128]{2,1,0:T(8,128)(2,1)}, u32[]{:S(2)}, u32[]{:S(2)}) async-start(bf16[16,96,128]{2,1,0:T(8,128)(2,1)} %copy.106), calls=%async_computation | async-start | bytes 786432 | tf_op jit(solution)/shard_map/all_to_all | solution.py:1506
  286.3 31.2 %all-to-all-start.1 = ((bf16[16,288,128]{2,1,0:T(8,128)(2,1)}), bf16[16,288,128]{2,1,0:T(8,128)(2,1)}, u32[]{:S(2)}, u32[]{:S(2)}) async-start(bf16[16,288,128]{2,1,0:T(8,128)(2,1)} %shard_map.271), calls=%async_computation.1 | async-start | bytes 2359296 | tf_op jit(solution)/shard_map/all_to_all | solution.py:1508
  295.9 10.1 %collective-permute-start.6 = (bf16[1024,512]{1,0:T(8,128)(2,1)S(1)}, bf16[1024,512]{1,0:T(8,128)(2,1)S(1)}, u32[]{:S(2)}, u32[]{:S(2)}) collective-permute-start(bf16[1024,512]{1,0:T(8,128)(2,1)S(1)} %convolution_convert_fusion.3), channel_id=1, source_target_pairs={{0,16},{16,0},{1,17},{17,1},{2,18},{18,2},{3,19},{19,3},{4,20},{20... | collective-permute-start | bytes 3145736 | tf_op jit(solution)/shard_map/ppermute | solution.py:1482
  300.5 120.0 %collective-permute-start.8 = (bf16[1024,2048]{1,0:T(8,128)(2,1)}, bf16[1024,2048]{1,0:T(8,128)(2,1)}, u32[]{:S(2)}, u32[]{:S(2)}) collective-permute-start(bf16[1024,2048]{1,0:T(8,128)(2,1)} %convolution_convert_fusion.2), channel_id=1, source_target_pairs={{0,16},{16,0},{1,17},{17,1},{2,18},{18,2},{3,19},{19,3},{4,20},{20... | collective-permute-start | bytes 12582920 | tf_op jit(solution)/shard_map/ppermute | solution.py:1482
  304.3 122.0 %collective-permute-start.7 = (bf16[4096,512]{1,0:T(8,128)(2,1)}, bf16[4096,512]{1,0:T(8,128)(2,1)}, u32[]{:S(2)}, u32[]{:S(2)}) collective-permute-start(bf16[4096,512]{1,0:T(8,128)(2,1)} %convolution_convert_fusion), channel_id=1, source_target_pairs={{0,16},{16,0},{1,17},{17,1},{2,18},{18,2},{3,19},{19,3},{4,20},{20... | collective-permute-start | bytes 12582920 | tf_op jit(solution)/shard_map/ppermute | solution.py:1482
  349.7 10.0 %copy-start.40 = (f32[32,192]{1,0:T(8,128)S(1)}, f32[32,192]{1,0:T(8,128)}, u32[]{:S(2)}) copy-start(f32[32,192]{1,0:T(8,128)} %param.15) | copy-start | bytes 73732
  349.7 10.0 %copy-start.48 = (f32[32,1]{1,0:T(8,128)S(1)}, f32[32,1]{1,0:T(8,128)}, u32[]{:S(2)}) copy-start(f32[32,1]{1,0:T(8,128)} %copy-done.47) | copy-start | bytes 388
  349.7 10.0 %copy-start.50 = (f32[32,1]{1,0:T(8,128)S(1)}, f32[32,1]{1,0:T(8,128)}, u32[]{:S(2)}) copy-start(f32[32,1]{1,0:T(8,128)} %copy-done.49) | copy-start | bytes 388
  349.7 10.0 %copy-start.52 = (f32[192]{0:T(256)S(1)}, f32[192]{0:T(256)}, u32[]{:S(2)}) copy-start(f32[192]{0:T(256)} %copy-done.51) | copy-start | bytes 2308
  349.7 10.0 %copy-start.55 = (f32[192]{0:T(256)S(1)}, f32[192]{0:T(256)}, u32[]{:S(2)}) copy-start(f32[192]{0:T(256)} %copy-done.54) | copy-start | bytes 2308
  349.7 10.0 %copy-start.58 = (f32[192]{0:T(256)S(1)}, f32[192]{0:T(256)}, u32[]{:S(2)}) copy-start(f32[192]{0:T(256)} %copy-done.57) | copy-start | bytes 2308
  397.5 151.6 %collective-permute-start.5 = (bf16[3072,512]{1,0:T(8,128)(2,1)}, bf16[3072,512]{1,0:T(8,128)(2,1)}, u32[]{:S(2)}, u32[]{:S(2)}) collective-permute-start(bf16[3072,512]{1,0:T(8,128)(2,1)} %convolution_convert_fusion.1), channel_id=1, source_target_pairs={{0,16},{16,0},{1,17},{17,1},{2,18},{18,2},{3,19},{19,3},{4,20},{20... | collective-permute-start | bytes 9437192 | tf_op jit(solution)/shard_map/ppermute | solution.py:1482
  400.3 9.8 %copy-start.25 = (f32[3,512,384]{2,1,0:T(8,128)S(1)}, f32[3,512,384]{2,1,0:T(8,128)}, u32[]{:S(2)}) copy-start(f32[3,512,384]{2,1,0:T(8,128)} %param.24) | copy-start | bytes 7077892
  400.3 9.8 %copy-start.44 = (bf16[12,1024]{1,0:T(8,128)(2,1)S(1)}, bf16[12,1024]{1,0:T(8,128)(2,1)}, u32[]{:S(2)}) copy-start(bf16[12,1024]{1,0:T(8,128)(2,1)} %copy-done.43) | copy-start | bytes 73732
  400.3 9.8 %copy-start.46 = (f32[12,384]{1,0:T(8,128)S(1)}, f32[12,384]{1,0:T(8,128)}, u32[]{:S(2)}) copy-start(f32[12,384]{1,0:T(8,128)} %reshape.286) | copy-start | bytes 55300
  403.1 12.2 %collective-permute-start.3 = (f32[32,1]{1,0:T(8,128)}, f32[32,1]{1,0:T(8,128)}, u32[]{:S(2)}, u32[]{:S(2)}) collective-permute-start(f32[32,1]{1,0:T(8,128)} %get-tuple-element.183), channel_id=1, source_target_pairs={{0,1},{1,2},{2,3},{3,4},{4,5},{5,6},{6,7},{7,8},{8,9},{9,10},{10,1... | collective-permute-start | bytes 392 | tf_op jit(solution)/shard_map/ppermute | solution.py:38
  413.3 5.8 collective-permute-start.4
  431.9 108.4 %copy-start.12 = (f32[1,512,256]{1,2,0:T(8,128)S(1)}, f32[1,512,256]{1,2,0:T(8,128)}, u32[]{:S(2)}) copy-start(f32[1,512,256]{1,2,0:T(8,128)} %copy-done.11) | copy-start | bytes 1572868
  431.9 108.4 %copy-start.29 = (f32[1,512,256]{1,2,0:T(8,128)S(1)}, f32[1,512,256]{1,2,0:T(8,128)}, u32[]{:S(2)}) copy-start(f32[1,512,256]{1,2,0:T(8,128)} %copy.120) | copy-start | bytes 1572868
  553.6 46.5 %copy-start.30 = (f32[3,512,192]{1,2,0:T(8,128)S(1)}, f32[3,512,192]{1,2,0:T(8,128)}, u32[]{:S(2)}) copy-start(f32[3,512,192]{1,2,0:T(8,128)} %param.20) | copy-start | bytes 3538948
  (50 other events, 240.5 us)

commit v3 on v2

--- a/solution.py
+++ b/solution.py
@@ -485,193 +485,6 @@
     return (core, z * 4 + yx)
 
 
-def scatter_kernel(count, *refs):
-    parts = refs[:count]
-    outs = refs[count : 2 * count]
-    bufs = refs[2 * count : 2 * count + 8 * count]
-    sems = refs[2 * count + 8 * count :]
-    send, recv = sems
-    core, z, yx = place()
-    x_dev, y_dev = at_dev(core, z, yx ^ 1), at_dev(core, z, yx ^ 2)
-    z_devs = [None] + [at_dev(core, lax.rem(z + r, 4), yx) for r in (1, 2, 3)]
-    entry_barrier([x_dev, y_dev] + z_devs[1:])
-    pending = []
-
-    def push(i, slot, src, dst, device):
-        copy = pltpu.make_async_remote_copy(
-            src_ref=src,
-            dst_ref=dst,
-            send_sem=send.at[i, slot],
-            recv_sem=recv.at[i, slot],
-            device_id=device,
-            device_id_type=MESH_ID,
-        )
-        copy.start()
-        pending.append(copy)
-        return copy
-
-    def part(i, dz, d):
-        return parts[i].at[lax.rem(z + dz, 4), yx ^ d]
-
-    def f32(ref):
-        return ref[...].astype(jnp.float32)
-
-    arrivals = []
-    for i in range(count):
-        a_x, a_y, r_x, r_y, t_x, t_y, s_z, r_z = bufs[8 * i : 8 * i + 8]
-        here = {}
-        for j, dz in enumerate((0, 1)):
-            here["ax", dz] = push(i, j, part(i, dz, 3), a_x.at[j], x_dev)
-        for j, dz in enumerate((2, 3)):
-            here["ay", dz] = push(i, 2 + j, part(i, dz, 3), a_y.at[j], y_dev)
-        for j, dz in enumerate((0, 1)):
-            here["rx", dz] = push(i, 4 + dz, part(i, dz, 1), r_x.at[dz], x_dev)
-        for j, dz in enumerate((2, 3)):
-            here["ry", dz] = push(i, 8 + dz, part(i, dz, 2), r_y.at[dz], y_dev)
-        arrivals.append(here)
-    for i in range(count):
-        a_x, a_y, r_x, r_y, t_x, t_y, s_z, r_z = bufs[8 * i : 8 * i + 8]
-        here = arrivals[i]
-        for j, (low, high) in enumerate(((1, 2), (0, 3))):
-            here["ax", low].wait_recv()
-            t_y[j] = (f32(part(i, low, 2)) + f32(a_x.at[low])).astype(jnp.bfloat16)
-            here["ry", low] = push(i, 8 + low, t_y.at[j], r_y.at[low], y_dev)
-            here["ay", high].wait_recv()
-            t_x[j] = (f32(part(i, high, 1)) + f32(a_y.at[high - 2])).astype(jnp.bfloat16)
-            here["rx", high] = push(i, 4 + high, t_x.at[j], r_x.at[high], x_dev)
-    for i in range(count):
-        a_x, a_y, r_x, r_y, t_x, t_y, s_z, r_z = bufs[8 * i : 8 * i + 8]
-        here = arrivals[i]
-        for dz in (1, 2, 3, 0):
-            here["rx", dz].wait_recv()
-            here["ry", dz].wait_recv()
-            total = f32(part(i, dz, 0)) + f32(r_x.at[dz]) + f32(r_y.at[dz])
-            if dz:
-                s_z[dz - 1] = total.astype(jnp.bfloat16)
-                here["rz", dz] = push(i, 12 + dz, s_z.at[dz - 1], r_z.at[dz - 1], z_devs[dz])
-            else:
-                outs[i][...] = total
-    for i in range(count):
-        r_z = bufs[8 * i + 7]
-        for dz in (1, 2, 3):
-            arrivals[i]["rz", dz].wait_recv()
-        outs[i][...] += f32(r_z.at[0]) + f32(r_z.at[1]) + f32(r_z.at[2])
-    for copy in pending:
-        copy.wait_send()
-
-
-def scatter_grads(parts, call_id):
-    count = len(parts)
-    scratch = []
-    for part in parts:
-        for depth in (2, 2, 4, 4, 2, 2, 3, 3):
-            scratch.append(pltpu.VMEM((depth,) + part.shape[2:], jnp.bfloat16))
-    dma = pltpu.SemaphoreType.DMA
-    scratch += [dma((count, 16)), dma((count, 16))]
-    return pl.pallas_call(
-        functools.partial(scatter_kernel, count),
-        out_shape=[jax.ShapeDtypeStruct(part.shape[2:], jnp.float32) for part in parts],
-        in_specs=[VM] * count,
-        out_specs=[VM] * count,
-        scratch_shapes=scratch,
-        compiler_params=pltpu.CompilerParams(
-            collective_id=call_id, has_side_effects=True, vmem_limit_bytes=VMEM_BYTES
-        ),
-    )(*parts)
-
-
-def small_kernel(ada_rows, slots, part_ref, ada_ref, all_ref, landed, summed, other, mine, *sems):
-    send_a, recv_a, send_b, recv_b, send_s, recv_s = sems
-    core, z, yx = place()
-    wide = z * 4 + yx
-    sib = (1 - core, wide)
-    peers = [(core, wide ^ r) for r in range(1, 16)]
-    entry_barrier(peers + [sib])
-    first = []
-    for r in range(1, 16):
-        copy = pltpu.make_async_remote_copy(
-            src_ref=part_ref.at[wide ^ r],
-            dst_ref=landed.at[r],
-            send_sem=send_a.at[r],
-            recv_sem=recv_a.at[r],
-            device_id=peers[r - 1],
-            device_id_type=MESH_ID,
-        )
-        copy.start()
-        first.append(copy)
-    total = part_ref[wide]
-    for r, copy in enumerate(first):
-        copy.wait_recv()
-        total = total + landed[r + 1]
-    summed[...] = total
-    swap = pltpu.make_async_remote_copy(
-        src_ref=summed,
-        dst_ref=other,
-        send_sem=send_s,
-        recv_sem=recv_s,
-        device_id=sib,
-        device_id_type=MESH_ID,
-    )
-    swap.start()
-    swap.wait()
-    ada_ref[core] = summed[0:ada_rows]
-    ada_ref[1 - core] = other[0:ada_rows]
-    both = summed[...] + other[...]
-    rest = both.shape[0] - ada_rows
-    width = ada_rows // slots
-    bias = both[0:width]
-    for j in range(1, slots):
-        bias = bias + both[j * width : (j + 1) * width]
-    mine[0:rest] = both[ada_rows:]
-    mine[rest : rest + width] = bias
-    all_ref[wide] = mine[...]
-    second = []
-    for r in range(1, 16):
-        copy = pltpu.make_async_remote_copy(
-            src_ref=mine,
-            dst_ref=all_ref.at[wide],
-            send_sem=send_b.at[r],
-            recv_sem=recv_b.at[r],
-            device_id=peers[r - 1],
-            device_id_type=MESH_ID,
-        )
-        copy.start()
-        second.append(copy)
-    for copy in second:
-        copy.wait_recv()
-    for copy in first + second:
-        copy.wait_send()
-
-
-def small_sums(parts, ada_rows, slots, call_id):
-    rows = parts.shape[1]
-    out_rows = rows - ada_rows + ada_rows // slots
-    dma = pltpu.SemaphoreType.DMA
-    f32 = jnp.float32
-    return pl.pallas_call(
-        functools.partial(small_kernel, ada_rows, slots),
-        out_shape=[
-            jax.ShapeDtypeStruct((2, ada_rows, LANES), f32),
-            jax.ShapeDtypeStruct((16, out_rows, LANES), f32),
-        ],
-        in_specs=[VM],
-        out_specs=[VM, VM],
-        scratch_shapes=[
-            pltpu.VMEM((16, rows, LANES), f32),
-            pltpu.VMEM((rows, LANES), f32),
-            pltpu.VMEM((rows, LANES), f32),
-            pltpu.VMEM((out_rows, LANES), f32),
-            dma((16,)),
-            dma((16,)),
-            dma((16,)),
-            dma((16,)),
-            dma,
-            dma,
-        ],
-        compiler_params=pltpu.CompilerParams(collective_id=call_id, has_side_effects=True),
-    )(parts)
-
-
 def lane_iota(shape):
     return lax.broadcasted_iota(jnp.int32, shape, len(shape) - 1)
 
@@ -692,55 +505,6 @@
         precision=HIGHEST_PRECISION,
         preferred_element_type=jnp.float32,
     )
-
-
-def heads_back_kernel(got_ref, kept_ref, gain_ref, out_ref, gain_grad_ref):
-    tokens = kept_ref.shape[0]
-    width = kept_ref.shape[1] // 2
-    mid = tokens // 2
-    f32, low = jnp.float32, jnp.bfloat16
-    lane = lane_iota((tokens, LANES))
-    lane_mid = lane_iota((mid, LANES))
-
-    def unnormalize(values, grad):
-        inverse = lax.rsqrt(head_sums(values * values) + NORM_EPS)
-        unit = values * inverse
-        return inverse * (grad - unit * head_sums(unit * grad)), unit
-
-    def step(pair, carry):
-        cols = pl.ds(pl.multiple_of(pair * LANES, LANES), LANES)
-        key_cols = pl.ds(pl.multiple_of(pair * LANES + width, LANES), LANES)
-        val_cols = pl.ds(pl.multiple_of(pair * LANES + 2 * width, LANES), LANES)
-        even = got_ref[2 * pair].astype(f32)
-        odd = got_ref[2 * pair + 1].astype(f32)
-        even_qk, odd_qk = even[:tokens], odd[:tokens]
-        d_query = jnp.where(lane < HALF_LANES, even_qk, swap_halves(odd_qk))
-        d_key = jnp.where(lane < HALF_LANES, swap_halves(even_qk), odd_qk)
-        even_v, odd_v = even[tokens:], odd[tokens:]
-        out_ref[0:mid, val_cols] = jnp.where(lane_mid < HALF_LANES, even_v, swap_halves(odd_v)).astype(low)
-        out_ref[mid:, val_cols] = jnp.where(lane_mid < HALF_LANES, swap_halves(even_v), odd_v).astype(low)
-        scaled = d_query * (8.0 * (1.0 + gain_ref[:, cols]))
-        d_q, unit = unnormalize(kept_ref[:, cols], scaled)
-        gain_grad_ref[:, cols] = jnp.sum(d_query * unit, axis=0, keepdims=True) * 8.0
-        out_ref[:, cols] = d_q.astype(low)
-        out_ref[:, key_cols] = unnormalize(kept_ref[:, key_cols], d_key)[0].astype(low)
-        return carry
-
-    lax.fori_loop(0, width // LANES, step, 0)
-
-
-def heads_backward(got, kept, gain):
-    tokens, width = kept.shape[0], kept.shape[1] // 2
-    return pl.pallas_call(
-        heads_back_kernel,
-        out_shape=[
-            jax.ShapeDtypeStruct((tokens, 3 * width), jnp.bfloat16),
-            jax.ShapeDtypeStruct((1, width), jnp.float32),
-        ],
-        in_specs=[VM] * 3,
-        out_specs=[VM] * 2,
-        compiler_params=pltpu.CompilerParams(vmem_limit_bytes=VMEM_BYTES),
-    )(got, kept, gain)
 
 
 ROWS = 256
@@ -797,99 +561,6 @@
     return jnp.where(
         lane == first, high, jnp.where(lane == first + 1, mid, jnp.where(lane == first + 2, rest, otherwise))
     )
-
-
-def attend_back_kernel(
-    groups, got_ref, out32_ref, q_ref, k_ref, kt_ref, vt_ref, pack_ref, g_ref, gt_ref, qt_ref, dq_ref, dkt_ref, dvt_ref
-):
-    owners = got_ref.shape[0]
-    mid = got_ref.shape[1]
-    tokens = 2 * mid
-    two = 2 * tokens
-    f32, low = jnp.float32, jnp.bfloat16
-    lane = lane_iota((two, LANES))
-    lane_mid = lane_iota((mid, LANES))
-
-    def unpack(pair, carry):
-        rows = pl.ds(pl.multiple_of(pair * two, two), two)
-        pieces = []
-        for e in range(2):
-            g = got_ref[2 * pair + e].astype(f32)
-            pieces += [g, swap_halves(g)]
-        grad = jnp.where(lane < HALF_LANES, jnp.concatenate(pieces, axis=0), 0.0)
-        delta = jnp.sum(grad * out32_ref[rows, :], axis=1, keepdims=True)
-        grad = lanes_three(lane, HALF_LANES, -delta, grad)
-        g_ref[rows, :] = grad.astype(low)
-        gt_ref[:, rows] = grad.T[:HALF_LANES].astype(low)
-        qt_ref[:, rows] = q_ref[rows, :].astype(f32).T[:HALF_LANES].astype(low)
-        return carry
-
-    lax.fori_loop(0, owners // 2, unpack, 0)
-    dkt_ref[...] = jnp.zeros_like(dkt_ref)
-    dvt_ref[...] = jnp.zeros_like(dvt_ref)
-
-    def query_block(limit, b, carry):
-        rows = pl.ds(pl.multiple_of(b * ROWS, ROWS), ROWS)
-        q, g = q_ref[rows, :], g_ref[rows, :]
-        qt, gt = qt_ref[:, rows], gt_ref[:, rows]
-
-        def chunk(cols, acc):
-            p = jnp.exp(nn(q, kt_ref[:, cols]))
-            ds = (p * nn(g, vt_ref[:, cols])).astype(low)
-            dvt_ref[:, cols] += nn(gt, p.astype(low))
-            dkt_ref[:, cols] += nn(qt, ds)
-            return acc + nn(ds, k_ref[cols, :])
-
-        whole, left = limit // CHUNK, limit % CHUNK
-        acc = lax.fori_loop(
-            0,
-            whole,
-            lambda c, acc: chunk(pl.ds(pl.multiple_of(c * CHUNK, CHUNK), CHUNK), acc),
-            jnp.zeros((ROWS, LANES), f32),
-        )
-        if left:
-            acc = chunk(slice(whole * CHUNK, limit), acc)
-        dq_ref[rows, :] = acc
-        return carry
-
-    for first, last, limit in groups:
-        lax.fori_loop(first, last, functools.partial(query_block, limit), 0)
-
-    def send_out(pair, carry):
-        first = pl.multiple_of(pair * two, two)
-        rows = pl.ds(first, two)
-        dkv = jnp.concatenate([dkt_ref[:, rows], dvt_ref[:, rows]], axis=0).T
-        dq = dq_ref[rows, :]
-        qk = jnp.where(lane < HALF_LANES, dq, swap_halves(dkv)).astype(low)
-        for e in range(2):
-            pack_ref[2 * pair + e, 0:tokens, :] = qk[e * tokens : (e + 1) * tokens]
-            a = dkv[e * tokens : e * tokens + mid]
-            b = dkv[e * tokens + mid : (e + 1) * tokens]
-            pack_ref[2 * pair + e, tokens:, :] = jnp.where(lane_mid < HALF_LANES, swap_halves(a), b).astype(low)
-        return carry
-
-    lax.fori_loop(0, owners // 2, send_out, 0)
-
-
-def attend_back(got, kept, groups):
-    owners, mid, _ = got.shape
-    group_len = owners * mid * 2
-    low = jnp.bfloat16
-    return pl.pallas_call(
-        functools.partial(attend_back_kernel, groups),
-        out_shape=jax.ShapeDtypeStruct((owners, 3 * mid, LANES), low),
-        in_specs=[VM] * 6,
-        out_specs=VM,
-        scratch_shapes=[
-            pltpu.VMEM((group_len, LANES), low),
-            pltpu.VMEM((HALF_LANES, group_len), low),
-            pltpu.VMEM((HALF_LANES, group_len), low),
-            pltpu.VMEM((group_len, LANES), jnp.float32),
-            pltpu.VMEM((HALF_LANES, group_len), jnp.float32),
-            pltpu.VMEM((HALF_LANES, group_len), jnp.float32),
-        ],
-        compiler_params=pltpu.CompilerParams(vmem_limit_bytes=VMEM_BYTES),
-    )(got, *kept)
 
 
 class Gather:
@@ -1356,6 +1027,541 @@
     )(*shards, ada_block, x_zero, one_hot, vectors, starts, ends, rule)
 
 
+class Scatter:
+    STAGES = 6
+
+    def __init__(self, parts, outs, bufs, sems, pieces):
+        self.parts, self.outs, self.bufs, self.pieces = parts, outs, bufs, pieces
+        self.send, self.recv = sems
+        core, z, yx = place()
+        self.z, self.yx = z, yx
+        self.x_dev, self.y_dev = at_dev(core, z, yx ^ 1), at_dev(core, z, yx ^ 2)
+        self.up_dev, self.down_dev = at_dev(core, lax.min(z + 1, 3), yx), at_dev(core, lax.max(z - 1, 0), yx)
+        self.ends = []
+
+    @staticmethod
+    def scratch(shapes, count):
+        low = jnp.bfloat16
+        out = []
+        for rows, cols in shapes:
+            out += [pltpu.VMEM((depth, rows, cols), low) for depth in (2, 2, 4, 4, 3, 3)]
+        dma = pltpu.SemaphoreType.DMA
+        return out + [dma((count, 8)), dma((count, 8))]
+
+    def push(self, p, slot, src, dst, device):
+        copy = pltpu.make_async_remote_copy(
+            src_ref=src,
+            dst_ref=dst,
+            send_sem=self.send.at[p, slot],
+            recv_sem=self.recv.at[p, slot],
+            device_id=device,
+            device_id_type=MESH_ID,
+        )
+        copy.start()
+        return copy
+
+    def arrive(self, p, slot, ref):
+        pltpu.make_async_copy(ref, ref, self.recv.at[p, slot]).wait()
+
+    def stage(self, p, s):
+        i, first, rows = self.pieces[p]
+        rows = pl.ds(first, rows)
+        part = self.parts[i]
+        names = ("turn_x", "turn_y", "rx", "ry", "up", "down")
+        buf = dict(zip(names, self.bufs[6 * i : 6 * i + 6]))
+        z, yx = self.z, self.yx
+        f32, low = jnp.float32, jnp.bfloat16
+        lo2, hi2 = pl.ds(0, 2), pl.ds(2, 2)
+
+        def view(name, which):
+            return buf[name].at[which, rows]
+
+        def wide(ref):
+            return ref[...].astype(f32)
+
+        def hop(condition, slot, name, which, device):
+            ref = view(name, which)
+
+            def start():
+                self.push(p, slot, ref, ref, device)
+
+            def end():
+                pltpu.make_async_copy(ref, ref, self.send.at[p, slot]).wait()
+
+            pl.when(condition)(start)
+            self.ends.append(lambda: pl.when(condition)(end))
+
+        if s == 0:
+            copies = [
+                self.push(p, 0, part.at[lo2, yx ^ 3, rows], view("turn_x", lo2), self.x_dev),
+                self.push(p, 1, part.at[hi2, yx ^ 3, rows], view("turn_y", lo2), self.y_dev),
+                self.push(p, 2, part.at[lo2, yx ^ 1, rows], view("rx", lo2), self.x_dev),
+                self.push(p, 3, part.at[hi2, yx ^ 2, rows], view("ry", hi2), self.y_dev),
+            ]
+            self.ends += [copy.wait_send for copy in copies]
+        elif s == 1:
+            turn = view("turn_x", lo2)
+            self.arrive(p, 0, turn)
+            turn[...] = (wide(part.at[lo2, yx ^ 2, rows]) + wide(turn)).astype(low)
+            self.ends.append(self.push(p, 4, turn, view("ry", lo2), self.y_dev).wait_send)
+            turn = view("turn_y", lo2)
+            self.arrive(p, 1, turn)
+            turn[...] = (wide(part.at[hi2, yx ^ 1, rows]) + wide(turn)).astype(low)
+            self.ends.append(self.push(p, 5, turn, view("rx", hi2), self.x_dev).wait_send)
+        elif s == 2:
+            self.arrive(p, 2, view("rx", lo2))
+            self.arrive(p, 3, view("ry", hi2))
+            self.arrive(p, 4, view("ry", lo2))
+            self.arrive(p, 5, view("rx", hi2))
+            self.outs[i][rows] = wide(part.at[z, yx, rows]) + wide(view("rx", z)) + wide(view("ry", z))
+            for z_at in range(4):
+                total = wide(part.at[z_at, yx, rows]) + wide(view("rx", z_at)) + wide(view("ry", z_at))
+                view("rx", z_at)[...] = total.astype(low)
+
+            def first_up():
+                view("up", pl.ds(0, 3))[...] = view("rx", pl.ds(1, 3))[...]
+
+            def first_down():
+                view("down", pl.ds(0, 3))[...] = view("rx", pl.ds(0, 3))[...]
+
+            pl.when(z == 0)(first_up)
+            hop(z == 0, 6, "up", pl.ds(0, 3), self.up_dev)
+            pl.when(z == 3)(first_down)
+            hop(z == 3, 7, "down", pl.ds(0, 3), self.down_dev)
+        elif s in (3, 4):
+            at = s - 2
+            count = 3 - at
+
+            def add_up():
+                self.arrive(p, 6, view("up", pl.ds(at - 1, count + 1)))
+                ref = view("up", pl.ds(at, count))
+                ref[...] = (wide(ref) + wide(view("rx", pl.ds(at + 1, count)))).astype(low)
+
+            def add_down():
+                self.arrive(p, 7, view("down", pl.ds(0, count + 1)))
+                ref = view("down", pl.ds(0, count))
+                ref[...] = (wide(ref) + wide(view("rx", pl.ds(0, count)))).astype(low)
+
+            pl.when(z == at)(add_up)
+            hop(z == at, 6, "up", pl.ds(at, count), self.up_dev)
+            pl.when(z == 3 - at)(add_down)
+            hop(z == 3 - at, 7, "down", pl.ds(0, count), self.down_dev)
+        else:
+            out = self.outs[i].at[rows]
+
+            def end_low():
+                self.arrive(p, 7, view("down", pl.ds(0, 1)))
+                out[...] += wide(view("down", 0))
+
+            def end_high():
+                self.arrive(p, 6, view("up", pl.ds(2, 1)))
+                out[...] += wide(view("up", 2))
+
+            def end_inner(at):
+                out[...] += wide(view("up", at - 1)) + wide(view("down", at))
+
+            pl.when(z == 0)(end_low)
+            pl.when(z == 1)(lambda: end_inner(1))
+            pl.when(z == 2)(lambda: end_inner(2))
+            pl.when(z == 3)(end_high)
+
+    def steps(self):
+        return len(self.pieces) + self.STAGES - 1
+
+    def run(self, t):
+        for s in reversed(range(self.STAGES)):
+            if 0 <= t - s < len(self.pieces):
+                self.stage(t - s, s)
+
+    def finish(self):
+        for end in self.ends:
+            end()
+
+
+COMMON_ROWS = 48
+
+
+def back_kernel(groups, splits, *refs):
+    (
+        d_att, out32_ref, q_ref, k_ref, kt_ref, vt_ref, kept_ref, vec_ref, h_ref, w_any,
+        p_down, p_up, p_out, x_ref, scale_ref, dx_one, hot_ref, g_one, g_two, g_scale, g_shift,
+        smooth_ref, embed_ref, mass_ref, ok_ref,
+    ) = refs[:25]
+    (o_down, o_up, o_out, o_qkv, ada_both, common_all, bias_all, map_ref) = refs[25:33]
+    (
+        send_ref, got_ref, back_send, back_got, g_ref, gt_ref, qt_ref, dq_ref, dkt_ref, dvt_ref,
+        w_ref, dproj, h_both, p_qkv, dh_ref, ada_ref, com_ref, ada_land, com_land, ada_sum, com_sum, ada_sib, com_sib,
+        bias_own, com_own, edge, edge_left, edge_right,
+    ) = refs[33:61]
+    rest = refs[61:]
+    flow_bufs, rest = rest[:18], rest[18:]
+    flow_sems, rest = rest[:2], rest[2:]
+    last_bufs, rest = rest[:6], rest[6:]
+    last_sems, rest = rest[:2], rest[2:]
+    (ex_s, ex_r, home_s, home_r, w_sem, sib_s, sib_r, small_s, small_r, spread_s, spread_r, edge_s, edge_r) = rest
+    core, z, yx = place()
+    wide = z * 4 + yx
+    sib = (1 - core, wide)
+    f32, low = jnp.float32, jnp.bfloat16
+    tokens, width = h_ref.shape
+    half = width // 2
+    mid = tokens // 2
+    two = 2 * tokens
+    flow = Scatter([p_down, p_up, p_out], [o_down, o_up, o_out], flow_bufs, flow_sems, splits[0])
+    last = Scatter([p_qkv], [o_qkv], last_bufs, last_sems, splits[1])
+    there = Exchange(back_send, back_got, (ex_s, ex_r))
+    home = Exchange(send_ref, got_ref, (home_s, home_r))
+    entry_barrier([(core, wide ^ r) for r in range(1, 16)] + [sib])
+
+    def to_sib(slot, src, dst):
+        copy = pltpu.make_async_remote_copy(
+            src_ref=src, dst_ref=dst, send_sem=sib_s.at[slot], recv_sem=sib_r.at[slot], device_id=sib, device_id_type=MESH_ID
+        )
+        copy.start()
+        return copy
+
+    lane = lane_iota((two, LANES))
+    lane_tok = lane_iota((tokens, LANES))
+    lane_mid = lane_iota((mid, LANES))
+
+    def pack(pair, carry):
+        cols = pl.ds(pl.multiple_of(pair * LANES, LANES), LANES)
+        a, b = d_att[0:mid, cols].astype(f32), d_att[mid:, cols].astype(f32)
+        back_send[2 * pair] = jnp.where(lane_mid < HALF_LANES, a, swap_halves(b)).astype(low)
+        back_send[2 * pair + 1] = jnp.where(lane_mid < HALF_LANES, swap_halves(a), b).astype(low)
+        there.push(2 * pair)
+        there.push(2 * pair + 1)
+        return carry
+
+    lax.fori_loop(0, 8, pack, 0)
+    slab = 3 * width // 4
+
+    def w_load(j):
+        rows = pl.ds(j * slab, slab)
+        return pltpu.make_async_copy(w_any.at[:, rows], w_ref.at[j % 2], w_sem.at[j % 2])
+
+    w_load(0).start()
+    w_load(1).start()
+    theirs = pl.ds(pl.multiple_of((1 - core) * half, half), half)
+    mine = pl.ds(pl.multiple_of(core * half, half), half)
+    h_copy = to_sib(0, h_ref.at[:, theirs], h_both.at[core])
+    h_both[core] = h_ref[:, mine]
+    flow.run(0)
+    dkt_ref[...] = jnp.zeros_like(dkt_ref)
+    dvt_ref[...] = jnp.zeros_like(dvt_ref)
+
+    def unpack(pair, carry):
+        there.wait(2 * pair)
+        there.wait(2 * pair + 1)
+        rows = pl.ds(pl.multiple_of(pair * two, two), two)
+        pieces = []
+        for e in range(2):
+            g = back_got[2 * pair + e].astype(f32)
+            pieces += [g, swap_halves(g)]
+        grad = jnp.where(lane < HALF_LANES, jnp.concatenate(pieces, axis=0), 0.0)
+        delta = jnp.sum(grad * out32_ref[rows, :], axis=1, keepdims=True)
+        grad = lanes_three(lane, HALF_LANES, -delta, grad)
+        g_ref[rows, :] = grad.astype(low)
+        gt_ref[:, rows] = grad.T[:HALF_LANES].astype(low)
+        qt_ref[:, rows] = q_ref[rows, :].astype(f32).T[:HALF_LANES].astype(low)
+        return carry
+
+    lax.fori_loop(0, 8, unpack, 0)
+    flow.run(1)
+
+    def query_block(limit, b, carry):
+        rows = pl.ds(pl.multiple_of(b * ROWS, ROWS), ROWS)
+        q, g = q_ref[rows, :], g_ref[rows, :]
+        qt, gt = qt_ref[:, rows], gt_ref[:, rows]
+
+        def chunk(cols, acc):
+            p = jnp.exp(nn(q, kt_ref[:, cols]))
+            ds = (p * nn(g, vt_ref[:, cols])).astype(low)
+            dvt_ref[:, cols] += nn(gt, p.astype(low))
+            dkt_ref[:, cols] += nn(qt, ds)
+            return acc + nn(ds, k_ref[cols, :])
+
+        whole, left = limit // CHUNK, limit % CHUNK
+        acc = lax.fori_loop(
+            0,
+            whole,
+            lambda c, acc: chunk(pl.ds(pl.multiple_of(c * CHUNK, CHUNK), CHUNK), acc),
+            jnp.zeros((ROWS, LANES), f32),
+        )
+        if left:
+            acc = chunk(slice(whole * CHUNK, limit), acc)
+        dq_ref[rows, :] = acc
+        return carry
+
+    t = 2
+    for first, stop, limit in groups:
+        for begin in range(first, stop, 2):
+            end = min(begin + 2, stop)
+            lax.fori_loop(begin, end, functools.partial(query_block, limit), 0)
+            if begin >= 3 and t < flow.steps():
+                flow.run(t)
+                t += 1
+
+    def send_out(pair, carry):
+        rows = pl.ds(pl.multiple_of(pair * two, two), two)
+        dkv = jnp.concatenate([dkt_ref[:, rows], dvt_ref[:, rows]], axis=0).T
+        qk = jnp.where(lane < HALF_LANES, dq_ref[rows, :], swap_halves(dkv)).astype(low)
+        for e in range(2):
+            send_ref[2 * pair + e, 0:tokens, :] = qk[e * tokens : (e + 1) * tokens]
+            a = dkv[e * tokens : e * tokens + mid]
+            b = dkv[e * tokens + mid : (e + 1) * tokens]
+            send_ref[2 * pair + e, tokens:, :] = jnp.where(lane_mid < HALF_LANES, swap_halves(a), b).astype(low)
+            home.push(2 * pair + e)
+        return carry
+
+    lax.fori_loop(0, 8, send_out, 0)
+
+    def per_slot(values):
+        return lax.dot_general(
+            hot_ref[...],
+            values,
+            (((1,), (0,)), ((), ())),
+            precision=HIGHEST_PRECISION,
+            preferred_element_type=f32,
+        )
+
+    for block, ref in ((0, g_one), (1, g_two), (3, g_scale), (5, g_shift)):
+        ada_ref[:, block * width : (block + 1) * width] = per_slot(ref[...])
+    while t < flow.steps() - 2:
+        flow.run(t)
+        t += 1
+
+    def unnormalize(values, grad):
+        inverse = lax.rsqrt(head_sums(values * values) + NORM_EPS)
+        unit = values * inverse
+        return inverse * (grad - unit * head_sums(unit * grad)), unit
+
+    com_ref[...] = jnp.zeros_like(com_ref)
+
+    def heads_back(pair, carry):
+        home.wait(2 * pair)
+        home.wait(2 * pair + 1)
+        cols = pl.ds(pl.multiple_of(pair * LANES, LANES), LANES)
+        key_cols = pl.ds(pl.multiple_of(pair * LANES + width, LANES), LANES)
+        val_cols = pl.ds(pl.multiple_of(pair * LANES + 2 * width, LANES), LANES)
+        even = got_ref[2 * pair].astype(f32)
+        odd = got_ref[2 * pair + 1].astype(f32)
+        even_qk, odd_qk = even[:tokens], odd[:tokens]
+        d_query = jnp.where(lane_tok < HALF_LANES, even_qk, swap_halves(odd_qk))
+        d_key = jnp.where(lane_tok < HALF_LANES, swap_halves(even_qk), odd_qk)
+        even_v, odd_v = even[tokens:], odd[tokens:]
+        dproj[core, 0:mid, val_cols] = jnp.where(lane_mid < HALF_LANES, even_v, swap_halves(odd_v)).astype(low)
+        dproj[core, mid:, val_cols] = jnp.where(lane_mid < HALF_LANES, swap_halves(even_v), odd_v).astype(low)
+        scaled = d_query * (8.0 * (1.0 + vec_ref[7:8, cols]))
+        d_q, unit = unnormalize(kept_ref[:, cols], scaled)
+        com_ref[33:34, cols] = jnp.sum(d_query * unit, axis=0, keepdims=True) * 8.0
+        dproj[core, :, cols] = d_q.astype(low)
+        dproj[core, :, key_cols] = unnormalize(kept_ref[:, key_cols], d_key)[0].astype(low)
+        return carry
+
+    lax.fori_loop(0, 8, heads_back, 0)
+    d_copy = to_sib(1, dproj.at[core], dproj.at[core])
+
+    for j in range(4):
+        w_load(j).wait()
+        for c in range(2):
+            part = nn(dproj[core, :, j * slab : (j + 1) * slab], w_ref[j % 2, c])
+            cols = slice(c * half, (c + 1) * half)
+            dh_ref[:, cols] = part if j == 0 else dh_ref[:, cols] + part
+        if j < 2:
+            w_load(j + 2).start()
+    h_copy.wait_recv()
+    d_copy.wait_recv()
+
+    def weight_grad(c, carry):
+        cols = pl.ds(pl.multiple_of(c * two, two), two)
+        total = nn(dproj[0, :, cols].astype(f32).T.astype(low), h_both[0])
+        total = total + nn(dproj[1, :, cols].astype(f32).T.astype(low), h_both[1])
+        p_qkv[c // 2, pl.ds(2 * (c % 2), 2)] = total.astype(low).reshape(2, tokens, half)
+        return carry
+
+    lax.fori_loop(0, 8, weight_grad, 0)
+    last.run(0)
+    while t < flow.steps():
+        flow.run(t)
+        t += 1
+
+    x = x_ref[...]
+    centred = x - jnp.mean(x, axis=1, keepdims=True)
+    rstd = lax.rsqrt(jnp.mean(centred * centred, axis=1, keepdims=True) + NORM_EPS)
+    unit = centred * rstd
+    d_h = dh_ref[...]
+    ada_ref[:, 2 * width : 3 * width] = per_slot(d_h * unit)
+    ada_ref[:, 4 * width : 5 * width] = per_slot(d_h)
+    d_unit = d_h * (1.0 + scale_ref[...])
+    d_x = rstd * (
+        d_unit
+        - jnp.mean(d_unit, axis=1, keepdims=True)
+        - unit * jnp.mean(d_unit * unit, axis=1, keepdims=True)
+    )
+    d_x = d_x + dx_one[...]
+    last.run(1)
+    com_ref[0:32, :] = lax.dot_general(
+        smooth_ref[...], d_x, (((1,), (0,)), ((), ())), precision=HIGHEST_PRECISION, preferred_element_type=f32
+    )
+    com_ref[32:33, :] = jnp.sum(d_x, axis=0, keepdims=True)
+    com_ref[34:38, :] = mass_ref[...]
+    small = []
+    quarter = COMMON_ROWS // 2
+
+    def common_part(ref, w):
+        rows = pl.ds(pl.multiple_of((w // 8) * quarter, 8), quarter)
+        return ref.at[rows, pl.ds(pl.multiple_of((w % 8) * LANES, LANES), LANES)]
+
+    ada_width = 6 * width // 16
+
+    def ada_part(ref, w):
+        return ref.at[:, pl.ds(pl.multiple_of(w * ada_width, LANES), ada_width)]
+
+    def spread(sem_s, sem_r, r, slot, src, dst):
+        copy = pltpu.make_async_remote_copy(
+            src_ref=src,
+            dst_ref=dst,
+            send_sem=sem_s.at[slot, r],
+            recv_sem=sem_r.at[slot, r],
+            device_id=(core, wide ^ r),
+            device_id_type=MESH_ID,
+        )
+        copy.start()
+        return copy
+
+    for r in range(1, 16):
+        small.append(spread(small_s, small_r, r, 0, ada_part(ada_ref, wide ^ r), ada_land.at[r]))
+        small.append(spread(small_s, small_r, r, 1, common_part(com_ref, wide ^ r), com_land.at[r]))
+    d_smooth = lax.dot_general(
+        embed_ref[...], d_x, (((1,), (1,)), ((), ())), precision=HIGHEST_PRECISION, preferred_element_type=f32
+    )
+    left, right = ok_ref[0:1, :], ok_ref[1:2, :]
+    share = d_smooth / (2.0 + left + right)
+    spot = lane_iota((32, LANES))
+    edge[...] = jnp.where(spot == 0, share[:, 0:1], jnp.where(spot == 1, share[:, tokens - 1 : tokens], 0.0))
+
+    def edge_copy(slot, dst, shift):
+        return pltpu.make_async_remote_copy(
+            src_ref=edge,
+            dst_ref=dst,
+            send_sem=edge_s.at[slot],
+            recv_sem=edge_r.at[slot],
+            device_id=(core, lax.rem(wide + shift, 16)),
+            device_id_type=MESH_ID,
+        )
+
+    to_right, to_left = edge_copy(0, edge_left, 1), edge_copy(1, edge_right, 15)
+    last.run(2)
+    ada_total, com_total = ada_part(ada_ref, wide)[...], common_part(com_ref, wide)[...]
+    for copy in small:
+        copy.wait_recv()
+    for r in range(1, 16):
+        ada_total = ada_total + ada_land[r]
+        com_total = com_total + com_land[r]
+    ada_sum[...] = ada_total
+    com_sum[...] = com_total
+    swaps = [to_sib(2, ada_sum, ada_sib), to_sib(3, com_sum, com_sib)]
+    last.run(3)
+    for copy in swaps:
+        copy.wait_recv()
+    ada_both[core] = ada_sum[...]
+    ada_both[1 - core] = ada_sib[...]
+    bias = jnp.sum(ada_sum[...] + ada_sib[...], axis=0, keepdims=True)
+    bias_own[...] = jnp.broadcast_to(bias, bias_own.shape)
+    com_own[...] = com_sum[...] + com_sib[...]
+    ada_part(bias_all, wide)[...] = bias_own[...]
+    common_part(common_all, wide)[...] = com_own[...]
+    back = []
+    for r in range(1, 16):
+        back.append(spread(spread_s, spread_r, r, 0, bias_own, ada_part(bias_all, wide)))
+        back.append(spread(spread_s, spread_r, r, 1, com_own, common_part(common_all, wide)))
+    for i in range(4, last.steps()):
+        last.run(i)
+    to_right.start()
+    to_left.start()
+    to_right.wait_recv()
+    to_left.wait_recv()
+    column = lane_iota((32, tokens))
+    before = jnp.where(column == 0, edge_left[:, 1:2], jnp.roll(share, 1, axis=1))
+    after = jnp.where(column == tokens - 1, edge_right[:, 0:1], jnp.roll(share, -1, axis=1))
+    map_ref[...] = 2.0 * share + left * before + right * after
+    for copy in back:
+        copy.wait_recv()
+    for copy in small + swaps + back + [h_copy, d_copy, to_right, to_left]:
+        copy.wait_send()
+    flow.finish()
+    last.finish()
+    there.finish()
+    home.finish()
+
+
+def back(args, groups, splits, call_id):
+    d_att, out32 = args[0], args[1]
+    tokens, width = d_att.shape
+    group_len = 16 * tokens
+    half, mid, packed = width // 2, tokens // 2, tokens * 3 // 2
+    f32, low = jnp.float32, jnp.bfloat16
+    dma = pltpu.SemaphoreType.DMA
+    shape = jax.ShapeDtypeStruct
+    parts = args[10:13]
+    sizes = [p.shape[2:] for p in parts] + [(3 * width // 16, half)]
+    counts = [p.shape[2] for p in parts]
+    first = pieces_of([shape(s, f32) for s in sizes[:3]], splits[0])
+    second = pieces_of([shape(sizes[3], f32)], splits[1])
+    ada_width, quarter = 6 * width // 16, COMMON_ROWS // 2
+    outs = [shape(s, f32) for s in sizes] + [
+        shape((2, 8, ada_width), f32),
+        shape((COMMON_ROWS, width), f32),
+        shape((8, 6 * width), f32),
+        shape((32, tokens), f32),
+    ]
+    vm = pltpu.VMEM
+    scratch = [
+        vm((16, packed, LANES), low),
+        vm((16, packed, LANES), low),
+        vm((16, mid, LANES), low),
+        vm((16, mid, LANES), low),
+        vm((group_len, LANES), low),
+        vm((HALF_LANES, group_len), low),
+        vm((HALF_LANES, group_len), low),
+        vm((group_len, LANES), f32),
+        vm((HALF_LANES, group_len), f32),
+        vm((HALF_LANES, group_len), f32),
+        vm((2, 2, 3 * width // 4, half), low),
+        vm((2, tokens, 3 * width), low),
+        vm((2, tokens, half), low),
+        vm((4, 4) + sizes[3], low),
+        vm((tokens, width), f32),
+        vm((8, 6 * width), f32),
+        vm((COMMON_ROWS, width), f32),
+        vm((16, 8, ada_width), f32),
+        vm((16, quarter, LANES), f32),
+        vm((8, ada_width), f32),
+        vm((quarter, LANES), f32),
+        vm((8, ada_width), f32),
+        vm((quarter, LANES), f32),
+        vm((8, ada_width), f32),
+        vm((quarter, LANES), f32),
+        vm((32, LANES), f32),
+        vm((32, LANES), f32),
+        vm((32, LANES), f32),
+    ]
+    scratch += Scatter.scratch(sizes[:3], len(first)) + Scatter.scratch(sizes[3:], len(second))
+    scratch += [dma((16,)) for _ in range(4)] + [dma((2,)), dma((4,)), dma((4,))]
+    scratch += [dma((2, 16)) for _ in range(4)] + [dma((2,)), dma((2,))]
+    return pl.pallas_call(
+        functools.partial(back_kernel, groups, (first, second)),
+        out_shape=outs,
+        in_specs=[VM] * 9 + [ANY] + [VM] * 15,
+        out_specs=[VM] * 8,
+        scratch_shapes=scratch,
+        compiler_params=pltpu.CompilerParams(
+            collective_id=call_id, has_side_effects=True, vmem_limit_bytes=60 * 1024 * 1024
+        ),
+    )(*args)
+
+
 def run_bounds(lengths, group_len):
     short_sq = jnp.array([side * side for side in SHORT_SIDES], jnp.int32)
     long_sq = jnp.array([side * side for side in LONG_SIDES], jnp.int32)
@@ -1382,12 +1588,6 @@
             if slot_a != slot_b or level_b > level_a:
                 rule[HALF_LANES + a, HALF_LANES + b] = -BIG
     return rule
-
-
-def to_heads(rows):
-    tokens = rows.shape[0]
-    split = rows.reshape(2, tokens // 2, HEADS, HALF_LANES)
-    return split.transpose(2, 1, 0, 3).reshape(HEADS, tokens // 2, LANES)
 
 
 def fast_shards(
@@ -1479,9 +1679,9 @@
         width = inputs.shape[1] // 2
         other = lax.dynamic_slice_in_dim(inputs, (1 - core) * width, width, 1)
         own = lax.dynamic_slice_in_dim(inputs, core * width, width, 1)
-        theirs = lax.ppermute(contract_rows(grad_rows, other).astype(low), "dp", swap)
-        total = (contract_rows(grad_rows, own) + theirs.astype(f32)).astype(low)
-        return total.reshape(4, 4, -1, width)
+        their_rows, theirs = lax.ppermute((grad_rows, other), "dp", swap)
+        total = contract_rows(grad_rows, own) + contract_rows(their_rows, theirs)
+        return total.astype(low).reshape(4, 4, -1, width)
 
     def both_halves(values, weights):
         return jnp.concatenate(
@@ -1501,48 +1701,23 @@
     d_gate_one = d_x_one * attn_proj
     p_out = summed_over_cores(d_attn, attn_low)
     d_attended = both_halves(d_attn, w_out).astype(low)
-    s_out, s_up, s_down = scatter_grads([p_out, p_up, p_down], 2)
-
-    back = lax.all_to_all(to_heads(d_attended), "wide", 0, 0, tiled=True)
-    d_pack = attend_back(back, kept, groups)
-    d_got = lax.all_to_all(d_pack, "wide", 0, 0, tiled=True)
-    d_projected_low, d_gain = heads_backward(d_got, kept_qk, gain)
-    p_qkv = summed_over_cores(d_projected_low, h_one_low)
-    (s_qkv,) = scatter_grads([p_qkv], 3)
-    d_h_one = both_halves(d_projected_low, w_qkv)
-    _, norm_back_one = jax.vjp(pre_norm, x_zero, scale_one, shift_one)
-    d_x_zero, d_scale_one, d_shift_one = norm_back_one(d_h_one)
-    d_x_zero = d_x_zero + d_x_one
-    d_token_ada = jnp.concatenate(
-        [d_gate_one, d_gate_two, d_scale_one, d_scale_two, d_shift_one, d_shift_two], axis=1
-    )
-    d_ada_part = contract_rows(one_hot, d_token_ada, HIGHEST_PRECISION)
-    d_smooth = lax.dot_general(embed_w, d_x_zero, (((1,), (1,)), ((), ())), precision=HIGHEST_PRECISION)
-    d_embed = lax.dot_general(smooth, d_x_zero, (((1,), (0,)), ((), ())), precision=HIGHEST_PRECISION)
-    grad_share = d_smooth / (2.0 + left_ok + right_ok)
-    rim_share = padded(grad_share, (("wide", 1),), 1)
-    map_grad = 2.0 * grad_share + left_ok * rim_share[:, :-2] + right_ok * rim_share[:, 2:]
-
-    wides = lax.axis_size("wide")
-    ada_rows = d_ada_part.reshape(slot_count, wides, -1, LANES)
-    per_slot = ada_rows.shape[2]
-    ada_rows = ada_rows.transpose(1, 0, 2, 3).reshape(wides, -1, LANES)
-    code_rows = code_mass.reshape(-1, model_width)
-    common = jnp.concatenate([d_embed, jnp.sum(d_x_zero, axis=0)[None], d_gain, code_rows], axis=0)
-    common_rows = common.shape[0]
-    common = common.reshape(common_rows, wides, -1).transpose(1, 0, 2).reshape(wides, -1, LANES)
-    plain_rows = common.shape[1]
-    small_in = jnp.concatenate([ada_rows, common], axis=1)
-    ada_count = ada_rows.shape[1]
-    d_ada_both, sums = small_sums(small_in, ada_count, slot_count, 4)
-    common_sum = sums[:, :plain_rows].reshape(wides, common_rows, -1).transpose(1, 0, 2)
-    common_sum = common_sum.reshape(common_rows, model_width)
+    flags = jnp.pad(jnp.stack([left_ok, right_ok]), ((0, 6), (0, 0)))
+    hot_rows = one_hot_wide.T
+    mass_rows = code_mass.reshape(-1, model_width)
+    s_down, s_up, s_out, s_qkv, d_ada_both, common_sum, bias_sum, map_grad = back(
+        [d_attended, *kept, kept_qk, vectors, h_one_low, w_qkv, p_down, p_up, p_out, x_zero, scale_one, d_x_one]
+        + [hot_rows, d_gate_one, d_gate_two, d_scale_two, d_shift_two, smooth, embed_w, mass_rows, flags],
+        groups,
+        ((2, 2, 1), (2,)),
+        1,
+    )
     embed_rows = embed_w.shape[0]
     d_embed_all = common_sum[:embed_rows]
-    bias_sum = sums[:, plain_rows:].reshape(6, model_width)
-    d_vectors_all = jnp.concatenate([bias_sum, common_sum[embed_rows : embed_rows + 2]], axis=0)
-    histogram = common_sum[embed_rows + 2 :].reshape(-1) * (code_book.shape[0] / tokens_all)
-    d_ada_own = d_ada_both.reshape(2 * slot_count, per_slot * LANES)
+    bias_rows = bias_sum[0].reshape(6, model_width)
+    d_vectors_all = jnp.concatenate([bias_rows, common_sum[embed_rows : embed_rows + 2]], axis=0)
+    mass_all = common_sum[embed_rows + 2 : embed_rows + 2 + mass_rows.shape[0]]
+    histogram = mass_all.reshape(-1) * (code_book.shape[0] / tokens_all)
+    d_ada_own = d_ada_both[:, :slot_count].reshape(2 * slot_count, -1)
     grad_ada = contract_rows(silu_rows.astype(f32), d_ada_own, HIGHEST_PRECISION)
 
     owned_grads = (s_qkv.T, s_out.T, s_up.T, s_down.T, grad_ada)

time: 613 us -> 527 us (0.86)
  local copies, waits for them, and re-layouts: 50.9 us -> 28.6 us
  waiting for transfers between devices: 18.5 us -> 0.02 us
  matrix products: 86.1 us -> 71.5 us
  starting transfers between devices: 21.8 us -> 8.69 us
  Pallas kernels: 384 us -> 375 us
    all_to_all x2 -> x0, waiting for transfers between devices: 14.6 us -> none  [the longest x1 9.94 us: fast_shards(): d_got = lax.all_to_all(d_pack, 'wide', 0, 0, tiled=True)]
    dot_general x10 -> x7, matrix products: 39.9 us -> 25.4 us  [contract_rows(): lax.dot_general(left_side, right_side, (((0,), (0,)), ((), ())), precisio...]
    all_to_all x2 -> x0, starting transfers between devices: 9.78 us -> none  [the longest x1 5.22 us: fast_shards(): back = lax.all_to_all(to_heads(d_attended), 'wide', 0, 0, tiled=True)]
    pallas_call x5 -> x1, Pallas kernels: 219 us -> 210 us  [back(): pl.pallas_call(functools.partial(back_kernel, groups, (first, second)), o...]
    dot_general x1 -> x0, local copies, waits for them, and re-layouts: 8.51 us -> none  [contract_rows(): lax.dot_general(left_side, right_side, (((0,), (0,)), ((), ())), precisio...]
    another operation x12 -> x13, other arithmetic: 6.69 us -> 13.2 us  [nesterov(): return jnp.stack([new_moment, new_weight, new_average])]
    unnamed x151 -> x93, local copies, waits for them, and re-layouts: 14.4 us -> 8.75 us
  transfers between devices with their start and end apart: 11 -> 9, of which waited for: 3 -> 0; matrix products, arithmetic and copies ran while one was open for 21% -> 9% of each run, Pallas kernels for 23% -> 0%
where the time goes in v3:
time: 527 us; the launch traced here: 519 us
  Pallas kernels  375 us (71%)
  matrix products  71.5 us (14%)
  other arithmetic  32 us (6%)
  local copies, waits for them, and re-layouts  28.6 us (5%)
  starting transfers between devices  8.69 us (2%)
    pallas_call x1, Pallas kernels, back(): pl.pallas_call(functools.partial(back_kernel, groups, (first, second)), o...  210 us
    pallas_call x1, Pallas kernels, front(): pl.pallas_call(functools.partial(front_kernel, groups), out_shape=outs, i...  165 us
    dot_general x7, matrix products, against(): lax.dot_general(left_side, right_side, (((1,), (1,)), ((), ())), preferre...  26.6 us
    dot_general x7, matrix products, contract_rows(): lax.dot_general(left_side, right_side, (((0,), (0,)), ((), ())), precisio...  25.4 us
    another operation x13, other arithmetic, nesterov(): return jnp.stack([new_moment, new_weight, new_average])  13.2 us
    dot_general x6, matrix products, both_halves(): jnp.dot(values, weights[h], preferred_element_type=f32)  11.5 us
  transfers between devices with their start and end apart: 9, of which 0 were waited for; matrix products, arithmetic and copies ran while one was open for 9% of the time, Pallas kernels for 0%

profile of v3, /device:TPU:0, one launch (start us, length us, event | category | flops | bytes accessed | tf_op | source)
XLA Modules:
  0.0 519.2 jit_solution(12332153806681058369)
XLA Ops:
  1.5 4.8 collective-permute-start
  8.4 1.8 all-gather
  22.5 1.8 fusion.64.refs_3_
  24.2 1.7 fusion.65.refs_0_
  25.9 1.5 fusion.82.refs_1_
  30.9 1.7 convolution_add_fusion.3.refs_5_.refs_13_
  33.2 165.3 %shard_map.270 = (bf16[2,3072,512]{2,1,0:T(8,128)(2,1)}, bf16[2,1024,512]{2,1,0:T(8,128)(2,1)}, bf16[2,4096,512]{2,1,0:T(8,128)(2,1)}, bf16[2,1024,2048]{2,1,0:T...) custom-call(bf16[192,512]{1,0:T(8,128)(2,1)} %fusion.65.refs_0_, ...), custom_call_target="tpu_custom_call" | custom-call | tf_op jit(solution)/shard_map/pallas_call | solution.py:1018
  198.5 2.0 fusion.38
  200.5 4.9 fusion.74
  206.8 2.3 copy-done.32
  210.2 2.2 fusion
  213.9 12.9 %fusion.29 = (bf16[192,4096]{1,0:T(8,128)(2,1)}, bf16[192,4096]{1,0:T(8,128)(2,1)S(1)}) fusion(f32[192,2048]{1,0:T(8,128)S(1)} %copy-done.33, f32[192,2048]{1,0:T(8,128)S(1)} %fusion.4, f32[192,4096]{1,0:T(8,128)S(1)} %fusion.13, bf16[2,4096,512]{2,1,0:T(8,128)(2,1)S(1)} %bitcast.325, bf16[192,1024]{1,0:T(8,128)(2,1)S(1)} %get-tuple-element.131), kind=kOutput, calls=%fused_computation.34 | convolution fusion | flops 824180736 | bytes 13828096 | tf_op jit(solution)/shard_map/dot_general | solution.py:113
  226.8 3.0 fusion.11
  229.9 2.6 fusion.8
  232.6 1.5 fusion.2
  235.6 5.0 fusion.106
  242.7 1.6 fusion.68
  245.3 6.2 %fusion.70 = f32[4096,512]{1,0:T(8,128)} fusion(bf16[192,4096]{1,0:T(8,128)(2,1)} %get-tuple-element.133, bf16[192,1024]{1,0:T(8,128)(2,1)S(1)} %get-tuple-element.131, s32[]{:T(128)S(6)} %select_n.57), kind=kOutput, calls=%fused_computation.126 | convolution fusion | flops 805306368 | bytes 10158084 | tf_op jit(solution)/shard_map/dot_general | solution.py:103
  252.0 3.0 fusion.111
  257.1 2.6 fusion.48
  264.2 2.6 add_convert_fusion.2
  266.8 4.6 add_convert_fusion.1
  271.4 4.8 add_convert_fusion
  276.2 209.5 %shard_map.271 = (f32[64,2048]{1,0:T(8,128)}, f32[256,512]{1,0:T(8,128)}, f32[64,512]{1,0:T(8,128)}, f32[192,512]{1,0:T(8,128)}, f32[2,8,384]{2,1,0:T(8,128)}, /...) custom-call(bf16[192,1024]{1,0:T(8,128)(2,1)} %pad_maximum_fusion.6.refs_0_, ...), custom_call_target="tpu_custom_call" | custom-call | tf_op jit(solution)/shard_map/pallas_call | solution.py:1553
  487.2 1.7 fusion.80
  493.4 3.1 fusion.100
  496.5 2.2 fusion.47
  498.7 2.1 fusion.101
  502.9 1.6 copy.50
  505.4 1.8 fusion.103
  508.1 2.1 fusion.104
  513.3 1.7 pad_maximum_fusion.1
  (186 shorter events, 51.2 us)
Async XLA Ops:
  1.5 29.3 %collective-permute-start = (f32[32,1]{1,0:T(8,128)S(1)}, f32[32,1]{1,0:T(8,128)S(1)}, u32[]{:S(2)}, u32[]{:S(2)}) collective-permute-start(f32[32,1]{1,0:T(8,128)S(1)} %get-tuple-element.148), channel_id=1, source_target_pairs={{0,1},{1,2},{2,3},{3,4},{4,5},{5,6},{6,7},{7,8},{8,9},{9,10},{10,1... | collective-permute-start | bytes 392 | tf_op jit(solution)/shard_map/ppermute | solution.py:38
  6.3 24.5 %collective-permute-start.1 = (f32[32,1]{1,0:T(8,128)S(1)}, f32[32,1]{1,0:T(8,128)S(1)}, u32[]{:S(2)}, u32[]{:S(2)}) collective-permute-start(f32[32,1]{1,0:T(8,128)S(1)} %get-tuple-element.149), channel_id=1, source_target_pairs={{1,0},{2,1},{3,2},{4,3},{5,4},{6,5},{7,6},{8,7},{9,8},{10,9},{11,1... | collective-permute-start | bytes 392 | tf_op jit(solution)/shard_map/ppermute | solution.py:40
  10.2 8.3 %copy-start.26 = (bf16[12,1024]{1,0:T(8,128)(2,1)}, bf16[12,1024]{1,0:T(8,128)(2,1)S(1)}, u32[]{:S(2)}) copy-start(bf16[12,1024]{1,0:T(8,128)(2,1)S(1)} %reshape.236) | copy-start | bytes 73732
  11.6 21.0 %collective-permute-start.2 = (f32[6,384]{1,0:T(8,128)S(1)}, f32[6,384]{1,0:T(8,128)S(1)}, u32[]{:S(2)}, u32[]{:S(2)}) collective-permute-start(f32[6,384]{1,0:T(8,128)S(1)} %constant_dynamic-slice_fusion.3), channel_id=1, source_target_pairs={{0,16},{16,0},{1,17},{17,1},{2,18},{18,2},{3,19},{19,3},{4,20},{20... | collective-permute-start | bytes 27656 | tf_op jit(solution)/shard_map/ppermute | solution.py:1627
  19.3 8.2 %copy-start.17 = (f32[3,32,1024]{2,1,0:T(8,128)S(1)}, f32[3,32,1024]{2,1,0:T(8,128)}, u32[]{:S(2)}) copy-start(f32[3,32,1024]{2,1,0:T(8,128)} %param.25) | copy-start | bytes 1179652
  21.5 9.2 %copy-start.28 = (f32[32,192]{1,0:T(8,128)S(1)}, f32[32,192]{1,0:T(8,128)}, u32[]{:S(2)}) copy-start(f32[32,192]{1,0:T(8,128)} %param.15) | copy-start | bytes 73732
  30.9 174.6 %copy-start.24 = (f32[32,192]{1,0:T(8,128)}, f32[32,192]{1,0:T(8,128)S(1)}, u32[]{:S(2)}) copy-start(f32[32,192]{1,0:T(8,128)S(1)} %fusion.86.refs_21_) | copy-start | bytes 73732
  198.5 6.9 %copy-start = (f32[192,1024]{1,0:T(8,128)S(1)}, f32[192,1024]{1,0:T(8,128)}, u32[]{:S(2)}) copy-start(f32[192,1024]{1,0:T(8,128)} %convolution_add_fusion.3.refs_5_.refs_13_) | copy-start | bytes 2359300
  198.5 6.9 %copy-start.9 = (bf16[2,1024,512]{2,1,0:T(8,128)(2,1)S(1)}, bf16[2,1024,512]{2,1,0:T(8,128)(2,1)}, u32[]{:S(2)}) copy-start(bf16[2,1024,512]{2,1,0:T(8,128)(2,1)} %get-tuple-element.39) | copy-start | bytes 6291460
  206.8 38.5 %copy-start.4 = (bf16[192,1024]{1,0:T(8,128)(2,1)}, bf16[192,1024]{1,0:T(8,128)(2,1)S(1)}, u32[]{:S(2)}) copy-start(bf16[192,1024]{1,0:T(8,128)(2,1)S(1)} %get-tuple-element.131) | copy-start | bytes 1179652
  226.8 8.8 %copy-start.15 = (bf16[192,4096]{1,0:T(8,128)(2,1)}, bf16[192,4096]{1,0:T(8,128)(2,1)S(1)}, u32[]{:S(2)}) copy-start(bf16[192,4096]{1,0:T(8,128)(2,1)S(1)} %get-tuple-element.134) | copy-start | bytes 4718596
  240.6 11.4 %copy-start.23 = (bf16[192,1024]{1,0:T(8,128)(2,1)}, bf16[192,1024]{1,0:T(8,128)(2,1)S(1)}, u32[]{:S(2)}) copy-start(bf16[192,1024]{1,0:T(8,128)(2,1)S(1)} %get-tuple-element.178) | copy-start | bytes 1179652
  241.7 9.7 %copy-start.1 = (f32[192,1024]{1,0:T(8,128)}, f32[192,1024]{1,0:T(8,128)S(1)}, u32[]{:S(2)}) copy-start(f32[192,1024]{1,0:T(8,128)S(1)} %get-tuple-element.122.refs_15_) | copy-start | bytes 2359300
  242.7 9.3 %slice-start.2 = ((s8[8388608]{0:T(1024)(128)(4,1)}), s8[4194304]{0:T(1024)(128)(4,1)S(1)}, s32[]{:S(2)}) async-start(s8[8388608]{0:T(1024)(128)(4,1)} %bitcast.317), calls=%async_computation.2 | async-start | bytes 8388608
  244.3 7.7 %slice-start.3 = ((s8[8388608]{0:T(1024)(128)(4,1)}), s8[4194304]{0:T(1024)(128)(4,1)S(1)}, s32[]{:S(2)}) async-start(s8[8388608]{0:T(1024)(128)(4,1)} %bitcast.317), calls=%async_computation.3 | async-start | bytes 8388608
  244.3 19.9 %collective-permute-start.7 = (bf16[192,1024]{1,0:T(8,128)(2,1)}, bf16[192,1024]{1,0:T(8,128)(2,1)}, u32[]{:S(2)}, u32[]{:S(2)}) collective-permute-start(bf16[192,1024]{1,0:T(8,128)(2,1)} %multiply_convert_fusion.1), channel_id=1, source_target_pairs={{0,16},{16,0},{1,17},{17,1},{2,18},{18,2},{3,19},{19,3},{4,20},{20... | collective-permute-start | bytes 1179656 | tf_op jit(solution)/shard_map/ppermute | solution.py:1682
  251.5 19.9 %collective-permute-start.5 = (bf16[192,4096]{1,0:T(8,128)(2,1)}, bf16[192,4096]{1,0:T(8,128)(2,1)}, u32[]{:S(2)}, u32[]{:S(2)}) collective-permute-start(bf16[192,4096]{1,0:T(8,128)(2,1)} %get-tuple-element.133), channel_id=1, source_target_pairs={{0,16},{16,0},{1,17},{17,1},{2,18},{18,2},{3,19},{19,3},{4,20},{20... | collective-permute-start | bytes 4718600 | tf_op jit(solution)/shard_map/ppermute | solution.py:1682
  251.5 15.3 %collective-permute-start.3 = (bf16[192,1024]{1,0:T(8,128)(2,1)S(1)}, bf16[192,1024]{1,0:T(8,128)(2,1)}, u32[]{:S(2)}, u32[]{:S(2)}) collective-permute-start(bf16[192,1024]{1,0:T(8,128)(2,1)S(1)} %get-tuple-element.130), channel_id=1, source_target_pairs={{0,16},{16,0},{1,17},{17,1},{2,18},{18,2},{3,19},{19,3},{4,20},{20... | collective-permute-start | bytes 1179656 | tf_op jit(solution)/shard_map/ppermute | solution.py:1682
  257.1 7.0 %collective-permute-start.8 = (bf16[192,512]{1,0:T(8,128)(2,1)S(1)}, bf16[192,512]{1,0:T(8,128)(2,1)S(1)}, u32[]{:S(2)}, u32[]{:S(2)}) collective-permute-start(bf16[192,512]{1,0:T(8,128)(2,1)S(1)} %constant_dynamic-slice_fusion), channel_id=1, source_target_pairs={{0,16},{16,0},{1,17},{17,1},{2,18},{18,2},{3,19},{19,3},{4,20},{20... | collective-permute-start | bytes 589832 | tf_op jit(solution)/shard_map/ppermute | solution.py:1682
  259.8 7.0 %collective-permute-start.4 = (bf16[192,2048]{1,0:T(8,128)(2,1)S(1)}, bf16[192,2048]{1,0:T(8,128)(2,1)S(1)}, u32[]{:S(2)}, u32[]{:S(2)}) collective-permute-start(bf16[192,2048]{1,0:T(8,128)(2,1)S(1)} %constant_dynamic-slice_fusion.2), channel_id=1, source_target_pairs={{0,16},{16,0},{1,17},{17,1},{2,18},{18,2},{3,19},{19,3},{4,20},{20... | collective-permute-start | bytes 2359304 | tf_op jit(solution)/shard_map/ppermute | solution.py:1682
  264.1 7.3 %collective-permute-start.6 = (bf16[192,512]{1,0:T(8,128)(2,1)S(1)}, bf16[192,512]{1,0:T(8,128)(2,1)S(1)}, u32[]{:S(2)}, u32[]{:S(2)}) collective-permute-start(bf16[192,512]{1,0:T(8,128)(2,1)S(1)} %constant_dynamic-slice_fusion.1), channel_id=1, source_target_pairs={{0,16},{16,0},{1,17},{17,1},{2,18},{18,2},{3,19},{19,3},{4,20},{20... | collective-permute-start | bytes 589832 | tf_op jit(solution)/shard_map/ppermute | solution.py:1682
  264.2 7.2 %slice-start = ((s8[8388608]{0:T(1024)(128)(4,1)}), s8[4194304]{0:T(1024)(128)(4,1)S(1)}, s32[]{:S(2)}) async-start(s8[8388608]{0:T(1024)(128)(4,1)} %bitcast.313), calls=%async_computation | async-start | bytes 8388608
  276.2 211.0 %copy-start.18 = (f32[3,32,1024]{2,1,0:T(8,128)S(1)}, f32[3,32,1024]{2,1,0:T(8,128)}, u32[]{:S(2)}) copy-start(f32[3,32,1024]{2,1,0:T(8,128)} %param.25) | copy-start | bytes 1179652
  276.2 217.2 %copy-start.27 = (bf16[12,1024]{1,0:T(8,128)(2,1)S(1)}, bf16[12,1024]{1,0:T(8,128)(2,1)}, u32[]{:S(2)}) copy-start(bf16[12,1024]{1,0:T(8,128)(2,1)} %copy-done.26) | copy-start | bytes 73732
  485.7 12.9 %copy-start.6 = (f32[3,2048,64]{1,2,0:T(8,128)S(1)}, f32[3,2048,64]{1,2,0:T(8,128)}, u32[]{:S(2)}) copy-start(f32[3,2048,64]{1,2,0:T(8,128)} %param.23) | copy-start | bytes 4718596
  504.5 7.4 %copy-start.25 = (f32[3,8,1024]{2,1,0:T(8,128)S(1)}, f32[3,8,1024]{2,1,0:T(8,128)}, u32[]{:S(2)}) copy-start(f32[3,8,1024]{2,1,0:T(8,128)} %param.26) | copy-start | bytes 294916
  504.5 7.4 %copy-start.29 = (f32[1,6,1024]{2,1,0:T(8,128)S(1)}, f32[1,6,1024]{2,1,0:T(8,128)}, u32[]{:S(2)}) copy-start(f32[1,6,1024]{2,1,0:T(8,128)} %concatenate.44) | copy-start | bytes 73732
  504.5 7.4 %copy-start.31 = (f32[1,2,1024]{2,1,0:T(2,128)S(1)}, f32[1,2,1024]{2,1,0:T(2,128)}, u32[]{:S(2)}) copy-start(f32[1,2,1024]{2,1,0:T(2,128)} %slice_bitcast_fusion.2) | copy-start | bytes 24580
  504.5 8.0 %copy-start.20 = (f32[1,32,1024]{2,1,0:T(8,128)S(1)}, f32[1,32,1024]{2,1,0:T(8,128)}, u32[]{:S(2)}) copy-start(f32[1,32,1024]{2,1,0:T(8,128)} %get-tuple-element.145) | copy-start | bytes 393220
  504.5 8.0 %copy-start.21 = (f32[1,32,1024]{2,1,0:T(8,128)S(1)}, f32[1,32,1024]{2,1,0:T(8,128)}, u32[]{:S(2)}) copy-start(f32[1,32,1024]{2,1,0:T(8,128)} %get-tuple-element.146) | copy-start | bytes 393220
  504.5 8.8 %copy-start.2 = (f32[1,512,384]{2,1,0:T(8,128)S(1)}, f32[1,512,384]{2,1,0:T(8,128)}, u32[]{:S(2)}) copy-start(f32[1,512,384]{2,1,0:T(8,128)} %get-tuple-element.132) | copy-start | bytes 2359300
  505.4 7.9 %copy-start.3 = (f32[1,512,384]{2,1,0:T(8,128)S(1)}, f32[1,512,384]{2,1,0:T(8,128)}, u32[]{:S(2)}) copy-start(f32[1,512,384]{2,1,0:T(8,128)} %fusion.47) | copy-start | bytes 2359300
  (19 other events, 72.5 us)

commit v4 on v3

--- a/solution.py
+++ b/solution.py
@@ -452,6 +452,10 @@
 ANY = pl.BlockSpec(memory_space=pl.ANY)
 VM = pl.BlockSpec(memory_space=pltpu.VMEM)
 VMEM_BYTES = 56 * 1024 * 1024
+SHORT_TOTAL = sum(side * side for side in SHORT_SIDES)
+LONG_TOTAL = sum(side * side for side in LONG_SIDES)
+GELU_SCALE = math.sqrt(2.0 / math.pi)
+GELU_CUBE = 0.044715
 LANES = 128
 HALF_LANES = 64
 BIG = 1e30
@@ -714,8 +718,8 @@
             if 0 <= t - s < len(self.pieces):
                 self.stage(t - s, s)
 
-    def landed(self):
-        for p in range(len(self.pieces)):
+    def landed(self, which=None):
+        for p in range(len(self.pieces)) if which is None else which:
             for d in range(4):
                 for z_at in range(4):
                     ref = self.spot(p, z_at, d, 1 - self.core)
@@ -771,26 +775,127 @@
             pl.when(w != self.wide)(lambda w=w: self.copy(w).wait_send())
 
 
-def front_kernel(groups, *refs):
-    (s_qkv, s_out, s_up, s_down, ada_in, x_ref, one_hot_ref, vec_ref, starts_ref, ends_ref, rule_ref) = refs[:11]
-    (f_qkv, f_out, f_up, f_down, ada_ref, h_ref, kept_ref, out32_ref, q_ref, k_ref, kt_ref, vt_ref, low_ref) = refs[11:24]
-    (w_ref, send_ref, got_ref, back_send, back_got, v_ref, s_ref, load_sem) = refs[24:32]
-    sems = refs[32:]
+def column_of(row):
+    return jnp.broadcast_to(row, (LANES, row.shape[1])).T[:, 0:1]
+
+
+def exact(left_side, right_side, contract=(1, 0)):
+    return lax.dot_general(
+        left_side,
+        right_side,
+        (((contract[0],), (contract[1],)), ((), ())),
+        precision=HIGHEST_PRECISION,
+        preferred_element_type=jnp.float32,
+    )
+
+
+def gelu(values):
+    return 0.5 * values * (1.0 + jnp.tanh(GELU_SCALE * (values + GELU_CUBE * values * values * values)))
+
+
+def front_kernel(groups, slots, *refs):
+    (s_qkv, s_out, s_up, s_down, cond_ref, ada_any, map_ref, embed_ref, vec3_ref, len_ref, squares_ref, tri_ref, pick_ref, rule_ref) = refs[:14]
+    (f_qkv, f_out, f_up, f_down, ada_ref, h_ref, kept_ref, out32_ref, q_ref, k_ref, kt_ref, vt_ref, low_ref) = refs[14:27]
+    (x_ref, smooth_ref, flags_ref, hot_ref, silu_ref, proj_ref, one_ref, two_ref, pre_ref, act_ref) = refs[27:37]
+    (w_ref, send_ref, got_ref, back_send, back_got, v_ref, s_ref, load_sem) = refs[37:45]
+    (w_ada, silu_own, theirs, ours, ada_in, edge, edge_left, edge_right, wo_ref, wu_ref) = refs[45:55]
+    sems = refs[55:]
     first_flow = Gather([s_qkv], [f_qkv], sems[:5], pieces_of([s_qkv], (2,)))
     flow = Gather([s_out, s_up, s_down], [f_out, f_up, f_down], sems[5:10], pieces_of([s_out, s_up, s_down], (1, 2, 2)))
     ada_send, ada_recv = sems[10:12]
     there = Exchange(send_ref, got_ref, sems[12:14])
     home = Exchange(back_send, back_got, sems[14:16])
+    ada_sem, sib_s, sib_r, edge_s, edge_r, wo_sem, wu_sem = sems[16:23]
     core, z, yx = place()
     wide = z * 4 + yx
+    sib = (1 - core, wide)
     tokens, width = x_ref.shape
     half = width // 2
     mid = tokens // 2
     two = 2 * tokens
+    group_len = q_ref.shape[0]
     f32, low = jnp.float32, jnp.bfloat16
-    entry_barrier([(core, wide ^ r) for r in range(1, 16)] + [(1 - core, wide)])
+    vec_ref = vec3_ref.at[1]
+    entry_barrier([(core, wide ^ r) for r in range(1, 16)] + [sib])
+
+    def to_sib(slot, src, dst):
+        copy = pltpu.make_async_remote_copy(
+            src_ref=src, dst_ref=dst, send_sem=sib_s.at[slot], recv_sem=sib_r.at[slot], device_id=sib, device_id_type=MESH_ID
+        )
+        copy.start()
+        return copy
 
     first_flow.run(0)
+    ada_copy = pltpu.make_async_copy(ada_any.at[1], w_ada, ada_sem)
+    ada_copy.start()
+    cond = cond_ref[...]
+    silu = (cond / (1.0 + jnp.exp(-cond))).astype(low).astype(f32)
+    silu_own[...] = jnp.zeros_like(silu_own)
+    silu_own[0:slots, :] = silu
+    their_half = pl.ds(pl.multiple_of((1 - core) * half, half), half)
+    my_half = pl.ds(pl.multiple_of(core * half, half), half)
+    silu_copy = to_sib(0, silu_own.at[:, their_half], silu_ref.at[core])
+    silu_ref[core] = silu_own[:, my_half]
+    spot = lane_iota((32, LANES))
+    cells = map_ref[...]
+    edge[...] = jnp.where(spot == 0, cells[:, 0:1], jnp.where(spot == 1, cells[:, tokens - 1 : tokens], 0.0))
+
+    def edge_copy(slot, dst, shift):
+        return pltpu.make_async_remote_copy(
+            src_ref=edge,
+            dst_ref=dst,
+            send_sem=edge_s.at[slot],
+            recv_sem=edge_r.at[slot],
+            device_id=(core, lax.rem(wide + shift, 16)),
+            device_id_type=MESH_ID,
+        )
+
+    edges = [edge_copy(0, edge_left, 1), edge_copy(1, edge_right, 15)]
+    for copy in edges:
+        copy.start()
+    first_flow.run(1)
+
+    run_lane = lane_iota((1, LANES))
+    run_slot = lax.rem(run_lane - HALF_LANES + slots * LANES, slots)
+    lens = jnp.zeros((1, LANES), jnp.int32)
+    for j in range(slots):
+        lens = jnp.where(run_slot == j, len_ref[0:1, j : j + 1], lens)
+    counts = jnp.where(lens == LONG_TOTAL, squares_ref[0:1, :], jnp.where(lens == SHORT_TOTAL, squares_ref[1:2, :], 0.0))
+    unused = group_len - jnp.sum(counts, axis=1, keepdims=True)
+    counts = jnp.where(run_lane == HALF_LANES + slots * LEVELS, unused, counts)
+    ends = exact(jnp.broadcast_to(counts, (8, LANES)), tri_ref[...])[0:1, :]
+    starts = ends - counts
+    start_col, end_col = column_of(starts), column_of(ends)
+    here = (wide * tokens + lane_iota((1, tokens))).astype(f32)
+    left = 1.0 - jnp.sum(((here == start_col) & (here < end_col)).astype(f32), axis=0, keepdims=True)
+    right = 1.0 - jnp.sum(((here == end_col - 1.0) & (here >= start_col)).astype(f32), axis=0, keepdims=True)
+    flags_ref[...] = jnp.zeros_like(flags_ref)
+    flags_ref[0:1, :] = left
+    flags_ref[1:2, :] = right
+    row_at = (wide * tokens + lax.broadcasted_iota(jnp.int32, (tokens, LANES), 0)).astype(f32)
+    my_runs = ((row_at >= starts) & (row_at < ends)).astype(low)
+    hot = nn(my_runs, pick_ref[...])[:, 0:8]
+    hot_ref[...] = hot
+
+    ada_copy.wait()
+    w_low = w_ada[...].astype(low)
+    silu_copy.wait_recv()
+    theirs[...] = nn(silu_ref[1 - core].astype(low), w_low)
+    part_copy = to_sib(1, theirs, ours)
+    mine = nn(silu_ref[core].astype(low), w_low)
+    first_flow.run(2)
+
+    for copy in edges:
+        copy.wait_recv()
+    column = lane_iota((32, tokens))
+    before = jnp.where(column == 0, edge_left[:, 1:2], jnp.roll(cells, 1, axis=1))
+    after = jnp.where(column == tokens - 1, edge_right[:, 0:1], jnp.roll(cells, -1, axis=1))
+    smooth = smooth_map(cells, left, right, before, after)
+    smooth_ref[...] = smooth
+    x = exact(smooth, embed_ref[1], (0, 0)) + vec_ref[6:7, :]
+    x_ref[...] = x
+    part_copy.wait_recv()
+    ada_in[...] = mine + ours[...]
     ada_copies = []
     for r in range(1, 16):
         copy = pltpu.make_async_remote_copy(
@@ -804,29 +909,32 @@
         copy.start()
         ada_copies.append(copy)
     ada_ref[wide] = ada_in[...]
-    first_flow.run(1)
-    x = x_ref[...]
-    centred = x - jnp.mean(x, axis=1, keepdims=True)
-    unit = centred * lax.rsqrt(jnp.mean(centred * centred, axis=1, keepdims=True) + NORM_EPS)
-    first_flow.run(2)
+
+    def standard(values):
+        centred = values - jnp.mean(values, axis=1, keepdims=True)
+        return centred * lax.rsqrt(jnp.mean(centred * centred, axis=1, keepdims=True) + NORM_EPS)
+
+    unit = standard(x)
+    first_flow.run(3)
     for copy in ada_copies:
         copy.wait_recv()
     ada = jnp.concatenate([ada_ref[w] for w in range(16)], axis=1)
 
     def of_tokens(block):
-        rows = ada[:, block * width : (block + 1) * width] + vec_ref[block : block + 1, :]
-        return lax.dot_general(
-            one_hot_ref[...],
-            rows,
-            (((1,), (0,)), ((), ())),
-            precision=HIGHEST_PRECISION,
-            preferred_element_type=f32,
-        )
+        return exact(hot, ada[:, block * width : (block + 1) * width] + vec_ref[block : block + 1, :])
 
     h_ref[...] = (unit * (1.0 + of_tokens(2)) + of_tokens(4)).astype(low)
-    for t in range(3, first_flow.steps()):
+    for t in range(4, first_flow.steps()):
         first_flow.run(t)
-    flow.run(0)
+    next_tick = [0]
+
+    def tick(n):
+        for _ in range(n):
+            if next_tick[0] < flow.steps():
+                flow.run(next_tick[0])
+                next_tick[0] += 1
+
+    tick(1)
     first_flow.landed()
 
     group = 256
@@ -857,8 +965,11 @@
             return nt(h_ref[:, :half], w_ref[j, 0, part]) + nt(h_ref[:, half:], w_ref[j, 1, part])
 
         q_all, k_all, v_all = (project(part) for part in range(3))
-        kept_ref[:, pl.ds(first, group)] = q_all
-        kept_ref[:, pl.ds(pl.multiple_of(first + width, group), group)] = k_all
+        for pair in range(group // LANES):
+            cols = slice(pair * LANES, (pair + 1) * LANES)
+            at = g * (group // LANES) + pair
+            kept_ref[at] = q_all[:, cols]
+            kept_ref[at + width // LANES] = k_all[:, cols]
         q_all = q_all * lax.rsqrt(head_sums(q_all * q_all) + NORM_EPS)
         q_all = q_all * (8.0 * (1.0 + vec_ref[7:8, pl.ds(first, group)]))
         k_all = k_all * lax.rsqrt(head_sums(k_all * k_all) + NORM_EPS)
@@ -873,8 +984,7 @@
             send_ref[head + 1, tokens:, :] = jnp.where(lane_mid < HALF_LANES, swap_halves(v_a), v_b).astype(low)
         for e in range(4):
             there.push(g * 4 + e)
-        if j == 1:
-            flow.run(1)
+        tick((0, 1, 0, 0)[j])
 
     lane_two = lane_iota((two, LANES))
 
@@ -883,8 +993,8 @@
             there.wait(2 * pair + e)
         first = pl.multiple_of(pair * two, two)
         qk = jnp.concatenate([got_ref[2 * pair + e, 0:tokens, :].astype(f32) for e in range(2)], axis=0)
-        spot = first + lax.broadcasted_iota(jnp.int32, (two, LANES), 0)
-        runs = ((spot >= starts_ref[...]) & (spot < ends_ref[...])).astype(f32)
+        spot = (first + lax.broadcasted_iota(jnp.int32, (two, LANES), 0)).astype(f32)
+        runs = ((spot >= starts) & (spot < ends)).astype(f32)
         barred = nn(runs.astype(low), rule_ref[...])
         rows = pl.ds(first, two)
         q_ref[rows, :] = jnp.where(lane_two < HALF_LANES, qk, barred).astype(low)
@@ -952,23 +1062,25 @@
         home.push(w)
         return carry
 
-    lax.fori_loop(0, 4, unpack, 0)
-    flow.run(2)
-    lax.fori_loop(4, 8, unpack, 0)
-    flow.run(3)
+    for i in range(4):
+        lax.fori_loop(2 * i, 2 * i + 2, unpack, 0)
+        tick((0, 1, 0, 1)[i])
     plane = 4 * tokens // ROWS
-    t = 4
+    done = 0
     for p in range(4):
         for first, last, limit in groups:
             begin, end = max(first, p * plane), min(last, (p + 1) * plane)
             if begin < end:
                 lax.fori_loop(begin, end, functools.partial(query_block, limit), 0)
+                tick((0, 1, 0, 1, 0, 1, 0, 1)[done])
+                done += 1
         lax.fori_loop(4 * p, 4 * p + 4, give_back, 0)
-        if p and t < flow.steps():
-            flow.run(t)
-            t += 1
-    for i in range(t, flow.steps()):
-        flow.run(i)
+    tick(1)
+    while next_tick[0] < 8:
+        tick(1)
+    flow.landed((0,))
+    wo_copy = pltpu.make_async_copy(f_out, wo_ref, wo_sem)
+    wo_copy.start()
     for pair in range(8):
         home.wait(2 * pair)
         home.wait(2 * pair + 1)
@@ -976,32 +1088,78 @@
         even, odd = back_got[2 * pair].astype(f32), back_got[2 * pair + 1].astype(f32)
         low_ref[0:mid, cols] = jnp.where(lane_mid < HALF_LANES, even, swap_halves(odd)).astype(low)
         low_ref[mid:, cols] = jnp.where(lane_mid < HALF_LANES, swap_halves(even), odd).astype(low)
-    flow.landed()
+
+    wo_copy.wait()
+    proj = nt(low_ref[:, :half], wo_ref[0]) + nt(low_ref[:, half:], wo_ref[1])
+    proj_ref[...] = proj
+    x_one = x_ref[...] + of_tokens(0) * proj
+    one_ref[...] = x_one
+    two_ref[...] = (standard(x_one) * (1.0 + of_tokens(3)) + of_tokens(5)).astype(low)
+    flow.landed((1, 2))
+    step = 512
+    hidden = pre_ref.shape[1]
+
+    def load_up(c):
+        rows = pl.ds(pl.multiple_of(c * step, step), step)
+        slot = lax.rem(c, 2)
+        return pltpu.make_async_copy(f_up.at[:, rows], wu_ref.at[slot], wu_sem.at[slot])
+
+    load_up(0).start()
+
+    def up_step(c, carry):
+        pl.when(c + 1 < hidden // step)(lambda: load_up(c + 1).start())
+        load_up(c).wait()
+        w = wu_ref.at[lax.rem(c, 2)]
+        pre = nt(two_ref[:, :half], w[0]) + nt(two_ref[:, half:], w[1])
+        cols = pl.ds(pl.multiple_of(c * step, step), step)
+        pre_ref[:, cols] = pre
+        act_ref[:, cols] = gelu(pre).astype(low)
+        return carry
+
+    for i in range(2):
+        lax.fori_loop(4 * i, 4 * i + 4, up_step, 0)
+        tick(1)
+    tick(flow.steps())
+    flow.landed(range(3, 5))
     first_flow.finish()
     flow.finish()
     there.finish()
     home.finish()
-    for copy in ada_copies:
+    for copy in ada_copies + edges + [silu_copy, part_copy]:
         copy.wait_send()
 
 
-def front(shards, ada_block, x_zero, one_hot, vectors, starts, ends, rule, groups):
-    tokens, width = x_zero.shape
+def front(shards, condition, ada_state, cells, embed_state, vector_state, lengths, tables, groups):
+    width = condition.shape[1]
+    tokens = cells.shape[1]
+    slots = lengths.shape[1]
     group_len = 16 * tokens
+    hidden = 16 * shards[2].shape[0]
     f32, low = jnp.float32, jnp.bfloat16
     dma = pltpu.SemaphoreType.DMA
     shape = jax.ShapeDtypeStruct
+    ada_width = ada_state.shape[2]
     fulls = [shape((2, 16 * s.shape[0], s.shape[1]), low) for s in shards]
     outs = fulls + [
-        shape((16,) + ada_block.shape, f32),
+        shape((16, 8, ada_width), f32),
         shape((tokens, width), low),
-        shape((tokens, 2 * width), f32),
+        shape((2 * width // LANES, tokens, LANES), f32),
         shape((group_len, LANES), f32),
         shape((group_len, LANES), low),
         shape((group_len, LANES), low),
         shape((LANES, group_len), low),
         shape((LANES, group_len), low),
         shape((tokens, width), low),
+        shape((tokens, width), f32),
+        shape(cells.shape, f32),
+        shape((8, tokens), f32),
+        shape((tokens, 8), f32),
+        shape((2, 8, width // 2), f32),
+        shape((tokens, width), f32),
+        shape((tokens, width), f32),
+        shape((tokens, width), low),
+        shape((tokens, hidden), f32),
+        shape((tokens, hidden), low),
     ]
     packed, mid = tokens * 3 // 2, tokens // 2
     scratch = [
@@ -1013,18 +1171,29 @@
         pltpu.VMEM((group_len, LANES), low),
         pltpu.VMEM((ROWS, group_len), f32),
         dma((4, 2, 3)),
+        pltpu.VMEM(ada_state.shape[1:], f32),
+        pltpu.VMEM((8, width), f32),
+        pltpu.VMEM((8, ada_width), f32),
+        pltpu.VMEM((8, ada_width), f32),
+        pltpu.VMEM((8, ada_width), f32),
+        pltpu.VMEM((32, LANES), f32),
+        pltpu.VMEM((32, LANES), f32),
+        pltpu.VMEM((32, LANES), f32),
+        pltpu.VMEM((2, width, width // 2), low),
+        pltpu.VMEM((2, 2, 512, width // 2), low),
     ]
     scratch += Gather.scratch(2) + Gather.scratch(5) + [dma((16,)) for _ in range(6)]
+    scratch += [dma, dma((2,)), dma((2,)), dma((2,)), dma((2,)), dma, dma((2,))]
     return pl.pallas_call(
-        functools.partial(front_kernel, groups),
+        functools.partial(front_kernel, groups, slots),
         out_shape=outs,
-        in_specs=[ANY] * 4 + [VM] * 7,
-        out_specs=[ANY] * 4 + [VM] * 9,
+        in_specs=[ANY] * 4 + [VM, ANY] + [VM] * 8,
+        out_specs=[ANY] * 4 + [VM] * 19,
         scratch_shapes=scratch,
         compiler_params=pltpu.CompilerParams(
             collective_id=0, has_side_effects=True, vmem_limit_bytes=VMEM_BYTES
         ),
-    )(*shards, ada_block, x_zero, one_hot, vectors, starts, ends, rule)
+    )(*shards, condition, ada_state, cells, embed_state, vector_state, lengths, *tables)
 
 
 class Scatter:
@@ -1033,6 +1202,7 @@
     def __init__(self, parts, outs, bufs, sems, pieces):
         self.parts, self.outs, self.bufs, self.pieces = parts, outs, bufs, pieces
         self.send, self.recv = sems
+        self.parts_left = {}
         core, z, yx = place()
         self.z, self.yx = z, yx
         self.x_dev, self.y_dev = at_dev(core, z, yx ^ 1), at_dev(core, z, yx ^ 2)
@@ -1098,7 +1268,7 @@
                 self.push(p, 2, part.at[lo2, yx ^ 1, rows], view("rx", lo2), self.x_dev),
                 self.push(p, 3, part.at[hi2, yx ^ 2, rows], view("ry", hi2), self.y_dev),
             ]
-            self.ends += [copy.wait_send for copy in copies]
+            self.parts_left[p] = [copy.wait_send for copy in copies]
         elif s == 1:
             turn = view("turn_x", lo2)
             self.arrive(p, 0, turn)
@@ -1173,7 +1343,13 @@
             if 0 <= t - s < len(self.pieces):
                 self.stage(t - s, s)
 
+    def sent(self, p):
+        for end in self.parts_left.pop(p, ()):
+            end()
+
     def finish(self):
+        for p in list(self.parts_left):
+            self.sent(p)
         for end in self.ends:
             end()
 
@@ -1181,32 +1357,59 @@
 COMMON_ROWS = 48
 
 
+def standard_of(values):
+    centred = values - jnp.mean(values, axis=1, keepdims=True)
+    rstd = lax.rsqrt(jnp.mean(centred * centred, axis=1, keepdims=True) + NORM_EPS)
+    return centred * rstd, rstd
+
+
+def standard_back(unit, rstd, d_unit):
+    along = jnp.mean(d_unit * unit, axis=1, keepdims=True)
+    return rstd * (d_unit - jnp.mean(d_unit, axis=1, keepdims=True) - unit * along)
+
+
+def gelu_slope(values):
+    square = values * values
+    inner = jnp.tanh(GELU_SCALE * (values + GELU_CUBE * values * square))
+    slope = GELU_SCALE * (1.0 + 3.0 * GELU_CUBE * square)
+    return 0.5 * (1.0 + inner) + 0.5 * values * (1.0 - inner * inner) * slope
+
+
 def back_kernel(groups, splits, *refs):
     (
-        d_att, out32_ref, q_ref, k_ref, kt_ref, vt_ref, kept_ref, vec_ref, h_ref, w_any,
-        p_down, p_up, p_out, x_ref, scale_ref, dx_one, hot_ref, g_one, g_two, g_scale, g_shift,
-        smooth_ref, embed_ref, mass_ref, ok_ref,
-    ) = refs[:25]
-    (o_down, o_up, o_out, o_qkv, ada_both, common_all, bias_all, map_ref) = refs[25:33]
+        cot_ref, hot_ref, ada_in, vec3_ref, x_ref, one_ref, proj_ref, h_any, two_any, low_any, act_any, pre_any,
+        w_any, wo_any, wu_any, wd_any, book_any, out32_any, q_ref, k_ref, kt_ref, vt_ref, kept_any,
+        smooth_ref, embed_ref, ok_ref,
+    ) = refs[:26]
+    (o_down, o_up, o_out, o_qkv, ada_both, common_all, bias_all, map_ref, block_ref) = refs[26:35]
     (
         send_ref, got_ref, back_send, back_got, g_ref, gt_ref, qt_ref, dq_ref, dkt_ref, dvt_ref,
-        w_ref, dproj, h_both, p_qkv, dh_ref, ada_ref, com_ref, ada_land, com_land, ada_sum, com_sum, ada_sib, com_sib,
+        w_buf, dhid, h_both, dh_ref, ada_ref, com_ref, ada_land, com_land, ada_sum, com_sum, ada_sib, com_sib,
         bias_own, com_own, edge, edge_left, edge_right,
-    ) = refs[33:61]
-    rest = refs[61:]
+        act_half, dmlp, two_half, low_half, dattn, mlp_ref, dx_one, act_buf, pre_buf, d_att, p_down, p_up, p_out,
+    ) = refs[35:75]
+    rest = refs[75:]
     flow_bufs, rest = rest[:18], rest[18:]
     flow_sems, rest = rest[:2], rest[2:]
     last_bufs, rest = rest[:6], rest[6:]
     last_sems, rest = rest[:2], rest[2:]
-    (ex_s, ex_r, home_s, home_r, w_sem, sib_s, sib_r, small_s, small_r, spread_s, spread_r, edge_s, edge_r) = rest
+    (
+        ex_s, ex_r, home_s, home_r, w_sem, sib_s, sib_r, small_s, small_r, spread_s, spread_r, edge_s, edge_r,
+        hid_s, hid_r, half_sem, kept_sem, free_sem,
+    ) = rest
     core, z, yx = place()
     wide = z * 4 + yx
     sib = (1 - core, wide)
     f32, low = jnp.float32, jnp.bfloat16
-    tokens, width = h_ref.shape
+    tokens, width = x_ref.shape
     half = width // 2
+    hidden = dhid.shape[2]
     mid = tokens // 2
     two = 2 * tokens
+    step = 512
+    vec_ref = vec3_ref.at[1]
+    dproj = dhid.at[:, :, pl.ds(0, 3 * width)]
+    p_qkv = p_up.at[:, :, pl.ds(0, tokens)]
     flow = Scatter([p_down, p_up, p_out], [o_down, o_up, o_out], flow_bufs, flow_sems, splits[0])
     last = Scatter([p_qkv], [o_qkv], last_bufs, last_sems, splits[1])
     there = Exchange(back_send, back_got, (ex_s, ex_r))
@@ -1220,9 +1423,146 @@
         copy.start()
         return copy
 
+    next_tick = [0]
+
+    def tick(n):
+        for _ in range(n):
+            if next_tick[0] < flow.steps():
+                flow.run(next_tick[0])
+                next_tick[0] += 1
+
     lane = lane_iota((two, LANES))
     lane_tok = lane_iota((tokens, LANES))
     lane_mid = lane_iota((mid, LANES))
+
+    def load_chunk(c):
+        slot = lax.rem(c, 2)
+        cols = pl.ds(pl.multiple_of(c * step, step), step)
+        down_cols = pl.ds(pl.multiple_of(lax.rem(c, hidden // 2 // step) * step, step), step)
+        down = wd_any.at[c // (hidden // 2 // step)]
+        pairs = [
+            (down.at[pl.ds(0, half), down_cols], w_buf.at[slot, 0]),
+            (down.at[pl.ds(half, half), down_cols], w_buf.at[slot, 1]),
+            (wu_any.at[0, cols], w_buf.at[slot, 2]),
+            (wu_any.at[1, cols], w_buf.at[slot, 3]),
+            (act_any.at[:, cols], act_buf.at[slot]),
+            (pre_any.at[:, cols], pre_buf.at[slot]),
+        ]
+        return [pltpu.make_async_copy(src, dst, w_sem.at[slot, i]) for i, (src, dst) in enumerate(pairs)]
+
+    def start_chunk(c):
+        for copy in load_chunk(c):
+            copy.start()
+
+    start_chunk(0)
+    out32_copy = pltpu.make_async_copy(out32_any, dq_ref, kept_sem)
+    out32_copy.start()
+    theirs = pl.ds(pl.multiple_of((1 - core) * half, half), half)
+    mine = pl.ds(pl.multiple_of(core * half, half), half)
+    hid_half = hidden // 2
+    hid_theirs = pl.ds(pl.multiple_of((1 - core) * hid_half, hid_half), hid_half)
+    hid_mine = pl.ds(pl.multiple_of(core * hid_half, hid_half), hid_half)
+    ada = jnp.concatenate([ada_in[w] for w in range(16)], axis=1)
+    hot = hot_ref[...]
+
+    def of_tokens(block):
+        return exact(hot, ada[:, block * width : (block + 1) * width] + vec_ref[block : block + 1, :])
+
+    live = jnp.sum(hot, axis=1, keepdims=True)
+    gate_two = of_tokens(1)
+    dmlp[core] = (gate_two * (cot_ref[...].astype(f32) * live)).astype(low)
+    sib_copies = [
+        to_sib(0, dmlp.at[core], dmlp.at[core]),
+        to_sib(1, act_any.at[:, hid_theirs], act_half.at[core]),
+        to_sib(2, two_any.at[:, theirs], two_half.at[core]),
+        to_sib(3, low_any.at[:, theirs], low_half.at[core]),
+        to_sib(4, h_any.at[:, theirs], h_both.at[core]),
+    ]
+    half_copies = [
+        pltpu.make_async_copy(src, dst.at[core], half_sem.at[i])
+        for i, (src, dst) in enumerate(
+            [
+                (act_any.at[:, hid_mine], act_half),
+                (two_any.at[:, mine], two_half),
+                (low_any.at[:, mine], low_half),
+                (h_any.at[:, mine], h_both),
+            ]
+        )
+    ]
+    for copy in half_copies:
+        copy.start()
+    mlp_ref[...] = jnp.zeros_like(mlp_ref)
+    dh_ref[...] = jnp.zeros_like(dh_ref)
+
+    def hid_copy(c):
+        cols = pl.ds(pl.multiple_of(c * step, step), step)
+        return pltpu.make_async_remote_copy(
+            src_ref=dhid.at[core, :, cols],
+            dst_ref=dhid.at[core, :, cols],
+            send_sem=hid_s.at[c],
+            recv_sem=hid_r.at[c],
+            device_id=sib,
+            device_id_type=MESH_ID,
+        )
+
+    def hidden_step(c, carry):
+        pl.when(c + 1 < hidden // step)(lambda: start_chunk(c + 1))
+        for copy in load_chunk(c):
+            copy.wait()
+        slot = lax.rem(c, 2)
+        w = w_buf.at[slot]
+        d_out = dmlp.at[core]
+        d_act = nn(d_out[:, :half], w[0]) + nn(d_out[:, half:], w[1])
+        d_hid = (d_act * gelu_slope(pre_buf[slot])).astype(low)
+        dhid[core, :, pl.ds(pl.multiple_of(c * step, step), step)] = d_hid
+        hid_copy(c).start()
+        act = act_buf[slot]
+        mlp_ref[:, :half] += nt(act, w[0])
+        mlp_ref[:, half:] += nt(act, w[1])
+        dh_ref[:, :half] += nn(d_hid, w[2])
+        dh_ref[:, half:] += nn(d_hid, w[3])
+        return carry
+
+    chunks = hidden // step
+    lax.fori_loop(0, 3, hidden_step, 0)
+    sib_copies[0].wait_recv()
+    sib_copies[1].wait_recv()
+    half_copies[0].wait()
+
+    def gradient(grads, inputs, out, rows, shard, lanes):
+        def body(c, carry):
+            cols = pl.ds(pl.multiple_of(c * rows, LANES), rows)
+            total = nn(grads[0, :, cols].astype(f32).T.astype(low), inputs[0])
+            total = total + nn(grads[1, :, cols].astype(f32).T.astype(low), inputs[1])
+            count = rows // shard
+            out[c * count // 4, pl.ds(lax.rem(c * count, 4), count)] = total.astype(low).reshape(count, shard, lanes)
+            return carry
+
+        return body
+
+    lax.fori_loop(0, width // LANES, gradient(dmlp, act_half, p_down, LANES, width // 16, hid_half), 0)
+    tick(1)
+    lax.fori_loop(3, chunks, hidden_step, 0)
+    tick(1)
+
+    wo_copies = [
+        pltpu.make_async_copy(wo_any.at[c, pl.ds(r * half, half)], w_buf.at[0, 2 * c + r], w_sem.at[0, 2 * c + r])
+        for c in range(2)
+        for r in range(2)
+    ]
+    for copy in wo_copies:
+        copy.start()
+    unit, rstd = standard_of(one_ref[...])
+    g_two = cot_ref[...].astype(f32) * live
+    d_one = standard_back(unit, rstd, dh_ref[...] * (1.0 + of_tokens(3))) + g_two
+    dx_one[...] = d_one
+    dattn[core] = (of_tokens(0) * d_one).astype(low)
+    sib_copies.append(to_sib(5, dattn.at[core], dattn.at[core]))
+    for copy in wo_copies:
+        copy.wait()
+    for c in range(2):
+        part = nn(dattn[core, :, :half], w_buf[0, 2 * c]) + nn(dattn[core, :, half:], w_buf[0, 2 * c + 1])
+        d_att[:, c * half : (c + 1) * half] = part.astype(low)
 
     def pack(pair, carry):
         cols = pl.ds(pl.multiple_of(pair * LANES, LANES), LANES)
@@ -1234,19 +1574,29 @@
         return carry
 
     lax.fori_loop(0, 8, pack, 0)
-    slab = 3 * width // 4
-
-    def w_load(j):
-        rows = pl.ds(j * slab, slab)
-        return pltpu.make_async_copy(w_any.at[:, rows], w_ref.at[j % 2], w_sem.at[j % 2])
-
-    w_load(0).start()
-    w_load(1).start()
-    theirs = pl.ds(pl.multiple_of((1 - core) * half, half), half)
-    mine = pl.ds(pl.multiple_of(core * half, half), half)
-    h_copy = to_sib(0, h_ref.at[:, theirs], h_both.at[core])
-    h_both[core] = h_ref[:, mine]
-    flow.run(0)
+
+    def per_slot(values):
+        return exact(hot, values, (0, 0))
+
+    ada_ref[:, 3 * width : 4 * width] = per_slot(dh_ref[...] * unit)
+    ada_ref[:, 5 * width : 6 * width] = per_slot(dh_ref[...])
+    ada_ref[:, 0:width] = per_slot(d_one * proj_ref[...])
+    ada_ref[:, width : 2 * width] = per_slot(g_two * mlp_ref[...])
+    block_ref[...] = (live * (one_ref[...] + gate_two * mlp_ref[...])).astype(low)
+    for c in range(chunks):
+        hid_copy(c).wait_recv()
+    half_copies[1].wait()
+    sib_copies[2].wait_recv()
+    lax.fori_loop(0, hidden // 256, gradient(dhid, two_half, p_up, 256, hidden // 16, half), 0)
+    for c in range(chunks):
+        hid_copy(c).wait_send()
+    pl.semaphore_signal(free_sem, inc=1, device_id=sib, device_id_type=MESH_ID)
+    tick(1)
+    half_copies[2].wait()
+    sib_copies[3].wait_recv()
+    sib_copies[5].wait_recv()
+    lax.fori_loop(0, width // LANES, gradient(dattn, low_half, p_out, LANES, width // 16, half), 0)
+    tick(1)
     dkt_ref[...] = jnp.zeros_like(dkt_ref)
     dvt_ref[...] = jnp.zeros_like(dvt_ref)
 
@@ -1259,15 +1609,17 @@
             g = back_got[2 * pair + e].astype(f32)
             pieces += [g, swap_halves(g)]
         grad = jnp.where(lane < HALF_LANES, jnp.concatenate(pieces, axis=0), 0.0)
-        delta = jnp.sum(grad * out32_ref[rows, :], axis=1, keepdims=True)
+        delta = jnp.sum(grad * dq_ref[rows, :], axis=1, keepdims=True)
         grad = lanes_three(lane, HALF_LANES, -delta, grad)
         g_ref[rows, :] = grad.astype(low)
         gt_ref[:, rows] = grad.T[:HALF_LANES].astype(low)
         qt_ref[:, rows] = q_ref[rows, :].astype(f32).T[:HALF_LANES].astype(low)
         return carry
 
-    lax.fori_loop(0, 8, unpack, 0)
-    flow.run(1)
+    out32_copy.wait()
+    for i in range(4):
+        lax.fori_loop(2 * i, 2 * i + 2, unpack, 0)
+        tick((0, 1, 0, 0)[i])
 
     def query_block(limit, b, carry):
         rows = pl.ds(pl.multiple_of(b * ROWS, ROWS), ROWS)
@@ -1293,14 +1645,10 @@
         dq_ref[rows, :] = acc
         return carry
 
-    t = 2
     for first, stop, limit in groups:
-        for begin in range(first, stop, 2):
-            end = min(begin + 2, stop)
-            lax.fori_loop(begin, end, functools.partial(query_block, limit), 0)
-            if begin >= 3 and t < flow.steps():
-                flow.run(t)
-                t += 1
+        for b in range(first, stop):
+            lax.fori_loop(b, b + 1, functools.partial(query_block, limit), 0)
+            tick((0, 0, 0, 1, 0, 1, 0, 1, 0, 1, 0, 0)[b])
 
     def send_out(pair, carry):
         rows = pl.ds(pl.multiple_of(pair * two, two), two)
@@ -1316,27 +1664,59 @@
 
     lax.fori_loop(0, 8, send_out, 0)
 
-    def per_slot(values):
-        return lax.dot_general(
-            hot_ref[...],
-            values,
-            (((1,), (0,)), ((), ())),
-            precision=HIGHEST_PRECISION,
-            preferred_element_type=f32,
-        )
-
-    for block, ref in ((0, g_one), (1, g_two), (3, g_scale), (5, g_shift)):
-        ada_ref[:, block * width : (block + 1) * width] = per_slot(ref[...])
-    while t < flow.steps() - 2:
-        flow.run(t)
-        t += 1
+    kept_copy = pltpu.make_async_copy(kept_any, dq_ref, kept_sem)
+    kept_copy.start()
+    tick(1)
+    com_ref[...] = jnp.zeros_like(com_ref)
+
+    def load_codes(c):
+        slot = lax.rem(c, 2)
+        rows = pl.ds(pl.multiple_of(lax.rem(c, chunks) * step, step), step)
+        return [
+            pltpu.make_async_copy(book_any.at[rows, pl.ds(r * half, half)], w_buf.at[slot, r], w_sem.at[slot, r])
+            for r in range(2)
+        ]
+
+    def start_codes(c):
+        for copy in load_codes(c):
+            copy.start()
+
+    start_codes(0)
+
+    def logits_of(c):
+        pl.when(c + 1 < 2 * chunks)(lambda: start_codes(c + 1))
+        for copy in load_codes(c):
+            copy.wait()
+        w = w_buf.at[lax.rem(c, 2)]
+        return nt(block_ref[:, :half], w[0]) + nt(block_ref[:, half:], w[1])
+
+    def sum_codes(c, carry):
+        top, total = carry
+        logits = logits_of(c)
+        new_top = jnp.maximum(top, jnp.max(logits, axis=1, keepdims=True))
+        return new_top, total * jnp.exp(top - new_top) + jnp.sum(jnp.exp(logits - new_top), axis=1, keepdims=True)
+
+    start = (jnp.full((tokens, 1), -3e38, f32), jnp.zeros((tokens, 1), f32))
+    top, total = lax.fori_loop(0, chunks, sum_codes, start)
+    share_of = live / total
+    for c in range(chunks):
+        mass = jnp.sum(jnp.exp(logits_of(chunks + c) - top) * share_of, axis=0, keepdims=True)
+        com_ref[34 + c // 2 : 35 + c // 2, (c % 2) * step : (c % 2 + 1) * step] = mass
+    slabs = 3 * width // step
+
+    def load_w(j):
+        rows = pl.ds(j * step, step)
+        return [pltpu.make_async_copy(w_any.at[c, rows], w_buf.at[j % 2, c], w_sem.at[j % 2, c]) for c in range(2)]
+
+    for j in range(2):
+        for copy in load_w(j):
+            copy.start()
+    kept_copy.wait()
 
     def unnormalize(values, grad):
         inverse = lax.rsqrt(head_sums(values * values) + NORM_EPS)
         unit = values * inverse
         return inverse * (grad - unit * head_sums(unit * grad)), unit
-
-    com_ref[...] = jnp.zeros_like(com_ref)
 
     def heads_back(pair, carry):
         home.wait(2 * pair)
@@ -1353,24 +1733,28 @@
         dproj[core, 0:mid, val_cols] = jnp.where(lane_mid < HALF_LANES, even_v, swap_halves(odd_v)).astype(low)
         dproj[core, mid:, val_cols] = jnp.where(lane_mid < HALF_LANES, swap_halves(even_v), odd_v).astype(low)
         scaled = d_query * (8.0 * (1.0 + vec_ref[7:8, cols]))
-        d_q, unit = unnormalize(kept_ref[:, cols], scaled)
+        d_q, unit = unnormalize(dq_ref[pl.ds(pl.multiple_of(pair * tokens, tokens), tokens), :], scaled)
         com_ref[33:34, cols] = jnp.sum(d_query * unit, axis=0, keepdims=True) * 8.0
         dproj[core, :, cols] = d_q.astype(low)
-        dproj[core, :, key_cols] = unnormalize(kept_ref[:, key_cols], d_key)[0].astype(low)
+        dproj[core, :, key_cols] = unnormalize(dq_ref[pl.ds(pl.multiple_of((pair + 8) * tokens, tokens), tokens), :], d_key)[0].astype(low)
         return carry
 
     lax.fori_loop(0, 8, heads_back, 0)
-    d_copy = to_sib(1, dproj.at[core], dproj.at[core])
-
-    for j in range(4):
-        w_load(j).wait()
+    pl.semaphore_wait(free_sem, 1)
+    d_copy = to_sib(6, dproj.at[core], dproj.at[core])
+
+    for j in range(slabs):
+        for copy in load_w(j):
+            copy.wait()
         for c in range(2):
-            part = nn(dproj[core, :, j * slab : (j + 1) * slab], w_ref[j % 2, c])
+            part = nn(dproj[core, :, j * step : (j + 1) * step], w_buf[j % 2, c])
             cols = slice(c * half, (c + 1) * half)
             dh_ref[:, cols] = part if j == 0 else dh_ref[:, cols] + part
-        if j < 2:
-            w_load(j + 2).start()
-    h_copy.wait_recv()
+        if j + 2 < slabs:
+            for copy in load_w(j + 2):
+                copy.start()
+    half_copies[3].wait()
+    sib_copies[4].wait_recv()
     d_copy.wait_recv()
 
     def weight_grad(c, carry):
@@ -1380,32 +1764,23 @@
         p_qkv[c // 2, pl.ds(2 * (c % 2), 2)] = total.astype(low).reshape(2, tokens, half)
         return carry
 
+    assert next_tick[0] >= 6
+    for p in range(len(splits[0])):
+        flow.sent(p)
     lax.fori_loop(0, 8, weight_grad, 0)
     last.run(0)
-    while t < flow.steps():
-        flow.run(t)
-        t += 1
-
-    x = x_ref[...]
-    centred = x - jnp.mean(x, axis=1, keepdims=True)
-    rstd = lax.rsqrt(jnp.mean(centred * centred, axis=1, keepdims=True) + NORM_EPS)
-    unit = centred * rstd
+    tick(flow.steps())
+
+    unit, rstd = standard_of(x_ref[...])
     d_h = dh_ref[...]
     ada_ref[:, 2 * width : 3 * width] = per_slot(d_h * unit)
     ada_ref[:, 4 * width : 5 * width] = per_slot(d_h)
-    d_unit = d_h * (1.0 + scale_ref[...])
-    d_x = rstd * (
-        d_unit
-        - jnp.mean(d_unit, axis=1, keepdims=True)
-        - unit * jnp.mean(d_unit * unit, axis=1, keepdims=True)
-    )
-    d_x = d_x + dx_one[...]
+    d_x = standard_back(unit, rstd, d_h * (1.0 + of_tokens(2))) + dx_one[...]
     last.run(1)
     com_ref[0:32, :] = lax.dot_general(
         smooth_ref[...], d_x, (((1,), (0,)), ((), ())), precision=HIGHEST_PRECISION, preferred_element_type=f32
     )
     com_ref[32:33, :] = jnp.sum(d_x, axis=0, keepdims=True)
-    com_ref[34:38, :] = mass_ref[...]
     small = []
     quarter = COMMON_ROWS // 2
 
@@ -1434,7 +1809,7 @@
         small.append(spread(small_s, small_r, r, 0, ada_part(ada_ref, wide ^ r), ada_land.at[r]))
         small.append(spread(small_s, small_r, r, 1, common_part(com_ref, wide ^ r), com_land.at[r]))
     d_smooth = lax.dot_general(
-        embed_ref[...], d_x, (((1,), (1,)), ((), ())), precision=HIGHEST_PRECISION, preferred_element_type=f32
+        embed_ref[1], d_x, (((1,), (1,)), ((), ())), precision=HIGHEST_PRECISION, preferred_element_type=f32
     )
     left, right = ok_ref[0:1, :], ok_ref[1:2, :]
     share = d_smooth / (2.0 + left + right)
@@ -1461,7 +1836,7 @@
         com_total = com_total + com_land[r]
     ada_sum[...] = ada_total
     com_sum[...] = com_total
-    swaps = [to_sib(2, ada_sum, ada_sib), to_sib(3, com_sum, com_sib)]
+    swaps = [to_sib(7, ada_sum, ada_sib), to_sib(8, com_sum, com_sib)]
     last.run(3)
     for copy in swaps:
         copy.wait_recv()
@@ -1488,7 +1863,7 @@
     map_ref[...] = 2.0 * share + left * before + right * after
     for copy in back:
         copy.wait_recv()
-    for copy in small + swaps + back + [h_copy, d_copy, to_right, to_left]:
+    for copy in small + swaps + back + sib_copies + [d_copy, to_right, to_left]:
         copy.wait_send()
     flow.finish()
     last.finish()
@@ -1497,16 +1872,15 @@
 
 
 def back(args, groups, splits, call_id):
-    d_att, out32 = args[0], args[1]
-    tokens, width = d_att.shape
+    x_zero, act = args[4], args[10]
+    tokens, width = x_zero.shape
+    hidden = act.shape[1]
     group_len = 16 * tokens
     half, mid, packed = width // 2, tokens // 2, tokens * 3 // 2
     f32, low = jnp.float32, jnp.bfloat16
     dma = pltpu.SemaphoreType.DMA
     shape = jax.ShapeDtypeStruct
-    parts = args[10:13]
-    sizes = [p.shape[2:] for p in parts] + [(3 * width // 16, half)]
-    counts = [p.shape[2] for p in parts]
+    sizes = [(width // 16, hidden // 2), (hidden // 16, half), (width // 16, half), (3 * width // 16, half)]
     first = pieces_of([shape(s, f32) for s in sizes[:3]], splits[0])
     second = pieces_of([shape(sizes[3], f32)], splits[1])
     ada_width, quarter = 6 * width // 16, COMMON_ROWS // 2
@@ -1515,6 +1889,7 @@
         shape((COMMON_ROWS, width), f32),
         shape((8, 6 * width), f32),
         shape((32, tokens), f32),
+        shape((tokens, width), low),
     ]
     vm = pltpu.VMEM
     scratch = [
@@ -1528,10 +1903,9 @@
         vm((group_len, LANES), f32),
         vm((HALF_LANES, group_len), f32),
         vm((HALF_LANES, group_len), f32),
-        vm((2, 2, 3 * width // 4, half), low),
-        vm((2, tokens, 3 * width), low),
+        vm((2, 4, 512, half), low),
+        vm((2, tokens, hidden), low),
         vm((2, tokens, half), low),
-        vm((4, 4) + sizes[3], low),
         vm((tokens, width), f32),
         vm((8, 6 * width), f32),
         vm((COMMON_ROWS, width), f32),
@@ -1546,36 +1920,43 @@
         vm((32, LANES), f32),
         vm((32, LANES), f32),
         vm((32, LANES), f32),
-    ]
+        vm((2, tokens, hidden // 2), low),
+        vm((2, tokens, width), low),
+        vm((2, tokens, half), low),
+        vm((2, tokens, half), low),
+        vm((2, tokens, width), low),
+        vm((tokens, width), f32),
+        vm((tokens, width), f32),
+        vm((2, tokens, 512), low),
+        vm((2, tokens, 512), f32),
+        vm((tokens, width), low),
+    ] + [vm((4, 4) + s, low) for s in sizes[:3]]
     scratch += Scatter.scratch(sizes[:3], len(first)) + Scatter.scratch(sizes[3:], len(second))
-    scratch += [dma((16,)) for _ in range(4)] + [dma((2,)), dma((4,)), dma((4,))]
+    scratch += [dma((16,)) for _ in range(4)] + [dma((2, 6)), dma((16,)), dma((16,))]
     scratch += [dma((2, 16)) for _ in range(4)] + [dma((2,)), dma((2,))]
+    scratch += [dma((8,)), dma((8,)), dma((4,)), dma, pltpu.SemaphoreType.REGULAR]
     return pl.pallas_call(
         functools.partial(back_kernel, groups, (first, second)),
         out_shape=outs,
-        in_specs=[VM] * 9 + [ANY] + [VM] * 15,
-        out_specs=[VM] * 8,
+        in_specs=[VM] * 7 + [ANY] * 11 + [VM] * 4 + [ANY] + [VM] * 3,
+        out_specs=[VM] * 9,
         scratch_shapes=scratch,
         compiler_params=pltpu.CompilerParams(
-            collective_id=call_id, has_side_effects=True, vmem_limit_bytes=60 * 1024 * 1024
+            collective_id=call_id, has_side_effects=True, vmem_limit_bytes=63 * 1024 * 1024
         ),
     )(*args)
 
 
-def run_bounds(lengths, group_len):
-    short_sq = jnp.array([side * side for side in SHORT_SIDES], jnp.int32)
-    long_sq = jnp.array([side * side for side in LONG_SIDES], jnp.int32)
-    counts = jnp.where(
-        lengths[None, :] == sum(side * side for side in LONG_SIDES),
-        long_sq[:, None],
-        jnp.where(lengths[None, :] == sum(side * side for side in SHORT_SIDES), short_sq[:, None], 0),
-    ).reshape(-1)
-    ends = jnp.cumsum(counts)
-    starts = ends - counts
-    pad = lambda v, last: jnp.concatenate([v, last])
-    ends = pad(ends, jnp.full((1,), group_len, jnp.int32))
-    starts = pad(starts, ends[-2:-1])
-    return starts, ends
+def run_tables(slots):
+    squares = np.zeros((8, LANES), np.float32)
+    pick = np.zeros((LANES, LANES), np.float32)
+    for run in range(slots * LEVELS):
+        squares[0, HALF_LANES + run] = LONG_SIDES[run // slots] ** 2
+        squares[1, HALF_LANES + run] = SHORT_SIDES[run // slots] ** 2
+        pick[HALF_LANES + run, run % slots] = 1.0
+    tri = np.triu(np.ones((LANES, LANES), np.float32))
+    low = jnp.bfloat16
+    return [jnp.asarray(squares), jnp.asarray(tri), jnp.asarray(pick, low), jnp.asarray(attention_rule(slots), low)]
 
 
 def attention_rule(slots):
@@ -1606,107 +1987,33 @@
 ):
     tok_rows, model_width = cotangent.shape
     low, f32 = jnp.bfloat16, jnp.float32
-    half = model_width // 2
-    core, wide = lax.axis_index("dp"), lax.axis_index("wide")
     group_len = tok_rows * lax.axis_size("wide")
     tokens_all = lax.axis_size("dp") * group_len
     lengths = item_lengths[0]
     slot_count = lengths.shape[0]
-    swap = [(0, 1), (1, 0)]
 
     states = (qkv_state, out_state, up_state, down_state, ada_state)
     flipped = tuple(stacked[1].astype(low).T for stacked in states[:4])
-    w_ada = ada_state[1].astype(low)
-
-    silu_own = jax.nn.silu(condition).astype(low)
-    silu_all = lax.all_gather(silu_own, "dp", axis=0, tiled=True)
-    silu_rows = lax.dynamic_slice_in_dim(silu_all, core * half, half, 1)
-    ada_part = jnp.dot(silu_rows, w_ada, preferred_element_type=f32)
-    ada_theirs = lax.dynamic_slice_in_dim(ada_part, (1 - core) * slot_count, slot_count, 0)
-    ada_mine = lax.dynamic_slice_in_dim(ada_part, core * slot_count, slot_count, 0)
-    ada_mine = ada_mine + lax.ppermute(ada_theirs, "dp", swap)
-    ada_block = jnp.pad(ada_mine, ((0, 8 - slot_count), (0, 0)))
-
-    starts, ends = run_bounds(lengths, group_len)
-    positions = wide * tok_rows + jnp.arange(tok_rows, dtype=jnp.int32)
-    after_start = positions[:, None] >= starts[None, :]
-    before_end = positions[:, None] < ends[None, :]
-    runs_of = (after_start & before_end).astype(f32)
-    live_rows = 1.0 - runs_of[:, -1:]
-    left_ok = 1.0 - jnp.sum(((positions[:, None] == starts[None, :]) & before_end).astype(f32), axis=1)
-    right_ok = 1.0 - jnp.sum(((positions[:, None] == ends[None, :] - 1) & after_start).astype(f32), axis=1)
-    one_hot = jnp.sum(runs_of[:, :-1].reshape(tok_rows, LEVELS, slot_count), axis=1)
-
-    rimmed = padded(feature_map, (("wide", 1),), 1)
-    smooth = smooth_map(feature_map, left_ok, right_ok, rimmed[:, :-2], rimmed[:, 2:])
+    groups = same_limits(key_limits(group_len, slot_count))
+    (
+        w_qkv, w_out, w_up, w_down, ada_gathered, h_one_low, kept_qk, out32, q_own, k_own, kt_own, vt_own, attn_low,
+        x_zero, smooth, flags, one_hot_wide, silu_rows, attn_proj, x_one, h_two_low, hidden_pre, act_low,
+    ) = front(
+        flipped,
+        condition,
+        ada_state,
+        feature_map,
+        embed_state,
+        vector_state,
+        item_lengths,
+        run_tables(slot_count),
+        groups,
+    )
     embed_w = embed_state[1]
-    vectors = vector_state[1]
-    gain = vectors[7:8]
-    x_zero = (
-        lax.dot_general(smooth, embed_w, (((0,), (0,)), ((), ())), precision=HIGHEST_PRECISION)
-        + vectors[6]
-    )
-    groups = same_limits(key_limits(group_len, slot_count))
-    lane_pad = lambda v: jnp.pad(v, (HALF_LANES, HALF_LANES - v.shape[0]))[None]
-    rule = jnp.asarray(attention_rule(slot_count), low)
-    one_hot_wide = jnp.pad(one_hot, ((0, 0), (0, 8 - slot_count)))
-    (w_qkv, w_out, w_up, w_down, ada_gathered, h_one_low, kept_qk, out32, *kept, attn_low) = front(
-        flipped, ada_block, x_zero, one_hot_wide, vectors, lane_pad(starts), lane_pad(ends), rule, groups
-    )
-    kept = [out32] + kept
-    ada_product = ada_gathered[:, :slot_count].transpose(1, 0, 2).reshape(slot_count, -1)
-    ada_all = ada_product + vectors[:6].reshape(-1)
-    token_ada = jnp.dot(one_hot, ada_all, precision=HIGHEST_PRECISION)
-    gate_one, gate_two, scale_one, scale_two, shift_one, shift_two = jnp.split(token_ada, 6, axis=1)
-
-    attn_proj = against(attn_low[:, :half], w_out[0]) + against(attn_low[:, half:], w_out[1])
-    x_one = x_zero + gate_one * attn_proj
-    h_two_low = pre_norm(x_one, scale_two, shift_two).astype(low)
-    hidden_pre = against(h_two_low[:, :half], w_up[0]) + against(h_two_low[:, half:], w_up[1])
-    act_low = jax.nn.gelu(hidden_pre, approximate=True).astype(low)
-    hidden_half = w_down.shape[2]
-    mlp_out = against(act_low[:, :hidden_half], w_down[0]) + against(act_low[:, hidden_half:], w_down[1])
-    x_two = x_one + gate_two * mlp_out
-    block_out = (x_two * live_rows).astype(low)
-    logits = against(block_out, code_book)
-    code_mass = jnp.sum(jax.nn.softmax(logits, axis=-1) * live_rows, axis=0)
-
-    g_two = cotangent.astype(f32) * live_rows
-    d_mlp = (gate_two * g_two).astype(low)
-    d_gate_two = g_two * mlp_out
-
-    def summed_over_cores(grad_rows, inputs):
-        width = inputs.shape[1] // 2
-        other = lax.dynamic_slice_in_dim(inputs, (1 - core) * width, width, 1)
-        own = lax.dynamic_slice_in_dim(inputs, core * width, width, 1)
-        their_rows, theirs = lax.ppermute((grad_rows, other), "dp", swap)
-        total = contract_rows(grad_rows, own) + contract_rows(their_rows, theirs)
-        return total.astype(low).reshape(4, 4, -1, width)
-
-    def both_halves(values, weights):
-        return jnp.concatenate(
-            [jnp.dot(values, weights[h], preferred_element_type=f32) for h in range(2)], axis=1
-        )
-
-    p_down = summed_over_cores(d_mlp, act_low)
-    d_act = both_halves(d_mlp, w_down)
-    _, gelu_back = jax.vjp(lambda inputs: jax.nn.gelu(inputs, approximate=True), hidden_pre)
-    d_hidden = gelu_back(d_act)[0].astype(low)
-    p_up = summed_over_cores(d_hidden, h_two_low)
-    d_h_two = both_halves(d_hidden, w_up)
-    _, norm_back_two = jax.vjp(pre_norm, x_one, scale_two, shift_two)
-    d_x_one, d_scale_two, d_shift_two = norm_back_two(d_h_two)
-    d_x_one = d_x_one + g_two
-    d_attn = (gate_one * d_x_one).astype(low)
-    d_gate_one = d_x_one * attn_proj
-    p_out = summed_over_cores(d_attn, attn_low)
-    d_attended = both_halves(d_attn, w_out).astype(low)
-    flags = jnp.pad(jnp.stack([left_ok, right_ok]), ((0, 6), (0, 0)))
-    hot_rows = one_hot_wide.T
-    mass_rows = code_mass.reshape(-1, model_width)
-    s_down, s_up, s_out, s_qkv, d_ada_both, common_sum, bias_sum, map_grad = back(
-        [d_attended, *kept, kept_qk, vectors, h_one_low, w_qkv, p_down, p_up, p_out, x_zero, scale_one, d_x_one]
-        + [hot_rows, d_gate_one, d_gate_two, d_scale_two, d_shift_two, smooth, embed_w, mass_rows, flags],
+    s_down, s_up, s_out, s_qkv, d_ada_both, common_sum, bias_sum, map_grad, block_out = back(
+        [cotangent, one_hot_wide, ada_gathered, vector_state, x_zero, x_one, attn_proj, h_one_low, h_two_low, attn_low]
+        + [act_low, hidden_pre, w_qkv, w_out, w_up, w_down, code_book, out32, q_own, k_own, kt_own, vt_own]
+        + [kept_qk.reshape(-1, LANES), smooth, embed_state, flags],
         groups,
         ((2, 2, 1), (2,)),
         1,
@@ -1715,10 +2022,10 @@
     d_embed_all = common_sum[:embed_rows]
     bias_rows = bias_sum[0].reshape(6, model_width)
     d_vectors_all = jnp.concatenate([bias_rows, common_sum[embed_rows : embed_rows + 2]], axis=0)
-    mass_all = common_sum[embed_rows + 2 : embed_rows + 2 + mass_rows.shape[0]]
+    mass_all = common_sum[embed_rows + 2 : embed_rows + 2 + code_book.shape[0] // model_width]
     histogram = mass_all.reshape(-1) * (code_book.shape[0] / tokens_all)
-    d_ada_own = d_ada_both[:, :slot_count].reshape(2 * slot_count, -1)
-    grad_ada = contract_rows(silu_rows.astype(f32), d_ada_own, HIGHEST_PRECISION)
+    d_ada_own = d_ada_both.reshape(16, -1)
+    grad_ada = contract_rows(silu_rows.reshape(16, -1), d_ada_own, HIGHEST_PRECISION)
 
     owned_grads = (s_qkv.T, s_out.T, s_up.T, s_down.T, grad_ada)
     root_tokens = math.sqrt(tokens_all)

time: 527 us -> 431 us (0.82)
  matrix products: 71.5 us -> 1.77 us
  other arithmetic: 32 us -> 14.5 us
  Pallas kernels: 375 us -> 389 us
  local copies, waits for them, and re-layouts: 28.6 us -> 17.3 us
  starting transfers between devices: 8.69 us -> 0 us
    dot_general x16 -> x0, matrix products: 46 us -> none  [the longest x7 26.6 us: against(): lax.dot_general(left_side, right_side, (((1,), (1,)), ((), ())), preferre...]
    dot_general x7 -> x1, matrix products: 25.4 us -> 1.77 us  [contract_rows(): lax.dot_general(left_side, right_side, (((0,), (0,)), ((), ())), precisio...]
    pallas_call x1, Pallas kernels: 210 us -> 218 us  [back(): pl.pallas_call(functools.partial(back_kernel, groups, (first, second)), o...]
    ppermute x9 -> x0, starting transfers between devices: 8.69 us -> none  [the longest x1 4.83 us: padded(): lax.ppermute(tail, axis, [(i, (i + 1) % count) for i in range(ends)])]
    another operation x13, other arithmetic: 13.2 us -> 7.64 us  [nesterov(): return jnp.stack([new_moment, new_weight, new_average])]
    pallas_call x1, Pallas kernels: 165 us -> 171 us  [front(): pl.pallas_call(functools.partial(front_kernel, groups, slots), out_shape=...]
  transfers between devices with their start and end apart: 9 -> 0, of which waited for: 0 -> 0; matrix products, arithmetic and copies ran while one was open for 9% -> 0% of each run, Pallas kernels for 0% -> 0%
where the time goes in v4:
time: 431 us; the launch traced here: 424 us
  Pallas kernels  389 us (90%)
  local copies, waits for them, and re-layouts  17.3 us (4%)
  other arithmetic  14.5 us (3%)
    pallas_call x1, Pallas kernels, back(): pl.pallas_call(functools.partial(back_kernel, groups, (first, second)), o...  218 us
    pallas_call x1, Pallas kernels, front(): pl.pallas_call(functools.partial(front_kernel, groups, slots), out_shape=...  171 us

profile of v4, /device:TPU:0, one launch (start us, length us, event | category | flops | bytes accessed | tf_op | source)
XLA Modules:
  0.0 423.9 jit_solution(12987518957439499970)
XLA Ops:
  0.6 1.5 fusion.23.refs_1_
  2.2 1.7 fusion.15.refs_0_
  3.9 1.8 fusion.14.refs_3_
  5.7 1.5 fusion.31
  7.1 1.0 copy.44
  8.3 0.7 fusion.13.refs_2_
  9.1 1.0 copy.43
  10.1 170.7 %shard_map.279 = (bf16[2,3072,512]{2,1,0:T(8,128)(2,1)}, bf16[2,1024,512]{2,1,0:T(8,128)(2,1)}, bf16[2,4096,512]{2,1,0:T(8,128)(2,1)}, bf16[2,1024,2048]{2,1,0:T...) custom-call(bf16[192,512]{1,0:T(8,128)(2,1)} %fusion.15.refs_0_, ...), custom_call_target="tpu_custom_call" | custom-call | tf_op jit(solution)/shard_map/pallas_call | solution.py:1187
  180.8 218.3 %shard_map.280 = (f32[64,2048]{1,0:T(8,128)}, f32[256,512]{1,0:T(8,128)}, f32[64,512]{1,0:T(8,128)}, f32[192,512]{1,0:T(8,128)}, f32[2,8,384]{2,1,0:T(8,128)}, /...) custom-call(bf16[192,1024]{1,0:T(8,128)(2,1)} %refs_0_.1, ...), custom_call_target="tpu_custom_call" | custom-call | tf_op jit(solution)/shard_map/pallas_call | solution.py:1938
  399.2 1.4 slice.108
  400.6 0.8 slice_bitcast_fusion
  401.3 0.8 multiply_bitcast_fusion
  402.1 0.6 copy.47
  402.7 1.0 slice_reduce_fusion
  403.7 0.9 multiply_add_fusion
  404.6 0.6 pad_maximum_fusion.6
  405.2 1.0 fusion.22
  406.2 0.8 pad_maximum_fusion.5
  407.0 1.0 fusion.28
  408.2 0.8 copy.41
  409.0 0.7 fusion.29
  409.7 0.8 pad_maximum_fusion.4
  410.5 0.8 fusion.30
  411.4 1.1 pad_maximum_fusion.3
  412.7 1.6 copy.40
  414.3 1.9 fusion.27
  416.3 1.2 pad_maximum_fusion.2
  417.6 1.0 copy-done
  418.5 1.8 fusion.26
  420.5 1.6 pad_maximum_fusion
  422.0 0.7 copy.50
  422.8 0.6 copy.51
  (37 shorter events, 0.9 us)
Async XLA Ops:
  180.8 224.5 %copy-start.1 = (f32[3,32,1024]{2,1,0:T(8,128)S(1)}, f32[3,32,1024]{2,1,0:T(8,128)}, u32[]{:S(2)}) copy-start(f32[3,32,1024]{2,1,0:T(8,128)} %refs_24_.1) | copy-start | bytes 1179652
  399.1 7.8 %copy-start.4 = (f32[1,512,256]{1,2,0:T(8,128)S(1)}, f32[1,512,256]{1,2,0:T(8,128)}, u32[]{:S(2)}) copy-start(f32[1,512,256]{1,2,0:T(8,128)} %copy.43) | copy-start | bytes 1572868
  403.7 3.3 copy-start.8
  407.0 1.0 copy-start.3
  408.0 1.0 copy-start.7
  408.0 1.0 copy-start.11
  408.1 2.4 copy-start.6
  408.2 2.4 copy-start.10
  411.3 1.2 copy-start.5
  412.7 1.6 copy-start.2
  416.3 2.2 copy-start
  416.3 2.2 copy-start.12
  416.3 2.2 copy-start.14
  420.5 1.6 copy-start.9
  420.5 2.3 copy-start.13

commit v5 on v4

--- a/solution.py
+++ b/solution.py
@@ -793,13 +793,27 @@
     return 0.5 * values * (1.0 + jnp.tanh(GELU_SCALE * (values + GELU_CUBE * values * values * values)))
 
 
+def gradient(grads, inputs, out, rows, shard):
+    count = rows // shard
+
+    def body(c, carry):
+        cols = pl.ds(pl.multiple_of(c * rows, LANES), rows)
+        total = nn(grads[0, :, cols].astype(jnp.float32).T.astype(jnp.bfloat16), inputs[0])
+        total = total + nn(grads[1, :, cols].astype(jnp.float32).T.astype(jnp.bfloat16), inputs[1])
+        first = lax.rem(c * count, 4)
+        out[c * count // 4, pl.ds(first, count)] = total.astype(jnp.bfloat16).reshape(count, shard, -1)
+        return carry
+
+    return body
+
+
 def front_kernel(groups, slots, *refs):
-    (s_qkv, s_out, s_up, s_down, cond_ref, ada_any, map_ref, embed_ref, vec3_ref, len_ref, squares_ref, tri_ref, pick_ref, rule_ref) = refs[:14]
-    (f_qkv, f_out, f_up, f_down, ada_ref, h_ref, kept_ref, out32_ref, q_ref, k_ref, kt_ref, vt_ref, low_ref) = refs[14:27]
-    (x_ref, smooth_ref, flags_ref, hot_ref, silu_ref, proj_ref, one_ref, two_ref, pre_ref, act_ref) = refs[27:37]
-    (w_ref, send_ref, got_ref, back_send, back_got, v_ref, s_ref, load_sem) = refs[37:45]
-    (w_ada, silu_own, theirs, ours, ada_in, edge, edge_left, edge_right, wo_ref, wu_ref) = refs[45:55]
-    sems = refs[55:]
+    (s_qkv, s_out, s_up, s_down, cond_ref, ada_any, map_ref, embed_ref, vec3_ref, len_ref, squares_ref, tri_ref, pick_ref, rule_ref, cot_ref) = refs[:15]
+    (f_qkv, f_out, f_up, f_down, ada_ref, h_ref, kept_ref, out32_ref, q_ref, k_ref, kt_ref, vt_ref, low_ref) = refs[15:28]
+    (x_ref, smooth_ref, flags_ref, hot_ref, silu_ref, proj_ref, one_ref, two_ref, pre_ref, act_ref, p_down) = refs[28:39]
+    (w_ref, send_ref, got_ref, back_send, back_got, v_ref, s_ref, load_sem) = refs[39:47]
+    (w_ada, silu_own, theirs, ours, ada_in, edge, edge_left, edge_right, wo_ref, wu_ref, dmlp, act_half) = refs[47:59]
+    sems = refs[59:]
     first_flow = Gather([s_qkv], [f_qkv], sems[:5], pieces_of([s_qkv], (2,)))
     flow = Gather([s_out, s_up, s_down], [f_out, f_up, f_down], sems[5:10], pieces_of([s_out, s_up, s_down], (1, 2, 2)))
     ada_send, ada_recv = sems[10:12]
@@ -1116,20 +1130,32 @@
         act_ref[:, cols] = gelu(pre).astype(low)
         return carry
 
+    live = jnp.sum(hot, axis=1, keepdims=True)
+    dmlp[core] = (of_tokens(1) * (cot_ref[...].astype(f32) * live)).astype(low)
+    pair_copies = [to_sib(2, dmlp.at[core], dmlp.at[core])]
+    hid_half = hidden // 2
+    hid_theirs = pl.ds(pl.multiple_of((1 - core) * hid_half, hid_half), hid_half)
+    hid_mine = pl.ds(pl.multiple_of(core * hid_half, hid_half), hid_half)
     for i in range(2):
         lax.fori_loop(4 * i, 4 * i + 4, up_step, 0)
         tick(1)
+    pair_copies.append(to_sib(3, act_ref.at[:, hid_theirs], act_half.at[core]))
+    act_half[core] = act_ref[:, hid_mine]
+    tick(1)
+    for copy in pair_copies:
+        copy.wait_recv()
+    lax.fori_loop(0, width // LANES, gradient(dmlp, act_half, p_down, LANES, width // 16), 0)
     tick(flow.steps())
     flow.landed(range(3, 5))
     first_flow.finish()
     flow.finish()
     there.finish()
     home.finish()
-    for copy in ada_copies + edges + [silu_copy, part_copy]:
+    for copy in ada_copies + edges + pair_copies + [silu_copy, part_copy]:
         copy.wait_send()
 
 
-def front(shards, condition, ada_state, cells, embed_state, vector_state, lengths, tables, groups):
+def front(shards, condition, ada_state, cells, embed_state, vector_state, lengths, tables, cotangent, groups):
     width = condition.shape[1]
     tokens = cells.shape[1]
     slots = lengths.shape[1]
@@ -1160,6 +1186,7 @@
         shape((tokens, width), low),
         shape((tokens, hidden), f32),
         shape((tokens, hidden), low),
+        shape((4, 4, width // 16, hidden // 2), low),
     ]
     packed, mid = tokens * 3 // 2, tokens // 2
     scratch = [
@@ -1181,19 +1208,21 @@
         pltpu.VMEM((32, LANES), f32),
         pltpu.VMEM((2, width, width // 2), low),
         pltpu.VMEM((2, 2, 512, width // 2), low),
+        pltpu.VMEM((2, tokens, width), low),
+        pltpu.VMEM((2, tokens, hidden // 2), low),
     ]
     scratch += Gather.scratch(2) + Gather.scratch(5) + [dma((16,)) for _ in range(6)]
-    scratch += [dma, dma((2,)), dma((2,)), dma((2,)), dma((2,)), dma, dma((2,))]
+    scratch += [dma, dma((4,)), dma((4,)), dma((2,)), dma((2,)), dma, dma((2,))]
     return pl.pallas_call(
         functools.partial(front_kernel, groups, slots),
         out_shape=outs,
-        in_specs=[ANY] * 4 + [VM, ANY] + [VM] * 8,
-        out_specs=[ANY] * 4 + [VM] * 19,
+        in_specs=[ANY] * 4 + [VM, ANY] + [VM] * 9,
+        out_specs=[ANY] * 4 + [VM] * 20,
         scratch_shapes=scratch,
         compiler_params=pltpu.CompilerParams(
             collective_id=0, has_side_effects=True, vmem_limit_bytes=VMEM_BYTES
         ),
-    )(*shards, condition, ada_state, cells, embed_state, vector_state, lengths, *tables)
+    )(*shards, condition, ada_state, cells, embed_state, vector_state, lengths, *tables, cotangent)
 
 
 class Scatter:
@@ -1355,6 +1384,8 @@
 
 
 COMMON_ROWS = 48
+BACK_SPLITS = ((4, 4, 1), (3,))
+BACK_TICKS = ((1, 1, 1, 1), (1, 0), (0, 0, 1, 0), (0, 0, 0, 0, 0, 1, 0, 0, 1, 0, 0, 1), (1, 1, 1), (1, 1))
 
 
 def standard_of(values):
@@ -1379,16 +1410,16 @@
     (
         cot_ref, hot_ref, ada_in, vec3_ref, x_ref, one_ref, proj_ref, h_any, two_any, low_any, act_any, pre_any,
         w_any, wo_any, wu_any, wd_any, book_any, out32_any, q_ref, k_ref, kt_ref, vt_ref, kept_any,
-        smooth_ref, embed_ref, ok_ref,
-    ) = refs[:26]
-    (o_down, o_up, o_out, o_qkv, ada_both, common_all, bias_all, map_ref, block_ref) = refs[26:35]
+        smooth_ref, embed_ref, ok_ref, p_down,
+    ) = refs[:27]
+    (o_down, o_up, o_out, o_qkv, ada_both, common_all, bias_all, map_ref, block_ref) = refs[27:36]
     (
         send_ref, got_ref, back_send, back_got, g_ref, gt_ref, qt_ref, dq_ref, dkt_ref, dvt_ref,
         w_buf, dhid, h_both, dh_ref, ada_ref, com_ref, ada_land, com_land, ada_sum, com_sum, ada_sib, com_sib,
         bias_own, com_own, edge, edge_left, edge_right,
-        act_half, dmlp, two_half, low_half, dattn, mlp_ref, dx_one, act_buf, pre_buf, d_att, p_down, p_up, p_out,
-    ) = refs[35:75]
-    rest = refs[75:]
+        dmlp, two_half, low_half, dattn, mlp_ref, dx_one, act_buf, pre_buf, d_att, p_up, p_out,
+    ) = refs[36:74]
+    rest = refs[74:]
     flow_bufs, rest = rest[:18], rest[18:]
     flow_sems, rest = rest[:2], rest[2:]
     last_bufs, rest = rest[:6], rest[6:]
@@ -1459,9 +1490,6 @@
     out32_copy.start()
     theirs = pl.ds(pl.multiple_of((1 - core) * half, half), half)
     mine = pl.ds(pl.multiple_of(core * half, half), half)
-    hid_half = hidden // 2
-    hid_theirs = pl.ds(pl.multiple_of((1 - core) * hid_half, hid_half), hid_half)
-    hid_mine = pl.ds(pl.multiple_of(core * hid_half, hid_half), hid_half)
     ada = jnp.concatenate([ada_in[w] for w in range(16)], axis=1)
     hot = hot_ref[...]
 
@@ -1470,10 +1498,8 @@
 
     live = jnp.sum(hot, axis=1, keepdims=True)
     gate_two = of_tokens(1)
-    dmlp[core] = (gate_two * (cot_ref[...].astype(f32) * live)).astype(low)
+    dmlp[...] = (gate_two * (cot_ref[...].astype(f32) * live)).astype(low)
     sib_copies = [
-        to_sib(0, dmlp.at[core], dmlp.at[core]),
-        to_sib(1, act_any.at[:, hid_theirs], act_half.at[core]),
         to_sib(2, two_any.at[:, theirs], two_half.at[core]),
         to_sib(3, low_any.at[:, theirs], low_half.at[core]),
         to_sib(4, h_any.at[:, theirs], h_both.at[core]),
@@ -1482,7 +1508,6 @@
         pltpu.make_async_copy(src, dst.at[core], half_sem.at[i])
         for i, (src, dst) in enumerate(
             [
-                (act_any.at[:, hid_mine], act_half),
                 (two_any.at[:, mine], two_half),
                 (low_any.at[:, mine], low_half),
                 (h_any.at[:, mine], h_both),
@@ -1511,8 +1536,7 @@
             copy.wait()
         slot = lax.rem(c, 2)
         w = w_buf.at[slot]
-        d_out = dmlp.at[core]
-        d_act = nn(d_out[:, :half], w[0]) + nn(d_out[:, half:], w[1])
+        d_act = nn(dmlp[:, :half], w[0]) + nn(dmlp[:, half:], w[1])
         d_hid = (d_act * gelu_slope(pre_buf[slot])).astype(low)
         dhid[core, :, pl.ds(pl.multiple_of(c * step, step), step)] = d_hid
         hid_copy(c).start()
@@ -1524,26 +1548,9 @@
         return carry
 
     chunks = hidden // step
-    lax.fori_loop(0, 3, hidden_step, 0)
-    sib_copies[0].wait_recv()
-    sib_copies[1].wait_recv()
-    half_copies[0].wait()
-
-    def gradient(grads, inputs, out, rows, shard, lanes):
-        def body(c, carry):
-            cols = pl.ds(pl.multiple_of(c * rows, LANES), rows)
-            total = nn(grads[0, :, cols].astype(f32).T.astype(low), inputs[0])
-            total = total + nn(grads[1, :, cols].astype(f32).T.astype(low), inputs[1])
-            count = rows // shard
-            out[c * count // 4, pl.ds(lax.rem(c * count, 4), count)] = total.astype(low).reshape(count, shard, lanes)
-            return carry
-
-        return body
-
-    lax.fori_loop(0, width // LANES, gradient(dmlp, act_half, p_down, LANES, width // 16, hid_half), 0)
-    tick(1)
-    lax.fori_loop(3, chunks, hidden_step, 0)
-    tick(1)
+    for i in range(4):
+        tick(BACK_TICKS[0][i])
+        lax.fori_loop(2 * i, 2 * i + 2, hidden_step, 0)
 
     wo_copies = [
         pltpu.make_async_copy(wo_any.at[c, pl.ds(r * half, half)], w_buf.at[0, 2 * c + r], w_sem.at[0, 2 * c + r])
@@ -1585,18 +1592,18 @@
     block_ref[...] = (live * (one_ref[...] + gate_two * mlp_ref[...])).astype(low)
     for c in range(chunks):
         hid_copy(c).wait_recv()
-    half_copies[1].wait()
-    sib_copies[2].wait_recv()
-    lax.fori_loop(0, hidden // 256, gradient(dhid, two_half, p_up, 256, hidden // 16, half), 0)
+    half_copies[0].wait()
+    sib_copies[0].wait_recv()
+    lax.fori_loop(0, hidden // 256, gradient(dhid, two_half, p_up, 256, hidden // 16), 0)
     for c in range(chunks):
         hid_copy(c).wait_send()
     pl.semaphore_signal(free_sem, inc=1, device_id=sib, device_id_type=MESH_ID)
-    tick(1)
-    half_copies[2].wait()
+    tick(BACK_TICKS[1][0])
+    half_copies[1].wait()
+    sib_copies[1].wait_recv()
     sib_copies[3].wait_recv()
-    sib_copies[5].wait_recv()
-    lax.fori_loop(0, width // LANES, gradient(dattn, low_half, p_out, LANES, width // 16, half), 0)
-    tick(1)
+    lax.fori_loop(0, width // LANES, gradient(dattn, low_half, p_out, LANES, width // 16), 0)
+    tick(BACK_TICKS[1][1])
     dkt_ref[...] = jnp.zeros_like(dkt_ref)
     dvt_ref[...] = jnp.zeros_like(dvt_ref)
 
@@ -1619,7 +1626,7 @@
     out32_copy.wait()
     for i in range(4):
         lax.fori_loop(2 * i, 2 * i + 2, unpack, 0)
-        tick((0, 1, 0, 0)[i])
+        tick(BACK_TICKS[2][i])
 
     def query_block(limit, b, carry):
         rows = pl.ds(pl.multiple_of(b * ROWS, ROWS), ROWS)
@@ -1648,7 +1655,7 @@
     for first, stop, limit in groups:
         for b in range(first, stop):
             lax.fori_loop(b, b + 1, functools.partial(query_block, limit), 0)
-            tick((0, 0, 0, 1, 0, 1, 0, 1, 0, 1, 0, 0)[b])
+            tick(BACK_TICKS[3][b])
 
     def send_out(pair, carry):
         rows = pl.ds(pl.multiple_of(pair * two, two), two)
@@ -1666,7 +1673,7 @@
 
     kept_copy = pltpu.make_async_copy(kept_any, dq_ref, kept_sem)
     kept_copy.start()
-    tick(1)
+    tick(BACK_TICKS[4][0])
     com_ref[...] = jnp.zeros_like(com_ref)
 
     def load_codes(c):
@@ -1699,6 +1706,7 @@
     start = (jnp.full((tokens, 1), -3e38, f32), jnp.zeros((tokens, 1), f32))
     top, total = lax.fori_loop(0, chunks, sum_codes, start)
     share_of = live / total
+    tick(BACK_TICKS[4][1])
     for c in range(chunks):
         mass = jnp.sum(jnp.exp(logits_of(chunks + c) - top) * share_of, axis=0, keepdims=True)
         com_ref[34 + c // 2 : 35 + c // 2, (c % 2) * step : (c % 2 + 1) * step] = mass
@@ -1712,6 +1720,7 @@
         for copy in load_w(j):
             copy.start()
     kept_copy.wait()
+    tick(BACK_TICKS[4][2])
 
     def unnormalize(values, grad):
         inverse = lax.rsqrt(head_sums(values * values) + NORM_EPS)
@@ -1739,7 +1748,9 @@
         dproj[core, :, key_cols] = unnormalize(dq_ref[pl.ds(pl.multiple_of((pair + 8) * tokens, tokens), tokens), :], d_key)[0].astype(low)
         return carry
 
-    lax.fori_loop(0, 8, heads_back, 0)
+    for i in range(2):
+        lax.fori_loop(4 * i, 4 * i + 4, heads_back, 0)
+        tick(BACK_TICKS[5][i])
     pl.semaphore_wait(free_sem, 1)
     d_copy = to_sib(6, dproj.at[core], dproj.at[core])
 
@@ -1753,8 +1764,8 @@
         if j + 2 < slabs:
             for copy in load_w(j + 2):
                 copy.start()
-    half_copies[3].wait()
-    sib_copies[4].wait_recv()
+    half_copies[2].wait()
+    sib_copies[2].wait_recv()
     d_copy.wait_recv()
 
     def weight_grad(c, carry):
@@ -1764,7 +1775,7 @@
         p_qkv[c // 2, pl.ds(2 * (c % 2), 2)] = total.astype(low).reshape(2, tokens, half)
         return carry
 
-    assert next_tick[0] >= 6
+    assert next_tick[0] >= len(splits[0]) + 2
     for p in range(len(splits[0])):
         flow.sent(p)
     lax.fori_loop(0, 8, weight_grad, 0)
@@ -1920,8 +1931,7 @@
         vm((32, LANES), f32),
         vm((32, LANES), f32),
         vm((32, LANES), f32),
-        vm((2, tokens, hidden // 2), low),
-        vm((2, tokens, width), low),
+        vm((tokens, width), low),
         vm((2, tokens, half), low),
         vm((2, tokens, half), low),
         vm((2, tokens, width), low),
@@ -1930,7 +1940,7 @@
         vm((2, tokens, 512), low),
         vm((2, tokens, 512), f32),
         vm((tokens, width), low),
-    ] + [vm((4, 4) + s, low) for s in sizes[:3]]
+    ] + [vm((4, 4) + s, low) for s in sizes[1:3]]
     scratch += Scatter.scratch(sizes[:3], len(first)) + Scatter.scratch(sizes[3:], len(second))
     scratch += [dma((16,)) for _ in range(4)] + [dma((2, 6)), dma((16,)), dma((16,))]
     scratch += [dma((2, 16)) for _ in range(4)] + [dma((2,)), dma((2,))]
@@ -1938,13 +1948,94 @@
     return pl.pallas_call(
         functools.partial(back_kernel, groups, (first, second)),
         out_shape=outs,
-        in_specs=[VM] * 7 + [ANY] * 11 + [VM] * 4 + [ANY] + [VM] * 3,
+        in_specs=[VM] * 7 + [ANY] * 11 + [VM] * 4 + [ANY] + [VM] * 4,
         out_specs=[VM] * 9,
         scratch_shapes=scratch,
         compiler_params=pltpu.CompilerParams(
             collective_id=call_id, has_side_effects=True, vmem_limit_bytes=63 * 1024 * 1024
         ),
     )(*args)
+
+
+def nesterov_rows(moment, weight, average, gradient, step_rate, decay_rate):
+    step_grad = gradient + decay_rate * weight
+    new_moment = MOMENTUM * moment + step_rate * step_grad
+    new_weight = weight - (step_rate * step_grad + MOMENTUM * new_moment)
+    retain = min(0.999, (1.0 + STEP) / (10.0 + STEP))
+    return new_moment, new_weight, retain * average + (1.0 - retain) * new_weight
+
+
+def update_kernel(rates, mass_scale, *refs):
+    states = refs[:5]
+    (embed_ref, vector_ref, s_down, s_up, s_out, s_qkv, d_ada, silu_ref, common_ref, bias_ref) = refs[5:15]
+    news, copies = refs[15:20], refs[20:25]
+    (embed_new, vector_new, mass_out, gain_out) = refs[25:29]
+    held, lows = refs[29:34], refs[34:39]
+    load_sem, store_sem, low_sem = refs[39:]
+    width = vector_ref.shape[2]
+
+    def grad_of(i):
+        if i == 4:
+            return exact(silu_ref[...], d_ada[...], (0, 0))
+        return (s_qkv, s_out, None, s_down)[i][...] if i != 2 else s_up[...].T
+
+    order = (3, 2, 4, 0, 1)
+    loads = {i: pltpu.make_async_copy(states[i], held[i], load_sem.at[i]) for i in order}
+    for i in order:
+        loads[i].start()
+    rows = embed_ref.shape[1]
+    parts = nesterov_rows(embed_ref[0], embed_ref[1], embed_ref[2], common_ref[0:rows, :], rates[5], 0.0)
+    for j in range(3):
+        embed_new[j] = parts[j]
+    for block in range(8):
+        if block < 6:
+            grad = bias_ref[0:1, block * width : (block + 1) * width]
+        else:
+            grad = common_ref[rows + block - 6 : rows + block - 5, :]
+        here = slice(block, block + 1)
+        parts = nesterov_rows(vector_ref[0, here], vector_ref[1, here], vector_ref[2, here], grad, rates[6], 0.0)
+        for j in range(3):
+            vector_new[j, here] = parts[j]
+    per_row = width // LANES
+    for r in range(per_row):
+        cols = slice(r * LANES, (r + 1) * LANES)
+        gain_out[r : r + 1, :] = common_ref[rows + 1 : rows + 2, cols]
+        for a in range(mass_out.shape[0] // per_row):
+            at = a * per_row + r
+            mass_out[at : at + 1, :] = common_ref[rows + 2 + a : rows + 3 + a, cols] * mass_scale
+    stores = []
+    for i in order:
+        loads[i].wait()
+        parts = nesterov_rows(held[i][0], held[i][1], held[i][2], grad_of(i), rates[i], WEIGHT_DECAY)
+        for j in range(3):
+            held[i][j] = parts[j]
+        lows[i][...] = parts[1].astype(jnp.bfloat16)
+        stores.append(pltpu.make_async_copy(held[i], news[i], store_sem.at[i]))
+        stores.append(pltpu.make_async_copy(lows[i], copies[i], low_sem.at[i]))
+        for copy in stores[-2:]:
+            copy.start()
+    for copy in stores:
+        copy.wait()
+
+
+def update(states, embed_state, vector_state, grads, rates, codes, mass_scale):
+    f32, low = jnp.float32, jnp.bfloat16
+    shape = jax.ShapeDtypeStruct
+    dma = pltpu.SemaphoreType.DMA
+    width = vector_state.shape[2]
+    outs = [shape(s.shape, f32) for s in states] + [shape(s.shape[1:], low) for s in states]
+    outs += [shape(embed_state.shape, f32), shape(vector_state.shape, f32)]
+    outs += [shape((codes // LANES, LANES), f32), shape((width // LANES, LANES), f32)]
+    return pl.pallas_call(
+        functools.partial(update_kernel, rates, mass_scale),
+        out_shape=outs,
+        in_specs=[ANY] * 5 + [VM] * 10,
+        out_specs=[ANY] * 10 + [VM] * 4,
+        scratch_shapes=[pltpu.VMEM(s.shape, f32) for s in states]
+        + [pltpu.VMEM(s.shape[1:], low) for s in states]
+        + [dma((5,)), dma((5,)), dma((5,))],
+        compiler_params=pltpu.CompilerParams(vmem_limit_bytes=VMEM_BYTES),
+    )(*states, embed_state, vector_state, *grads)
 
 
 def run_tables(slots):
@@ -1986,7 +2077,7 @@
     vector_state,
 ):
     tok_rows, model_width = cotangent.shape
-    low, f32 = jnp.bfloat16, jnp.float32
+    low = jnp.bfloat16
     group_len = tok_rows * lax.axis_size("wide")
     tokens_all = lax.axis_size("dp") * group_len
     lengths = item_lengths[0]
@@ -1997,7 +2088,7 @@
     groups = same_limits(key_limits(group_len, slot_count))
     (
         w_qkv, w_out, w_up, w_down, ada_gathered, h_one_low, kept_qk, out32, q_own, k_own, kt_own, vt_own, attn_low,
-        x_zero, smooth, flags, one_hot_wide, silu_rows, attn_proj, x_one, h_two_low, hidden_pre, act_low,
+        x_zero, smooth, flags, one_hot_wide, silu_rows, attn_proj, x_one, h_two_low, hidden_pre, act_low, p_down,
     ) = front(
         flipped,
         condition,
@@ -2007,27 +2098,18 @@
         vector_state,
         item_lengths,
         run_tables(slot_count),
+        cotangent,
         groups,
     )
-    embed_w = embed_state[1]
     s_down, s_up, s_out, s_qkv, d_ada_both, common_sum, bias_sum, map_grad, block_out = back(
         [cotangent, one_hot_wide, ada_gathered, vector_state, x_zero, x_one, attn_proj, h_one_low, h_two_low, attn_low]
         + [act_low, hidden_pre, w_qkv, w_out, w_up, w_down, code_book, out32, q_own, k_own, kt_own, vt_own]
-        + [kept_qk.reshape(-1, LANES), smooth, embed_state, flags],
+        + [kept_qk.reshape(-1, LANES), smooth, embed_state, flags, p_down],
         groups,
-        ((2, 2, 1), (2,)),
+        BACK_SPLITS,
         1,
     )
-    embed_rows = embed_w.shape[0]
-    d_embed_all = common_sum[:embed_rows]
-    bias_rows = bias_sum[0].reshape(6, model_width)
-    d_vectors_all = jnp.concatenate([bias_rows, common_sum[embed_rows : embed_rows + 2]], axis=0)
-    mass_all = common_sum[embed_rows + 2 : embed_rows + 2 + code_book.shape[0] // model_width]
-    histogram = mass_all.reshape(-1) * (code_book.shape[0] / tokens_all)
-    d_ada_own = d_ada_both.reshape(16, -1)
-    grad_ada = contract_rows(silu_rows.reshape(16, -1), d_ada_own, HIGHEST_PRECISION)
-
-    owned_grads = (s_qkv.T, s_out.T, s_up.T, s_down.T, grad_ada)
+    flip = lambda values: jnp.swapaxes(values, -1, -2)
     root_tokens = math.sqrt(tokens_all)
     spreads = (
         model_width ** (-0.5),
@@ -2036,18 +2118,24 @@
         w_up.shape[1] ** (-0.5),
         model_width ** (-0.5),
     )
-    new_states = tuple(
-        nesterov(stacked, gradient, BASE_RATE * spread_w / (factor_g * root_tokens), WEIGHT_DECAY)
-        for stacked, gradient, spread_w, factor_g in zip(states, owned_grads, spreads, GRAD_FACTORS)
-    )
-    embed_new = nesterov(
-        embed_state, d_embed_all, BASE_RATE * embed_rows ** (-0.5) / (EMBED_FACTOR * root_tokens), 0.0
-    )
-    vector_new = nesterov(vector_state, d_vectors_all, VECTOR_RATE / root_tokens, 0.0)
-    outputs = [block_out, map_grad, histogram]
-    for state in new_states:
-        outputs += [state, state[1].astype(low)]
-    return tuple(outputs + [embed_new, vector_new, d_vectors_all[7]])
+    rates = [BASE_RATE * spread_w / (factor_g * root_tokens) for spread_w, factor_g in zip(spreads, GRAD_FACTORS)]
+    rates.append(BASE_RATE * embed_state.shape[1] ** (-0.5) / (EMBED_FACTOR * root_tokens))
+    rates.append(VECTOR_RATE / root_tokens)
+    codes = code_book.shape[0]
+    results = update(
+        [flip(qkv_state), flip(out_state), up_state, flip(down_state), ada_state],
+        embed_state,
+        vector_state,
+        [s_down, s_up, s_out, s_qkv, d_ada_both.reshape(16, -1), silu_rows.reshape(16, -1), common_sum, bias_sum],
+        tuple(rates),
+        codes,
+        codes / tokens_all,
+    )
+    outputs = [block_out, map_grad, results[12].reshape(-1)]
+    for i in range(5):
+        new, copied = results[i], results[5 + i]
+        outputs += [flip(new), flip(copied)] if i in (0, 1, 3) else [new, copied]
+    return tuple(outputs + [results[10], results[11], results[13].reshape(-1)])
 
 
 def solution(mesh):

time: 431 us -> 390 us (0.905)
  Pallas kernels: 389 us -> 374 us
  other arithmetic: 14.5 us -> 0 us
  local copies, waits for them, and re-layouts: 17.3 us -> 8.3 us
    pallas_call x1, Pallas kernels: 218 us -> 189 us  [back(): pl.pallas_call(functools.partial(back_kernel, groups, (first, second)), o...]
    pallas_call x0 -> x1, Pallas kernels: none -> 8.42 us  [update(): pl.pallas_call(functools.partial(update_kernel, rates, mass_scale), out_s...]
    another operation x13 -> x0, other arithmetic: 7.64 us -> none  [nesterov(): return jnp.stack([new_moment, new_weight, new_average])]
    pallas_call x1, Pallas kernels: 171 us -> 177 us  [front(): pl.pallas_call(functools.partial(front_kernel, groups, slots), out_shape=...]
    unnamed x38 -> x7, local copies, waits for them, and re-layouts: 7.68 us -> 2.22 us
    convert_element_type x4 -> x0, other arithmetic: 4.44 us -> none  [fast_shards(): outputs += [state, state[1].astype(low)]]
where the time goes in v5:
time: 390 us; the launch traced here: 384 us
  Pallas kernels  374 us (96%)
  local copies, waits for them, and re-layouts  8.3 us (2%)
    pallas_call x1, Pallas kernels, back(): pl.pallas_call(functools.partial(back_kernel, groups, (first, second)), o...  189 us
    pallas_call x1, Pallas kernels, front(): pl.pallas_call(functools.partial(front_kernel, groups, slots), out_shape=...  177 us
    pallas_call x1, Pallas kernels, update(): pl.pallas_call(functools.partial(update_kernel, rates, mass_scale), out_s...  8.42 us

profile of v5, /device:TPU:0, one launch (start us, length us, event | category | flops | bytes accessed | tf_op | source)
XLA Modules:
  0.0 383.6 jit_solution(12060109228153858444)
XLA Ops:
  0.6 1.5 fusion.2.refs_1_
  2.2 1.7 fusion.1.refs_0_
  3.9 1.1 slice.22
  5.0 0.8 copy.33
  5.8 1.8 fusion.refs_3_
  7.6 177.1 %shard_map.279 = (bf16[2,3072,512]{2,1,0:T(8,128)(2,1)}, bf16[2,1024,512]{2,1,0:T(8,128)(2,1)}, bf16[2,4096,512]{2,1,0:T(8,128)(2,1)}, bf16[2,1024,2048]{2,1,0:T...) custom-call(bf16[192,512]{1,0:T(8,128)(2,1)} %fusion.1.refs_0_, ...), custom_call_target="tpu_custom_call" | custom-call | tf_op jit(solution)/shard_map/pallas_call | solution.py:1216
  184.7 188.6 %shard_map.280 = (f32[64,2048]{1,0:T(8,128)}, f32[256,512]{1,0:T(8,128)}, f32[64,512]{1,0:T(8,128)}, f32[192,512]{1,0:T(8,128)}, f32[2,8,384]{2,1,0:T(8,128)}, /...) custom-call(bf16[192,1024]{1,0:T(8,128)(2,1)} %refs_0_.1, ...), custom_call_target="tpu_custom_call" | custom-call | tf_op jit(solution)/shard_map/pallas_call | solution.py:1948
  373.3 0.0 copy-start
  373.3 0.0 copy-start.1
  373.3 8.4 %shard_map.281 = (f32[3,192,512]{2,1,0:T(8,128)}, f32[3,64,512]{2,1,0:T(8,128)}, f32[3,512,256]{2,1,0:T(8,128)}, f32[3,64,2048]{2,1,0:T(8,128)}, f32[3,512,384]{...) custom-call(f32[3,192,512]{2,1,0:T(8,128)} %bitcast.32, ...), custom_call_target="tpu_custom_call" | custom-call | tf_op jit(solution)/shard_map/pallas_call | solution.py:2029
  381.8 0.0 copy-done
  381.8 0.7 copy.36
  382.5 0.0 copy-done.1
  382.5 0.6 copy.37
Async XLA Ops:
  373.3 8.5 %copy-start = (bf16[192,1024]{1,0:T(8,128)(2,1)S(1)}, bf16[192,1024]{1,0:T(8,128)(2,1)}, u32[]{:S(2)}) copy-start(bf16[192,1024]{1,0:T(8,128)(2,1)} %get-tuple-element.126) | copy-start | bytes 1179652
  373.3 9.2 %copy-start.1 = (f32[32,192]{1,0:T(8,128)S(1)}, f32[32,192]{1,0:T(8,128)}, u32[]{:S(2)}) copy-start(f32[32,192]{1,0:T(8,128)} %get-tuple-element.127) | copy-start | bytes 73732

commit v6 on v5

--- a/solution.py
+++ b/solution.py
@@ -808,14 +808,16 @@
 
 
 def front_kernel(groups, slots, *refs):
-    (s_qkv, s_out, s_up, s_down, cond_ref, ada_any, map_ref, embed_ref, vec3_ref, len_ref, squares_ref, tri_ref, pick_ref, rule_ref, cot_ref) = refs[:15]
-    (f_qkv, f_out, f_up, f_down, ada_ref, h_ref, kept_ref, out32_ref, q_ref, k_ref, kt_ref, vt_ref, low_ref) = refs[15:28]
-    (x_ref, smooth_ref, flags_ref, hot_ref, silu_ref, proj_ref, one_ref, two_ref, pre_ref, act_ref, p_down) = refs[28:39]
+    (m_qkv, m_out, m_up, m_down, cond_ref, ada_any, map_ref, embed_ref, vec3_ref, len_ref, squares_ref, tri_ref, pick_ref, rule_ref, cot_ref) = refs[:15]
+    (f_qkv, f_out, f_up, f_down, ada_ref, h_ref, kept_any, out32_any, q_any, k_any, kt_any, vt_any, low_ref) = refs[15:28]
+    (x_ref, smooth_ref, flags_ref, hot_ref, silu_ref, proj_ref, one_ref, two_ref, pre_any, act_any, p_any) = refs[28:39]
     (w_ref, send_ref, got_ref, back_send, back_got, v_ref, s_ref, load_sem) = refs[39:47]
     (w_ada, silu_own, theirs, ours, ada_in, edge, edge_left, edge_right, wo_ref, wu_ref, dmlp, act_half) = refs[47:59]
-    sems = refs[59:]
-    first_flow = Gather([s_qkv], [f_qkv], sems[:5], pieces_of([s_qkv], (2,)))
-    flow = Gather([s_out, s_up, s_down], [f_out, f_up, f_down], sems[5:10], pieces_of([s_out, s_up, s_down], (1, 2, 2)))
+    (kept_ref, out32_ref, q_ref, k_ref, kt_ref, vt_ref, pre_ref, act_ref, p_down) = refs[59:68]
+    (c_qkv, c_out, c_up, c_down, s_qkv, s_out, s_up, s_down, cast_sem, store_sem) = refs[68:78]
+    sems = refs[78:]
+    first_flow = Gather([s_qkv], [f_qkv], sems[:5], pieces_of([s_qkv], FRONT_SPLITS[0]))
+    flow = Gather([s_out, s_up, s_down], [f_out, f_up, f_down], sems[5:10], pieces_of([s_out, s_up, s_down], FRONT_SPLITS[1]))
     ada_send, ada_recv = sems[10:12]
     there = Exchange(send_ref, got_ref, sems[12:14])
     home = Exchange(back_send, back_got, sems[14:16])
@@ -830,6 +832,19 @@
     group_len = q_ref.shape[0]
     f32, low = jnp.float32, jnp.bfloat16
     vec_ref = vec3_ref.at[1]
+    casts = []
+    for i, (src, dst) in enumerate(((m_qkv, c_qkv), (m_out, c_out), (m_up, c_up), (m_down, c_down))):
+        casts.append(pltpu.make_async_copy(src.at[1], dst, cast_sem.at[i]))
+        casts[-1].start()
+    stores = []
+
+    def store(*pairs):
+        for src, dst in pairs:
+            stores.append(pltpu.make_async_copy(src, dst, store_sem.at[len(stores)]))
+            stores[-1].start()
+
+    casts[0].wait()
+    s_qkv[...] = c_qkv[...].astype(low)
     entry_barrier([(core, wide ^ r) for r in range(1, 16)] + [sib])
 
     def to_sib(slot, src, dst):
@@ -838,6 +853,17 @@
         )
         copy.start()
         return copy
+
+    next_tick = [0]
+
+    def tick(n):
+        for _ in range(n):
+            if next_tick[0] < flow.steps():
+                flow.run(next_tick[0])
+                next_tick[0] += 1
+
+    def tick_to(n):
+        tick(max(0, n - next_tick[0]))
 
     first_flow.run(0)
     ada_copy = pltpu.make_async_copy(ada_any.at[1], w_ada, ada_sem)
@@ -868,6 +894,12 @@
     for copy in edges:
         copy.start()
     first_flow.run(1)
+
+    for copy in casts[1:]:
+        copy.wait()
+    s_out[...] = c_out[...].astype(low)
+    s_up[...] = c_up[...].T.astype(low)
+    s_down[...] = c_down[...].astype(low)
 
     run_lane = lane_iota((1, LANES))
     run_slot = lax.rem(run_lane - HALF_LANES + slots * LANES, slots)
@@ -938,17 +970,9 @@
         return exact(hot, ada[:, block * width : (block + 1) * width] + vec_ref[block : block + 1, :])
 
     h_ref[...] = (unit * (1.0 + of_tokens(2)) + of_tokens(4)).astype(low)
-    for t in range(4, first_flow.steps()):
+    for i, t in enumerate(range(4, first_flow.steps())):
         first_flow.run(t)
-    next_tick = [0]
-
-    def tick(n):
-        for _ in range(n):
-            if next_tick[0] < flow.steps():
-                flow.run(next_tick[0])
-                next_tick[0] += 1
-
-    tick(1)
+        tick(FRONT_TICKS[0][min(i, 3)])
     first_flow.landed()
 
     group = 256
@@ -998,7 +1022,7 @@
             send_ref[head + 1, tokens:, :] = jnp.where(lane_mid < HALF_LANES, swap_halves(v_a), v_b).astype(low)
         for e in range(4):
             there.push(g * 4 + e)
-        tick((0, 1, 0, 0)[j])
+        tick(FRONT_TICKS[1][j])
 
     lane_two = lane_iota((two, LANES))
 
@@ -1076,23 +1100,23 @@
         home.push(w)
         return carry
 
+    store((kept_ref, kept_any))
     for i in range(4):
         lax.fori_loop(2 * i, 2 * i + 2, unpack, 0)
-        tick((0, 1, 0, 1)[i])
+        tick(FRONT_TICKS[2][i])
+    store((k_ref, k_any), (kt_ref, kt_any), (vt_ref, vt_any))
     plane = 4 * tokens // ROWS
-    done = 0
     for p in range(4):
         for first, last, limit in groups:
             begin, end = max(first, p * plane), min(last, (p + 1) * plane)
-            if begin < end:
-                lax.fori_loop(begin, end, functools.partial(query_block, limit), 0)
-                tick((0, 1, 0, 1, 0, 1, 0, 1)[done])
-                done += 1
+            for b in range(begin, end):
+                lax.fori_loop(b, b + 1, functools.partial(query_block, limit), 0)
+                tick(FRONT_TICKS[3][b])
         lax.fori_loop(4 * p, 4 * p + 4, give_back, 0)
-    tick(1)
-    while next_tick[0] < 8:
-        tick(1)
-    flow.landed((0,))
+    store((q_ref, q_any), (out32_ref, out32_any))
+    splits = FRONT_SPLITS[1]
+    tick_to(splits[0] + 5)
+    flow.landed(range(splits[0]))
     wo_copy = pltpu.make_async_copy(f_out, wo_ref, wo_sem)
     wo_copy.start()
     for pair in range(8):
@@ -1109,7 +1133,8 @@
     x_one = x_ref[...] + of_tokens(0) * proj
     one_ref[...] = x_one
     two_ref[...] = (standard(x_one) * (1.0 + of_tokens(3)) + of_tokens(5)).astype(low)
-    flow.landed((1, 2))
+    tick_to(splits[0] + splits[1] + 5)
+    flow.landed(range(splits[0], splits[0] + splits[1]))
     step = 512
     hidden = pre_ref.shape[1]
 
@@ -1138,34 +1163,39 @@
     hid_mine = pl.ds(pl.multiple_of(core * hid_half, hid_half), hid_half)
     for i in range(2):
         lax.fori_loop(4 * i, 4 * i + 4, up_step, 0)
-        tick(1)
+        tick(FRONT_TICKS[4][i])
+    store((pre_ref, pre_any), (act_ref, act_any))
     pair_copies.append(to_sib(3, act_ref.at[:, hid_theirs], act_half.at[core]))
     act_half[core] = act_ref[:, hid_mine]
-    tick(1)
+    tick(FRONT_TICKS[4][2])
     for copy in pair_copies:
         copy.wait_recv()
     lax.fori_loop(0, width // LANES, gradient(dmlp, act_half, p_down, LANES, width // 16), 0)
+    store((p_down, p_any))
     tick(flow.steps())
-    flow.landed(range(3, 5))
+    flow.landed(range(splits[0] + splits[1], sum(splits)))
     first_flow.finish()
     flow.finish()
     there.finish()
     home.finish()
     for copy in ada_copies + edges + pair_copies + [silu_copy, part_copy]:
         copy.wait_send()
-
-
-def front(shards, condition, ada_state, cells, embed_state, vector_state, lengths, tables, cotangent, groups):
+    for copy in stores:
+        copy.wait()
+
+
+def front(states, condition, ada_state, cells, embed_state, vector_state, lengths, tables, cotangent, groups):
     width = condition.shape[1]
     tokens = cells.shape[1]
     slots = lengths.shape[1]
     group_len = 16 * tokens
-    hidden = 16 * shards[2].shape[0]
+    hidden = 16 * states[2].shape[2]
     f32, low = jnp.float32, jnp.bfloat16
     dma = pltpu.SemaphoreType.DMA
     shape = jax.ShapeDtypeStruct
     ada_width = ada_state.shape[2]
-    fulls = [shape((2, 16 * s.shape[0], s.shape[1]), low) for s in shards]
+    shards = [s.shape[1:] if i != 2 else s.shape[:0:-1] for i, s in enumerate(states)]
+    fulls = [shape((2, 16 * s[0], s[1]), low) for s in shards]
     outs = fulls + [
         shape((16, 8, ada_width), f32),
         shape((tokens, width), low),
@@ -1211,18 +1241,21 @@
         pltpu.VMEM((2, tokens, width), low),
         pltpu.VMEM((2, tokens, hidden // 2), low),
     ]
-    scratch += Gather.scratch(2) + Gather.scratch(5) + [dma((16,)) for _ in range(6)]
+    scratch += [pltpu.VMEM(o.shape, o.dtype) for o in outs[6:12] + outs[21:24]]
+    scratch += [pltpu.VMEM(s.shape[1:], f32) for s in states] + [pltpu.VMEM(s, low) for s in shards]
+    scratch += [dma((4,)), dma((10,))]
+    scratch += Gather.scratch(sum(FRONT_SPLITS[0])) + Gather.scratch(sum(FRONT_SPLITS[1])) + [dma((16,)) for _ in range(6)]
     scratch += [dma, dma((4,)), dma((4,)), dma((2,)), dma((2,)), dma, dma((2,))]
     return pl.pallas_call(
         functools.partial(front_kernel, groups, slots),
         out_shape=outs,
         in_specs=[ANY] * 4 + [VM, ANY] + [VM] * 9,
-        out_specs=[ANY] * 4 + [VM] * 20,
+        out_specs=[ANY] * 4 + [VM] * 2 + [ANY] * 6 + [VM] * 9 + [ANY] * 3,
         scratch_shapes=scratch,
         compiler_params=pltpu.CompilerParams(
             collective_id=0, has_side_effects=True, vmem_limit_bytes=VMEM_BYTES
         ),
-    )(*shards, condition, ada_state, cells, embed_state, vector_state, lengths, *tables, cotangent)
+    )(*states, condition, ada_state, cells, embed_state, vector_state, lengths, *tables, cotangent)
 
 
 class Scatter:
@@ -1384,6 +1417,8 @@
 
 
 COMMON_ROWS = 48
+FRONT_SPLITS = ((2,), (1, 4, 4))
+FRONT_TICKS = ((1, 1, 1, 0), (0, 1, 0, 1), (0, 1, 0, 1), (0, 0, 0, 0, 0, 1, 0, 0, 1, 0, 0, 1), (1, 1, 1))
 BACK_SPLITS = ((4, 4, 1), (3,))
 BACK_TICKS = ((1, 1, 1, 1), (1, 0), (0, 0, 1, 0), (0, 0, 0, 0, 0, 1, 0, 0, 1, 0, 0, 1), (1, 1, 1), (1, 1))
 
@@ -1409,17 +1444,17 @@
 def back_kernel(groups, splits, *refs):
     (
         cot_ref, hot_ref, ada_in, vec3_ref, x_ref, one_ref, proj_ref, h_any, two_any, low_any, act_any, pre_any,
-        w_any, wo_any, wu_any, wd_any, book_any, out32_any, q_ref, k_ref, kt_ref, vt_ref, kept_any,
-        smooth_ref, embed_ref, ok_ref, p_down,
+        w_any, wo_any, wu_any, wd_any, book_any, out32_any, q_any, k_any, kt_any, vt_any, kept_any,
+        smooth_ref, embed_ref, ok_ref, p_any,
     ) = refs[:27]
     (o_down, o_up, o_out, o_qkv, ada_both, common_all, bias_all, map_ref, block_ref) = refs[27:36]
     (
         send_ref, got_ref, back_send, back_got, g_ref, gt_ref, qt_ref, dq_ref, dkt_ref, dvt_ref,
         w_buf, dhid, h_both, dh_ref, ada_ref, com_ref, ada_land, com_land, ada_sum, com_sum, ada_sib, com_sib,
         bias_own, com_own, edge, edge_left, edge_right,
-        dmlp, two_half, low_half, dattn, mlp_ref, dx_one, act_buf, pre_buf, d_att, p_up, p_out,
-    ) = refs[36:74]
-    rest = refs[74:]
+        dmlp, two_half, low_half, dattn, mlp_ref, dx_one, act_buf, pre_buf, d_att, p_up, p_out, p_down, q_ref, k_ref, kt_ref, vt_ref, early_sem,
+    ) = refs[36:80]
+    rest = refs[80:]
     flow_bufs, rest = rest[:18], rest[18:]
     flow_sems, rest = rest[:2], rest[2:]
     last_bufs, rest = rest[:6], rest[6:]
@@ -1445,6 +1480,14 @@
     last = Scatter([p_qkv], [o_qkv], last_bufs, last_sems, splits[1])
     there = Exchange(back_send, back_got, (ex_s, ex_r))
     home = Exchange(send_ref, got_ref, (home_s, home_r))
+    early = [
+        pltpu.make_async_copy(src, dst, early_sem.at[i])
+        for i, (src, dst) in enumerate(
+            [(p_any, p_down), (q_any, q_ref), (k_any, k_ref), (kt_any, kt_ref), (vt_any, vt_ref)]
+        )
+    ]
+    for copy in early:
+        copy.start()
     entry_barrier([(core, wide ^ r) for r in range(1, 16)] + [sib])
 
     def to_sib(slot, src, dst):
@@ -1548,6 +1591,7 @@
         return carry
 
     chunks = hidden // step
+    early[0].wait()
     for i in range(4):
         tick(BACK_TICKS[0][i])
         lax.fori_loop(2 * i, 2 * i + 2, hidden_step, 0)
@@ -1624,6 +1668,8 @@
         return carry
 
     out32_copy.wait()
+    for copy in early[1:]:
+        copy.wait()
     for i in range(4):
         lax.fori_loop(2 * i, 2 * i + 2, unpack, 0)
         tick(BACK_TICKS[2][i])
@@ -1940,7 +1986,8 @@
         vm((2, tokens, 512), low),
         vm((2, tokens, 512), f32),
         vm((tokens, width), low),
-    ] + [vm((4, 4) + s, low) for s in sizes[1:3]]
+    ] + [vm((4, 4) + s, low) for s in (sizes[1], sizes[2], sizes[0])]
+    scratch += [vm((group_len, LANES), low)] * 2 + [vm((LANES, group_len), low)] * 2 + [dma((5,))]
     scratch += Scatter.scratch(sizes[:3], len(first)) + Scatter.scratch(sizes[3:], len(second))
     scratch += [dma((16,)) for _ in range(4)] + [dma((2, 6)), dma((16,)), dma((16,))]
     scratch += [dma((2, 16)) for _ in range(4)] + [dma((2,)), dma((2,))]
@@ -1948,7 +1995,7 @@
     return pl.pallas_call(
         functools.partial(back_kernel, groups, (first, second)),
         out_shape=outs,
-        in_specs=[VM] * 7 + [ANY] * 11 + [VM] * 4 + [ANY] + [VM] * 4,
+        in_specs=[VM] * 7 + [ANY] * 16 + [VM] * 3 + [ANY],
         out_specs=[VM] * 9,
         scratch_shapes=scratch,
         compiler_params=pltpu.CompilerParams(
@@ -2083,8 +2130,8 @@
     lengths = item_lengths[0]
     slot_count = lengths.shape[0]
 
-    states = (qkv_state, out_state, up_state, down_state, ada_state)
-    flipped = tuple(stacked[1].astype(low).T for stacked in states[:4])
+    flip = lambda values: jnp.swapaxes(values, -1, -2)
+    flipped = [flip(qkv_state), flip(out_state), up_state, flip(down_state)]
     groups = same_limits(key_limits(group_len, slot_count))
     (
         w_qkv, w_out, w_up, w_down, ada_gathered, h_one_low, kept_qk, out32, q_own, k_own, kt_own, vt_own, attn_low,
@@ -2109,7 +2156,6 @@
         BACK_SPLITS,
         1,
     )
-    flip = lambda values: jnp.swapaxes(values, -1, -2)
     root_tokens = math.sqrt(tokens_all)
     spreads = (
         model_width ** (-0.5),
@@ -2123,7 +2169,7 @@
     rates.append(VECTOR_RATE / root_tokens)
     codes = code_book.shape[0]
     results = update(
-        [flip(qkv_state), flip(out_state), up_state, flip(down_state), ada_state],
+        flipped + [ada_state],
         embed_state,
         vector_state,
         [s_down, s_up, s_out, s_qkv, d_ada_both.reshape(16, -1), silu_rows.reshape(16, -1), common_sum, bias_sum],

time: 390 us -> 369 us (0.946)
  Pallas kernels: 374 us -> 359 us
  local copies, waits for them, and re-layouts: 8.3 us -> 1.37 us
    pallas_call x1, Pallas kernels: 177 us -> 161 us  [front(): pl.pallas_call(functools.partial(front_kernel, groups, slots), out_shape=...]
    transpose x3 -> x0, local copies, waits for them, and re-layouts: 5.01 us -> none  [fast_shards(): flipped = tuple((stacked[1].astype(low).T for stacked in states[:4]))]
where the time goes in v6:
time: 369 us; the launch traced here: 362 us
  Pallas kernels  359 us (97%)
    pallas_call x1, Pallas kernels, back(): pl.pallas_call(functools.partial(back_kernel, groups, (first, second)), o...  190 us
    pallas_call x1, Pallas kernels, front(): pl.pallas_call(functools.partial(front_kernel, groups, slots), out_shape=...  161 us
    pallas_call x1, Pallas kernels, update(): pl.pallas_call(functools.partial(update_kernel, rates, mass_scale), out_s...  8.42 us

profile of v6, /device:TPU:0, one launch (start us, length us, event | category | flops | bytes accessed | tf_op | source)
XLA Modules:
  0.0 361.9 jit_solution(7036248665955694737)
XLA Ops:
  0.6 161.3 %shard_map.279 = (bf16[2,3072,512]{2,1,0:T(8,128)(2,1)}, bf16[2,1024,512]{2,1,0:T(8,128)(2,1)}, bf16[2,4096,512]{2,1,0:T(8,128)(2,1)}, bf16[2,1024,2048]{2,1,0:T...) custom-call(f32[3,192,512]{2,1,0:T(8,128)} %bitcast.16, ...), custom_call_target="tpu_custom_call" | custom-call | tf_op jit(solution)/shard_map/pallas_call | solution.py:1249
  162.0 189.7 %shard_map.280 = (f32[64,2048]{1,0:T(8,128)}, f32[256,512]{1,0:T(8,128)}, f32[64,512]{1,0:T(8,128)}, f32[192,512]{1,0:T(8,128)}, f32[2,8,384]{2,1,0:T(8,128)}, /...) custom-call(bf16[192,1024]{1,0:T(8,128)(2,1)} %refs_0_.1, ...), custom_call_target="tpu_custom_call" | custom-call | tf_op jit(solution)/shard_map/pallas_call | solution.py:1995
  351.7 0.0 copy-start
  351.7 0.0 copy-start.1
  351.7 8.4 %shard_map.281 = (f32[3,192,512]{2,1,0:T(8,128)}, f32[3,64,512]{2,1,0:T(8,128)}, f32[3,512,256]{2,1,0:T(8,128)}, f32[3,64,2048]{2,1,0:T(8,128)}, f32[3,512,384]{...) custom-call(f32[3,192,512]{2,1,0:T(8,128)} %bitcast.17, ...), custom_call_target="tpu_custom_call" | custom-call | tf_op jit(solution)/shard_map/pallas_call | solution.py:2076
  360.1 0.0 copy-done
  360.1 0.7 copy.34
  360.9 0.0 copy-done.1
  360.9 0.6 copy.35
Async XLA Ops:
  351.7 8.5 %copy-start = (bf16[192,1024]{1,0:T(8,128)(2,1)S(1)}, bf16[192,1024]{1,0:T(8,128)(2,1)}, u32[]{:S(2)}) copy-start(bf16[192,1024]{1,0:T(8,128)(2,1)} %get-tuple-element.126) | copy-start | bytes 1179652
  351.7 9.2 %copy-start.1 = (f32[32,192]{1,0:T(8,128)S(1)}, f32[32,192]{1,0:T(8,128)}, u32[]{:S(2)}) copy-start(f32[32,192]{1,0:T(8,128)} %get-tuple-element.127) | copy-start | bytes 73732

commit v7 on v6

--- a/solution.py
+++ b/solution.py
@@ -817,7 +817,8 @@
     (c_qkv, c_out, c_up, c_down, s_qkv, s_out, s_up, s_down, cast_sem, store_sem) = refs[68:78]
     sems = refs[78:]
     first_flow = Gather([s_qkv], [f_qkv], sems[:5], pieces_of([s_qkv], FRONT_SPLITS[0]))
-    flow = Gather([s_out, s_up, s_down], [f_out, f_up, f_down], sems[5:10], pieces_of([s_out, s_up, s_down], FRONT_SPLITS[1]))
+    shards = [s_out, s_up, s_down]
+    flow = Gather(shards, [f_out, f_up, f_down], sems[5:10], pieces_of(shards, FRONT_SPLITS[1]))
     ada_send, ada_recv = sems[10:12]
     there = Exchange(send_ref, got_ref, sems[12:14])
     home = Exchange(back_send, back_got, sems[14:16])
@@ -1133,8 +1134,9 @@
     x_one = x_ref[...] + of_tokens(0) * proj
     one_ref[...] = x_one
     two_ref[...] = (standard(x_one) * (1.0 + of_tokens(3)) + of_tokens(5)).astype(low)
-    tick_to(splits[0] + splits[1] + 5)
-    flow.landed(range(splits[0], splits[0] + splits[1]))
+    ups = range(splits[0], splits[0] + splits[1])
+    tick_to(ups[-1] + 6)
+    flow.landed(ups)
     step = 512
     hidden = pre_ref.shape[1]
 
@@ -1173,7 +1175,7 @@
     lax.fori_loop(0, width // LANES, gradient(dmlp, act_half, p_down, LANES, width // 16), 0)
     store((p_down, p_any))
     tick(flow.steps())
-    flow.landed(range(splits[0] + splits[1], sum(splits)))
+    flow.landed(range(ups[-1] + 1, sum(splits)))
     first_flow.finish()
     flow.finish()
     there.finish()
@@ -1273,10 +1275,9 @@
 
     @staticmethod
     def scratch(shapes, count):
-        low = jnp.bfloat16
         out = []
         for rows, cols in shapes:
-            out += [pltpu.VMEM((depth, rows, cols), low) for depth in (2, 2, 4, 4, 3, 3)]
+            out += [pltpu.VMEM((depth, rows, cols), jnp.bfloat16) for depth in (2, 2, 4, 4, 3, 3)]
         dma = pltpu.SemaphoreType.DMA
         return out + [dma((count, 8)), dma((count, 8))]
 
@@ -1418,9 +1419,9 @@
 
 COMMON_ROWS = 48
 FRONT_SPLITS = ((2,), (1, 4, 4))
-FRONT_TICKS = ((1, 1, 1, 0), (0, 1, 0, 1), (0, 1, 0, 1), (0, 0, 0, 0, 0, 1, 0, 0, 1, 0, 0, 1), (1, 1, 1))
+FRONT_TICKS = ((1, 1, 1, 0), (0, 1, 0, 1), (0, 0, 0, 1), (0, 0, 0, 0, 0, 1, 0, 0, 1, 0, 0, 1), (1, 1, 1))
 BACK_SPLITS = ((4, 4, 1), (3,))
-BACK_TICKS = ((1, 1, 1, 1), (1, 0), (0, 0, 1, 0), (0, 0, 0, 0, 0, 1, 0, 0, 1, 0, 0, 1), (1, 1, 1), (1, 1))
+BACK_TICKS = ((1, 0, 1, 1), (1, 0), (0, 0, 0, 1), (0, 1, 1, 0), (1, 1, 1), (1, 1))
 
 
 def standard_of(values):
@@ -1452,9 +1453,9 @@
         send_ref, got_ref, back_send, back_got, g_ref, gt_ref, qt_ref, dq_ref, dkt_ref, dvt_ref,
         w_buf, dhid, h_both, dh_ref, ada_ref, com_ref, ada_land, com_land, ada_sum, com_sum, ada_sib, com_sib,
         bias_own, com_own, edge, edge_left, edge_right,
-        dmlp, two_half, low_half, dattn, mlp_ref, dx_one, act_buf, pre_buf, d_att, p_up, p_out, p_down, q_ref, k_ref, kt_ref, vt_ref, early_sem,
-    ) = refs[36:80]
-    rest = refs[80:]
+        dmlp, two_half, low_half, dattn, mlp_ref, dx_one, act_buf, pre_buf, d_att, p_up, p_out, p_down, q_ref, k_ref, kt_ref, vt_ref, early_sem, att_send, att_got, dq_s, dq_r,
+    ) = refs[36:84]
+    rest = refs[84:]
     flow_bufs, rest = rest[:18], rest[18:]
     flow_sems, rest = rest[:2], rest[2:]
     last_bufs, rest = rest[:6], rest[6:]
@@ -1478,8 +1479,9 @@
     p_qkv = p_up.at[:, :, pl.ds(0, tokens)]
     flow = Scatter([p_down, p_up, p_out], [o_down, o_up, o_out], flow_bufs, flow_sems, splits[0])
     last = Scatter([p_qkv], [o_qkv], last_bufs, last_sems, splits[1])
-    there = Exchange(back_send, back_got, (ex_s, ex_r))
+    there = Exchange(att_send, att_got, (ex_s, ex_r))
     home = Exchange(send_ref, got_ref, (home_s, home_r))
+    back = Exchange(back_send, back_got, (dq_s, dq_r))
     early = [
         pltpu.make_async_copy(src, dst, early_sem.at[i])
         for i, (src, dst) in enumerate(
@@ -1618,8 +1620,8 @@
     def pack(pair, carry):
         cols = pl.ds(pl.multiple_of(pair * LANES, LANES), LANES)
         a, b = d_att[0:mid, cols].astype(f32), d_att[mid:, cols].astype(f32)
-        back_send[2 * pair] = jnp.where(lane_mid < HALF_LANES, a, swap_halves(b)).astype(low)
-        back_send[2 * pair + 1] = jnp.where(lane_mid < HALF_LANES, swap_halves(a), b).astype(low)
+        att_send[2 * pair] = jnp.where(lane_mid < HALF_LANES, a, swap_halves(b)).astype(low)
+        att_send[2 * pair + 1] = jnp.where(lane_mid < HALF_LANES, swap_halves(a), b).astype(low)
         there.push(2 * pair)
         there.push(2 * pair + 1)
         return carry
@@ -1657,7 +1659,7 @@
         rows = pl.ds(pl.multiple_of(pair * two, two), two)
         pieces = []
         for e in range(2):
-            g = back_got[2 * pair + e].astype(f32)
+            g = att_got[2 * pair + e].astype(f32)
             pieces += [g, swap_halves(g)]
         grad = jnp.where(lane < HALF_LANES, jnp.concatenate(pieces, axis=0), 0.0)
         delta = jnp.sum(grad * dq_ref[rows, :], axis=1, keepdims=True)
@@ -1674,48 +1676,53 @@
         lax.fori_loop(2 * i, 2 * i + 2, unpack, 0)
         tick(BACK_TICKS[2][i])
 
-    def query_block(limit, b, carry):
+    def query_block(first, size, b, carry):
         rows = pl.ds(pl.multiple_of(b * ROWS, ROWS), ROWS)
+        cols = slice(first, first + size)
         q, g = q_ref[rows, :], g_ref[rows, :]
-        qt, gt = qt_ref[:, rows], gt_ref[:, rows]
-
-        def chunk(cols, acc):
-            p = jnp.exp(nn(q, kt_ref[:, cols]))
-            ds = (p * nn(g, vt_ref[:, cols])).astype(low)
-            dvt_ref[:, cols] += nn(gt, p.astype(low))
-            dkt_ref[:, cols] += nn(qt, ds)
-            return acc + nn(ds, k_ref[cols, :])
-
-        whole, left = limit // CHUNK, limit % CHUNK
-        acc = lax.fori_loop(
-            0,
-            whole,
-            lambda c, acc: chunk(pl.ds(pl.multiple_of(c * CHUNK, CHUNK), CHUNK), acc),
-            jnp.zeros((ROWS, LANES), f32),
-        )
-        if left:
-            acc = chunk(slice(whole * CHUNK, limit), acc)
-        dq_ref[rows, :] = acc
+        p = jnp.exp(nn(q, kt_ref[:, cols]))
+        ds = (p * nn(g, vt_ref[:, cols])).astype(low)
+        dvt_ref[:, cols] += nn(gt_ref[:, rows], p.astype(low))
+        dkt_ref[:, cols] += nn(qt_ref[:, rows], ds)
+        part = nn(ds, k_ref[cols, :])
+        if first == 0:
+            dq_ref[rows, :] = part
+        else:
+            dq_ref[rows, :] += part
         return carry
 
-    for first, stop, limit in groups:
-        for b in range(first, stop):
-            lax.fori_loop(b, b + 1, functools.partial(query_block, limit), 0)
-            tick(BACK_TICKS[3][b])
-
-    def send_out(pair, carry):
+    def send_keys(pair, carry):
         rows = pl.ds(pl.multiple_of(pair * two, two), two)
-        dkv = jnp.concatenate([dkt_ref[:, rows], dvt_ref[:, rows]], axis=0).T
-        qk = jnp.where(lane < HALF_LANES, dq_ref[rows, :], swap_halves(dkv)).astype(low)
+        dkv = jnp.concatenate([dkt_ref[:, rows], dvt_ref[:, rows]], axis=0).T.astype(low)
         for e in range(2):
-            send_ref[2 * pair + e, 0:tokens, :] = qk[e * tokens : (e + 1) * tokens]
-            a = dkv[e * tokens : e * tokens + mid]
-            b = dkv[e * tokens + mid : (e + 1) * tokens]
-            send_ref[2 * pair + e, tokens:, :] = jnp.where(lane_mid < HALF_LANES, swap_halves(a), b).astype(low)
+            send_ref[2 * pair + e] = dkv[e * tokens : (e + 1) * tokens]
             home.push(2 * pair + e)
         return carry
 
-    lax.fori_loop(0, 8, send_out, 0)
+    def send_queries(w, carry):
+        rows = pl.multiple_of(w * tokens, tokens)
+        a = dq_ref[pl.ds(rows, mid), :]
+        b = dq_ref[pl.ds(pl.multiple_of(rows + mid, mid), mid), :]
+        back_send[w] = jnp.where(lane_mid < HALF_LANES, a, swap_halves(b)).astype(low)
+        back.push(w)
+        return carry
+
+    plane = 4 * tokens
+    sent = 0
+    for c in range(4):
+        for first, stop, limit in groups:
+            if limit > c * plane:
+                size = min(plane, limit - c * plane)
+                lax.fori_loop(first, stop, functools.partial(query_block, c * plane, size), 0)
+        lax.fori_loop(2 * c, 2 * c + 2, send_keys, 0)
+        while sent < 4 and all(
+            limit <= (c + 1) * plane
+            for first, stop, limit in groups
+            if first * ROWS < (sent + 1) * plane and stop * ROWS > sent * plane
+        ):
+            lax.fori_loop(4 * sent, 4 * sent + 4, send_queries, 0)
+            sent += 1
+        tick(BACK_TICKS[3][c])
 
     kept_copy = pltpu.make_async_copy(kept_any, dq_ref, kept_sem)
     kept_copy.start()
@@ -1774,19 +1781,23 @@
         return inverse * (grad - unit * head_sums(unit * grad)), unit
 
     def heads_back(pair, carry):
-        home.wait(2 * pair)
-        home.wait(2 * pair + 1)
+        for e in range(2):
+            home.wait(2 * pair + e)
+            back.wait(2 * pair + e)
         cols = pl.ds(pl.multiple_of(pair * LANES, LANES), LANES)
         key_cols = pl.ds(pl.multiple_of(pair * LANES + width, LANES), LANES)
         val_cols = pl.ds(pl.multiple_of(pair * LANES + 2 * width, LANES), LANES)
-        even = got_ref[2 * pair].astype(f32)
-        odd = got_ref[2 * pair + 1].astype(f32)
-        even_qk, odd_qk = even[:tokens], odd[:tokens]
-        d_query = jnp.where(lane_tok < HALF_LANES, even_qk, swap_halves(odd_qk))
-        d_key = jnp.where(lane_tok < HALF_LANES, swap_halves(even_qk), odd_qk)
-        even_v, odd_v = even[tokens:], odd[tokens:]
-        dproj[core, 0:mid, val_cols] = jnp.where(lane_mid < HALF_LANES, even_v, swap_halves(odd_v)).astype(low)
-        dproj[core, mid:, val_cols] = jnp.where(lane_mid < HALF_LANES, swap_halves(even_v), odd_v).astype(low)
+        even, odd = got_ref[2 * pair].astype(f32), got_ref[2 * pair + 1].astype(f32)
+        d_key = jnp.where(lane_tok < HALF_LANES, even, swap_halves(odd))
+        dproj[core, :, val_cols] = jnp.where(lane_tok < HALF_LANES, swap_halves(even), odd).astype(low)
+        even, odd = back_got[2 * pair].astype(f32), back_got[2 * pair + 1].astype(f32)
+        d_query = jnp.concatenate(
+            [
+                jnp.where(lane_mid < HALF_LANES, even, swap_halves(odd)),
+                jnp.where(lane_mid < HALF_LANES, swap_halves(even), odd),
+            ],
+            axis=0,
+        )
         scaled = d_query * (8.0 * (1.0 + vec_ref[7:8, cols]))
         d_q, unit = unnormalize(dq_ref[pl.ds(pl.multiple_of(pair * tokens, tokens), tokens), :], scaled)
         com_ref[33:34, cols] = jnp.sum(d_query * unit, axis=0, keepdims=True) * 8.0
@@ -1821,7 +1832,7 @@
         p_qkv[c // 2, pl.ds(2 * (c % 2), 2)] = total.astype(low).reshape(2, tokens, half)
         return carry
 
-    assert next_tick[0] >= len(splits[0]) + 2
+    assert next_tick[0] >= len(splits[0]) + 3
     for p in range(len(splits[0])):
         flow.sent(p)
     lax.fori_loop(0, 8, weight_grad, 0)
@@ -1884,6 +1895,8 @@
         )
 
     to_right, to_left = edge_copy(0, edge_left, 1), edge_copy(1, edge_right, 15)
+    to_right.start()
+    to_left.start()
     last.run(2)
     ada_total, com_total = ada_part(ada_ref, wide)[...], common_part(com_ref, wide)[...]
     for copy in small:
@@ -1904,28 +1917,27 @@
     com_own[...] = com_sum[...] + com_sib[...]
     ada_part(bias_all, wide)[...] = bias_own[...]
     common_part(common_all, wide)[...] = com_own[...]
-    back = []
+    spreads = []
     for r in range(1, 16):
-        back.append(spread(spread_s, spread_r, r, 0, bias_own, ada_part(bias_all, wide)))
-        back.append(spread(spread_s, spread_r, r, 1, com_own, common_part(common_all, wide)))
+        spreads.append(spread(spread_s, spread_r, r, 0, bias_own, ada_part(bias_all, wide)))
+        spreads.append(spread(spread_s, spread_r, r, 1, com_own, common_part(common_all, wide)))
     for i in range(4, last.steps()):
         last.run(i)
-    to_right.start()
-    to_left.start()
     to_right.wait_recv()
     to_left.wait_recv()
     column = lane_iota((32, tokens))
     before = jnp.where(column == 0, edge_left[:, 1:2], jnp.roll(share, 1, axis=1))
     after = jnp.where(column == tokens - 1, edge_right[:, 0:1], jnp.roll(share, -1, axis=1))
     map_ref[...] = 2.0 * share + left * before + right * after
-    for copy in back:
+    for copy in spreads:
         copy.wait_recv()
-    for copy in small + swaps + back + sib_copies + [d_copy, to_right, to_left]:
+    for copy in small + swaps + spreads + sib_copies + [d_copy, to_right, to_left]:
         copy.wait_send()
     flow.finish()
     last.finish()
     there.finish()
     home.finish()
+    back.finish()
 
 
 def back(args, groups, splits, call_id):
@@ -1933,7 +1945,7 @@
     tokens, width = x_zero.shape
     hidden = act.shape[1]
     group_len = 16 * tokens
-    half, mid, packed = width // 2, tokens // 2, tokens * 3 // 2
+    half, mid = width // 2, tokens // 2
     f32, low = jnp.float32, jnp.bfloat16
     dma = pltpu.SemaphoreType.DMA
     shape = jax.ShapeDtypeStruct
@@ -1950,8 +1962,8 @@
     ]
     vm = pltpu.VMEM
     scratch = [
-        vm((16, packed, LANES), low),
-        vm((16, packed, LANES), low),
+        vm((16, tokens, LANES), low),
+        vm((16, tokens, LANES), low),
         vm((16, mid, LANES), low),
         vm((16, mid, LANES), low),
         vm((group_len, LANES), low),
@@ -1988,6 +2000,7 @@
         vm((tokens, width), low),
     ] + [vm((4, 4) + s, low) for s in (sizes[1], sizes[2], sizes[0])]
     scratch += [vm((group_len, LANES), low)] * 2 + [vm((LANES, group_len), low)] * 2 + [dma((5,))]
+    scratch += [vm((16, mid, LANES), low)] * 2 + [dma((16,))] * 2
     scratch += Scatter.scratch(sizes[:3], len(first)) + Scatter.scratch(sizes[3:], len(second))
     scratch += [dma((16,)) for _ in range(4)] + [dma((2, 6)), dma((16,)), dma((16,))]
     scratch += [dma((2, 16)) for _ in range(4)] + [dma((2,)), dma((2,))]
@@ -2015,10 +2028,12 @@
 def update_kernel(rates, mass_scale, *refs):
     states = refs[:5]
     (embed_ref, vector_ref, s_down, s_up, s_out, s_qkv, d_ada, silu_ref, common_ref, bias_ref) = refs[5:15]
-    news, copies = refs[15:20], refs[20:25]
-    (embed_new, vector_new, mass_out, gain_out) = refs[25:29]
-    held, lows = refs[29:34], refs[34:39]
-    load_sem, store_sem, low_sem = refs[39:]
+    passed, news, copies, passed_out = refs[15:17], refs[17:22], refs[22:27], refs[27:29]
+    for src, dst in zip(passed, passed_out):
+        dst[...] = src[...]
+    (embed_new, vector_new, mass_out, gain_out) = refs[29:33]
+    held, lows = refs[33:38], refs[38:43]
+    load_sem, store_sem, low_sem = refs[43:]
     width = vector_ref.shape[2]
 
     def grad_of(i):
@@ -2065,24 +2080,25 @@
         copy.wait()
 
 
-def update(states, embed_state, vector_state, grads, rates, codes, mass_scale):
+def update(states, embed_state, vector_state, grads, passed, rates, codes, mass_scale):
     f32, low = jnp.float32, jnp.bfloat16
     shape = jax.ShapeDtypeStruct
     dma = pltpu.SemaphoreType.DMA
     width = vector_state.shape[2]
     outs = [shape(s.shape, f32) for s in states] + [shape(s.shape[1:], low) for s in states]
+    outs += [shape(p.shape, p.dtype) for p in passed]
     outs += [shape(embed_state.shape, f32), shape(vector_state.shape, f32)]
     outs += [shape((codes // LANES, LANES), f32), shape((width // LANES, LANES), f32)]
     return pl.pallas_call(
         functools.partial(update_kernel, rates, mass_scale),
         out_shape=outs,
-        in_specs=[ANY] * 5 + [VM] * 10,
-        out_specs=[ANY] * 10 + [VM] * 4,
+        in_specs=[ANY] * 5 + [VM] * 12,
+        out_specs=[ANY] * 10 + [VM] * 6,
         scratch_shapes=[pltpu.VMEM(s.shape, f32) for s in states]
         + [pltpu.VMEM(s.shape[1:], low) for s in states]
         + [dma((5,)), dma((5,)), dma((5,))],
         compiler_params=pltpu.CompilerParams(vmem_limit_bytes=VMEM_BYTES),
-    )(*states, embed_state, vector_state, *grads)
+    )(*states, embed_state, vector_state, *grads, *passed)
 
 
 def run_tables(slots):
@@ -2173,15 +2189,16 @@
         embed_state,
         vector_state,
         [s_down, s_up, s_out, s_qkv, d_ada_both.reshape(16, -1), silu_rows.reshape(16, -1), common_sum, bias_sum],
+        [block_out, map_grad],
         tuple(rates),
         codes,
         codes / tokens_all,
     )
-    outputs = [block_out, map_grad, results[12].reshape(-1)]
+    outputs = [results[10], results[11], results[14].reshape(-1)]
     for i in range(5):
         new, copied = results[i], results[5 + i]
         outputs += [flip(new), flip(copied)] if i in (0, 1, 3) else [new, copied]
-    return tuple(outputs + [results[10], results[11], results[13].reshape(-1)])
+    return tuple(outputs + [results[12], results[13], results[15].reshape(-1)])
 
 
 def solution(mesh):

time: 369 us -> 352 us (0.954)
  Pallas kernels: 359 us -> 344 us
    pallas_call x1, Pallas kernels: 190 us -> 178 us  [back(): pl.pallas_call(functools.partial(back_kernel, groups, (first, second)), o...]
    pallas_call x1, Pallas kernels: 161 us -> 157 us  [front(): pl.pallas_call(functools.partial(front_kernel, groups, slots), out_shape=...]
where the time goes in v7:
time: 352 us; the launch traced here: 345 us
  Pallas kernels  344 us (98%)
    pallas_call x1, Pallas kernels, back(): pl.pallas_call(functools.partial(back_kernel, groups, (first, second)), o...  178 us
    pallas_call x1, Pallas kernels, front(): pl.pallas_call(functools.partial(front_kernel, groups, slots), out_shape=...  157 us
    pallas_call x1, Pallas kernels, update(): pl.pallas_call(functools.partial(update_kernel, rates, mass_scale), out_s...  8.71 us

profile of v7, /device:TPU:0, one launch (start us, length us, event | category | flops | bytes accessed | tf_op | source)
XLA Modules:
  0.0 344.8 jit_solution(16560348400446246598)
XLA Ops:
  0.6 157.1 %shard_map.279 = (bf16[2,3072,512]{2,1,0:T(8,128)(2,1)}, bf16[2,1024,512]{2,1,0:T(8,128)(2,1)}, bf16[2,4096,512]{2,1,0:T(8,128)(2,1)}, bf16[2,1024,2048]{2,1,0:T...) custom-call(f32[3,192,512]{2,1,0:T(8,128)} %bitcast.16, ...), custom_call_target="tpu_custom_call" | custom-call | tf_op jit(solution)/shard_map/pallas_call | solution.py:1251
  157.8 177.8 %shard_map.280 = (f32[64,2048]{1,0:T(8,128)}, f32[256,512]{1,0:T(8,128)}, f32[64,512]{1,0:T(8,128)}, f32[192,512]{1,0:T(8,128)}, f32[2,8,384]{2,1,0:T(8,128)}, /...) custom-call(bf16[192,1024]{1,0:T(8,128)(2,1)} %refs_0_.1, ...), custom_call_target="tpu_custom_call" | custom-call | tf_op jit(solution)/shard_map/pallas_call | solution.py:2008
  335.6 8.7 %shard_map.281 = (f32[3,192,512]{2,1,0:T(8,128)}, f32[3,64,512]{2,1,0:T(8,128)}, f32[3,512,256]{2,1,0:T(8,128)}, f32[3,64,2048]{2,1,0:T(8,128)}, f32[3,512,384]{...) custom-call(f32[3,192,512]{2,1,0:T(8,128)} %bitcast.17, ...), custom_call_target="tpu_custom_call" | custom-call | tf_op jit(solution)/shard_map/pallas_call | solution.py:2092
